TPU v7x, 32 devices: a whole 2x2x4 slice. The times are simulated.
32 devices in a mesh: sample: 2 (over x), row: 16 (over z, y, core).
Axes of the slice: x: 2, y: 2, z: 4, core: 2. Of those that a mesh axis runs over, the one named last changes fastest.
Arguments:
- sample_index: int32 [2], P('sample'), parts along dimension 0, may hold values from 0 to 32767
- lattice_vector: int32 [1024], replicated, may hold values from 1 to 32767
- mode_table: int32 [2, 1024], replicated, may hold values from -16 to 31, as said below
- connectivity: int32 [3, 32768], replicated, may hold values from 0 to 16639, as said below
- density: bfloat16 [64, 32768], P(None, 'row'), may hold values from -3.5 to 3.5
Outputs:
- potential: float32 [8192, 64], P(('sample', 'row')), parts along dimension 0
There are 2 independent parts, one for each index of `sample`. A program takes and returns all parts, laid end to end along the dimension named above; an argument that names none is the same for every part. Nothing has to cross between parts.
Inputs may be any that keep to these rules, and one draw needn't show every extreme that they name: `mode_table`: the 1024 columns are distinct frequency pairs, the polar one from 0 to 31 and the azimuthal one from -16 to 15. `connectivity`: vertex i * 256 + j lies on latitude cycle i and azimuth j. The columns are the triangles of that grid, two per cell between neighbouring cycles (azimuth wrapping around), each once and oriented with outward normals, in random order.
All inputs are finite; a program needn't handle non-finite values.
Results may differ from a plain program's by a relative error of at most 0.0035.
Values may be sent and summed in bfloat16 or wider, within the bound.
No kernel may reach another device: no remote copies, remote signals or barrier semaphores. Data moves between devices by JAX's collectives and lax.ppermute only.
A program may use at most 256 MiB of HBM per device.

v0:
```python
import math

import jax
import jax.numpy as jnp
from jax import lax
from jax.sharding import PartitionSpec as P

NLAT = 32768
NPH = 256
BAND_DEV = 256


def vertex_grid(sample_index, lattice_vector, mode_table, cycle_count):
    lattice_steps = sample_index[0] * lattice_vector % NLAT
    shifts = lattice_steps.astype(jnp.float32) / NLAT - 0.5
    polar_freq = mode_table[0].astype(jnp.float32)
    azim_freq = mode_table[1].astype(jnp.float32)
    mode_coef = 0.8 * shifts / (1.0 + polar_freq + jnp.abs(azim_freq)) ** 2
    polar_angle = math.pi * (jnp.arange(cycle_count, dtype=jnp.float32) + 1.0) / (cycle_count + 1)
    azimuth = 2.0 * math.pi * jnp.arange(NPH, dtype=jnp.float32) / NPH
    polar_phase = polar_angle[:, None] * polar_freq[None, :]
    azim_phase = azim_freq[:, None] * azimuth[None, :]
    cos_part = jnp.dot(
        jnp.cos(polar_phase) * mode_coef[None, :],
        jnp.cos(azim_phase),
        precision=lax.Precision.HIGHEST,
    )
    sin_part = jnp.dot(
        jnp.sin(polar_phase) * mode_coef[None, :],
        jnp.sin(azim_phase),
        precision=lax.Precision.HIGHEST,
    )
    radius = jnp.exp(cos_part - sin_part)
    cycle_sin = jnp.sin(polar_angle)[:, None]
    coord_x = radius * cycle_sin * jnp.cos(azimuth)[None, :]
    coord_y = radius * cycle_sin * jnp.sin(azimuth)[None, :]
    coord_z = radius * jnp.cos(polar_angle)[:, None]
    return jnp.stack([coord_x, coord_y, coord_z]).reshape(3, cycle_count * NPH)


def panel_geometry(vertices, corners):
    corner_one = vertices[:, corners[0]]
    corner_two = vertices[:, corners[1]]
    corner_three = vertices[:, corners[2]]
    centers = (corner_one + corner_two + corner_three) / 3.0
    edge_one = corner_two - corner_one
    edge_two = corner_three - corner_one
    area_vectors = 0.5 * jnp.stack(
        [
            edge_one[1] * edge_two[2] - edge_one[2] * edge_two[1],
            edge_one[2] * edge_two[0] - edge_one[0] * edge_two[2],
            edge_one[0] * edge_two[1] - edge_one[1] * edge_two[0],
        ]
    )
    return (centers, area_vectors)


def kernel_tile(target_centers, target_ids, source_centers, source_areas, source_ids):
    delta_x = target_centers[0][:, None] - source_centers[0][None, :]
    delta_y = target_centers[1][:, None] - source_centers[1][None, :]
    delta_z = target_centers[2][:, None] - source_centers[2][None, :]
    dist_sq = delta_x * delta_x + delta_y * delta_y + delta_z * delta_z
    self_pair = target_ids[:, None] == source_ids[None, :]
    safe_dist = jnp.where(self_pair, 1.0, dist_sq)
    numerator = (
        delta_x * source_areas[0][None, :]
        + delta_y * source_areas[1][None, :]
        + delta_z * source_areas[2][None, :]
    )
    kernel_value = numerator / (4.0 * math.pi * safe_dist * jnp.sqrt(safe_dist))
    return jnp.where(self_pair, 0.0, kernel_value).astype(jnp.bfloat16)


def apply_tile(tile, density_block):
    return lax.dot_general(
        tile, density_block, (((1,), (1,)), ((), ())), preferred_element_type=jnp.float32
    )


def per_device(sample_index, lattice_vector, mode_table, connectivity, density):
    columns, src_dev = density.shape
    band_dev = BAND_DEV
    row_total = lax.axis_size("row")
    row_index = lax.axis_index("row")
    panel_total = src_dev * row_total
    cycle_count = panel_total // (2 * NPH) + 1
    vertices = vertex_grid(sample_index, lattice_vector, mode_table, cycle_count)
    own_first = row_index * src_dev
    own_ids = own_first + jnp.arange(src_dev, dtype=jnp.int32)
    own_corners = lax.dynamic_slice_in_dim(connectivity, own_first, src_dev, 1)
    own_centers, own_areas = panel_geometry(vertices, own_corners)
    local_term = 0.5 * density[:, :band_dev].astype(jnp.float32).T
    band_centers = lax.all_gather(own_centers[:, :band_dev], "row", axis=1, tiled=True)
    block = math.gcd(band_dev * lax.axis_size("row"), 1024)

    def one_block(turn):
        first_row = turn * block
        rows = first_row + jnp.arange(block, dtype=jnp.int32)
        target_ids = rows // band_dev * src_dev + rows % band_dev
        target_centers = lax.dynamic_slice_in_dim(band_centers, first_row, block, 1)
        tile = kernel_tile(target_centers, target_ids, own_centers, own_areas, own_ids)
        return apply_tile(tile, density)

    blocks = lax.map(
        one_block, jnp.arange(band_dev * lax.axis_size("row") // block, dtype=jnp.int32)
    )
    sums = lax.psum_scatter(
        blocks.reshape(band_dev * lax.axis_size("row"), columns),
        "row",
        scatter_dimension=0,
        tiled=True,
    )
    return local_term + sums


def solution(mesh):
    placed = (P("sample"), P(), P(), P(), P(None, "row"))
    return jax.shard_map(
        per_device,
        mesh=mesh,
        in_specs=placed,
        out_specs=P(("sample", "row"), None),
        check_vma=False,
    )
```

profile of v0, /device:TPU:0, one launch (start us, length us, event | category | flops | bytes accessed | tf_op | source)
XLA Modules:
  0.0 187.6 jit_solution(3020884002444759545)
XLA Ops:
  6.5 0.8 slice_convert_fusion.1
  7.3 0.7 broadcast_add_fusion
  8.8 0.7 fusion.46
  9.5 5.1 %fusion.25 = f32[65,256]{1,0:T(8,128)S(1)} fusion(f32[256]{0:T(256)S(1)} %iota_multiply_fusion, f32[1024]{0:T(1024)S(1)} %bitcast.108, f32[1024]{0:T(1024)S(1)} %fusion.46, f32[1024]{0:T(1024)S(1)} %bitcast.110, f32[65]{0:T(128)S(1)} %add_multiply_fusion), kind=kOutput, calls=%fused_computation.44 | convolution fusion | flops 204867584 | bytes 80132 | tf_op jit(solution)/shard_map/dot_general | solution.py:23
  14.6 5.2 %multiply_bitcast_fusion.2 = (f32[1,1,65,256]{3,2,1,0:T(8,128)S(1)}, f32[1,1,65,256]{3,2,1,0:T(8,128)S(1)}, f32[1,1,65,256]{3,2,1,0:T(8,128)S(1)}) fusion(f32[256]{0:T(256)S(1)} %get-tuple-element.196, f32[65]{0:T(128)S(1)} %get-tuple-element.198, f32[256]{0:T(256)S(1)} %get-tuple-element.195, f32[65]{0:T(128)S(1)} %get-tuple-element.197, ...), kind=kOutput, calls=%fused_computation.62 | convolution fusion | flops 204950784 | bytes 282380 | tf_op jit(solution)/shard_map/dot_general | solution.py:28
  20.3 5.3 %copy.38 = f32[3,16640]{0,1:T(8,128)} copy(f32[3,16640]{1,0:T(4,128)S(1)} %pad_maximum_fusion) | data formatting | bytes 399360 | tf_op jit(solution)/shard_map/stack | solution.py:38
  25.6 1.0 compare_select_fusion.4
  26.6 8.9 %gather_fusion = f32[2048,3]{1,0:T(8,128)S(1)} fusion(f32[3,16640]{0,1:T(8,128)} %copy.38, s32[2048]{0:T(1024)S(1)} %broadcast_clamp_fusion.2), kind=kCustom, calls=%fused_computation | custom fusion | bytes 57344 | tf_op jit(solution)/shard_map/gather | solution.py:42
  35.5 0.3 copy.39
  35.8 8.9 %gather_fusion.1 = f32[2048,3]{1,0:T(8,128)S(1)} fusion(f32[3,16640]{0,1:T(8,128)} %copy.38, s32[2048]{0:T(1024)S(1)} %broadcast_clamp_fusion.1), kind=kCustom, calls=%fused_computation.1 | custom fusion | bytes 57344 | tf_op jit(solution)/shard_map/gather | solution.py:43
  44.7 0.3 copy.41
  45.0 8.9 %gather_fusion.2 = f32[2048,3]{1,0:T(8,128)S(1)} fusion(f32[3,16640]{0,1:T(8,128)} %copy.38, s32[2048]{0:T(1024)S(1)} %broadcast_clamp_fusion), kind=kCustom, calls=%fused_computation.2 | custom fusion | bytes 57344 | tf_op jit(solution)/shard_map/gather | solution.py:44
  53.9 0.3 copy.43
  54.3 23.3 %all_gather.3 = f32[3,4096]{1,0:T(4,128)S(1)} all-gather(f32[3,256]{1,0:T(4,128)S(1)} %slice.127), channel_id=1, replica_groups=mesh['sample'=2,'row'=16] {'row'}, dimensions={1}, use_global_device_ids=true | all-gather | bytes 52224 | tf_op jit(solution)/shard_map/all_gather | solution.py:93
  77.7 45.2 %while.13 = (s32[]{:T(128)}, f32[4,1024,64]{1,0,2:T(4,128)S(1)}, s32[4]{0:T(128)S(1)}, f32[3,4096]{1,0:T(4,128)S(1)}, f32[3,2048]{1,0:T(4,128)S(1)}, /*index=5*/...) while((s32[]{:T(128)}, f32[4,1024,64]{1,0,2:T(4,128)S(1)}, ...), condition=%wide.region_1.2_spmd.clone, body=%wide.region_0.1_spmd.clone.sunk | while | flops 310403072 | bytes 1781999 | solution.py:104
  77.7 0.7 dynamic_slice.20
  79.1 7.5 %fusion.65 = f32[1,1024,64]{1,2,0:T(8,128)S(1)} fusion(bf16[64,2048]{1,0:T(8,128)(2,1)S(1)} %get-tuple-element.300, f32[2048]{0:T(1024)S(1)} %bitcast.98, f32[2048]{0:T(1024)S(1)} %bitcast.95, f32[1024]{0:T(1024)S(1)} %bitcast.102, f32[2048]{0:T(1024)S(1)} %bitcast.97, f32[2048]{0:T(1024)S(1)} %bitcast.96, f32[1024]{0:T(1024)S(1)} %bitcast.101, ...), kind=kOutput, calls=%fused_computation.20.clone.1 | convolution fusion | flops 310378496 | bytes 598016 | tf_op jit(solution)/shard_map/while/body/eval_jaxpr/dot_general | solution.py:75
  86.9 2.1 %dynamic_update_slice.9 = f32[4,1024,64]{1,0,2:T(4,128)S(1)} dynamic-update-slice(f32[4,1024,64]{1,0,2:T(4,128)S(1)} %get-tuple-element.281, f32[1,1024,64]{1,0,2:T(1,128)S(1)} %copy.52, s32[]{:T(128)} %get-tuple-element.280, s32[]{:T(128)} %constant.123.clone.1..sunk, s32[]{:T(128)} %constant.123.clone.1..sunk) | dynamic-update-slice | bytes 524292 | tf_op jit(solution)/shard_map/while/body/jit(dynamic_update_index_in_dim)/dynamic_update_slice | solution.py:104
  89.0 0.7 dynamic_slice.20
  90.4 7.5 %fusion.65 = f32[1,1024,64]{1,2,0:T(8,128)S(1)} fusion(bf16[64,2048]{1,0:T(8,128)(2,1)S(1)} %get-tuple-element.300, f32[2048]{0:T(1024)S(1)} %bitcast.98, f32[2048]{0:T(1024)S(1)} %bitcast.95, f32[1024]{0:T(1024)S(1)} %bitcast.102, f32[2048]{0:T(1024)S(1)} %bitcast.97, f32[2048]{0:T(1024)S(1)} %bitcast.96, f32[1024]{0:T(1024)S(1)} %bitcast.101, ...), kind=kOutput, calls=%fused_computation.20.clone.1 | convolution fusion | flops 310378496 | bytes 598016 | tf_op jit(solution)/shard_map/while/body/eval_jaxpr/dot_general | solution.py:75
  98.2 2.1 %dynamic_update_slice.9 = f32[4,1024,64]{1,0,2:T(4,128)S(1)} dynamic-update-slice(f32[4,1024,64]{1,0,2:T(4,128)S(1)} %get-tuple-element.281, f32[1,1024,64]{1,0,2:T(1,128)S(1)} %copy.52, s32[]{:T(128)} %get-tuple-element.280, s32[]{:T(128)} %constant.123.clone.1..sunk, s32[]{:T(128)} %constant.123.clone.1..sunk) | dynamic-update-slice | bytes 524292 | tf_op jit(solution)/shard_map/while/body/jit(dynamic_update_index_in_dim)/dynamic_update_slice | solution.py:104
  100.3 0.7 dynamic_slice.20
  101.7 7.5 %fusion.65 = f32[1,1024,64]{1,2,0:T(8,128)S(1)} fusion(bf16[64,2048]{1,0:T(8,128)(2,1)S(1)} %get-tuple-element.300, f32[2048]{0:T(1024)S(1)} %bitcast.98, f32[2048]{0:T(1024)S(1)} %bitcast.95, f32[1024]{0:T(1024)S(1)} %bitcast.102, f32[2048]{0:T(1024)S(1)} %bitcast.97, f32[2048]{0:T(1024)S(1)} %bitcast.96, f32[1024]{0:T(1024)S(1)} %bitcast.101, ...), kind=kOutput, calls=%fused_computation.20.clone.1 | convolution fusion | flops 310378496 | bytes 598016 | tf_op jit(solution)/shard_map/while/body/eval_jaxpr/dot_general | solution.py:75
  109.2 0.3 copy.52
  109.4 2.1 %dynamic_update_slice.9 = f32[4,1024,64]{1,0,2:T(4,128)S(1)} dynamic-update-slice(f32[4,1024,64]{1,0,2:T(4,128)S(1)} %get-tuple-element.281, f32[1,1024,64]{1,0,2:T(1,128)S(1)} %copy.52, s32[]{:T(128)} %get-tuple-element.280, s32[]{:T(128)} %constant.123.clone.1..sunk, s32[]{:T(128)} %constant.123.clone.1..sunk) | dynamic-update-slice | bytes 524292 | tf_op jit(solution)/shard_map/while/body/jit(dynamic_update_index_in_dim)/dynamic_update_slice | solution.py:104
  111.6 0.7 dynamic_slice.20
  113.0 7.5 %fusion.65 = f32[1,1024,64]{1,2,0:T(8,128)S(1)} fusion(bf16[64,2048]{1,0:T(8,128)(2,1)S(1)} %get-tuple-element.300, f32[2048]{0:T(1024)S(1)} %bitcast.98, f32[2048]{0:T(1024)S(1)} %bitcast.95, f32[1024]{0:T(1024)S(1)} %bitcast.102, f32[2048]{0:T(1024)S(1)} %bitcast.97, f32[2048]{0:T(1024)S(1)} %bitcast.96, f32[1024]{0:T(1024)S(1)} %bitcast.101, ...), kind=kOutput, calls=%fused_computation.20.clone.1 | convolution fusion | flops 310378496 | bytes 598016 | tf_op jit(solution)/shard_map/while/body/eval_jaxpr/dot_general | solution.py:75
  120.5 0.3 copy.52
  120.7 2.1 %dynamic_update_slice.9 = f32[4,1024,64]{1,0,2:T(4,128)S(1)} dynamic-update-slice(f32[4,1024,64]{1,0,2:T(4,128)S(1)} %get-tuple-element.281, f32[1,1024,64]{1,0,2:T(1,128)S(1)} %copy.52, s32[]{:T(128)} %get-tuple-element.280, s32[]{:T(128)} %constant.123.clone.1..sunk, s32[]{:T(128)} %constant.123.clone.1..sunk) | dynamic-update-slice | bytes 524292 | tf_op jit(solution)/shard_map/while/body/jit(dynamic_update_index_in_dim)/dynamic_update_slice | solution.py:104
  122.8 1.6 copy.50
  124.5 54.8 %reduce-scatter.2.cloned.1.call-done = f32[256,64]{0,1:T(8,128)} async-done(((f32[4096,64]{0,1:T(8,128)}), f32[256,64]{0,1:T(8,128)}) %reduce-scatter.2.cloned.1.call-update) | async-done | bytes 65552 | tf_op jit(solution)/shard_map/reduce_scatter | solution.py:107
  179.3 1.5 bitcast_add_fusion
  (39 shorter events, 1.8 us)
Async XLA Ops:
  6.5 71.1 %copy-start = (bf16[64,2048]{1,0:T(8,128)(2,1)S(1)}, bf16[64,2048]{1,0:T(8,128)(2,1)}, u32[]{:S(2)}) copy-start(bf16[64,2048]{1,0:T(8,128)(2,1)} %param.11) | copy-start | bytes 786436
  6.5 172.7 %reduce-scatter.2.cloned.1.call-start = ((), (), s32[]{:S(2)}) async-start(), calls=%async_computation.1 | async-start | bytes 1114112 | tf_op jit(solution)/shard_map/reduce_scatter | solution.py:107
Sparse Core Ops, SparseCore 0:
  124.6 54.6 reduce-scatter.1
where the time goes:
time: 188 us
  waiting for transfers between devices  54.8 us (29%)
  local copies, waits for them, and re-layouts  47.3 us (25%)
  matrix products  40.1 us (21%)
  blocking collectives  23.3 us (12%)
  between operations  14.2 us (8%)
  other arithmetic  5.11 us (3%)
  loops' own time  2.73 us (1%)
    reduce_scatter x1, waiting for transfers between devices, per_device(): lax.psum_scatter(blocks.reshape(band_dev * lax.axis_size('row'), columns)...  54.8 us
    dot_general x4, matrix products, apply_tile(): lax.dot_general(tile, density_block, (((1,), (1,)), ((), ())), preferred_...  29.8 us
    all_gather x1, blocking collectives, per_device(): lax.all_gather(own_centers[:, :band_dev], 'row', axis=1, tiled=True)  23.3 us
    dynamic_update_slice x8, local copies, waits for them, and re-layouts, per_device(): lax.map(one_block, jnp.arange(band_dev * lax.axis_size('row') // block, d...  9.44 us
    gather x2, local copies, waits for them, and re-layouts, panel_geometry(): corner_two = vertices[:, corners[1]]  9.22 us
    gather x2, local copies, waits for them, and re-layouts, panel_geometry(): corner_three = vertices[:, corners[2]]  9.22 us
    gather x2, local copies, waits for them, and re-layouts, panel_geometry(): corner_one = vertices[:, corners[0]]  9.21 us
    another operation x1, local copies, waits for them, and re-layouts, vertex_grid(): return jnp.stack([coord_x, coord_y, coord_z]).reshape(3, cycle_count * NPH)  5.32 us
  transfers between devices with their start and end apart: 1, of which 1 were waited for; matrix products, arithmetic and copies ran while one was open for 0% of the time, Pallas kernels for 0%

commit v1 on v0

v1 whole, which is shorter than its diff:
```python
import math

import jax
import jax.numpy as jnp
import numpy as np
from jax import lax
from jax.experimental import pallas as pl
from jax.experimental.pallas import tpu as pltpu
from jax.sharding import PartitionSpec as P

NLAT = 32768
NPH = 256
BAND_DEV = 256
FREQS = 32
HALF = 24
FEATS = 128
CHUNK = 1024
SRC_STEP = 1024
TGT_STEP = 1024
VMEM = 56 << 20
F32 = jnp.float32
BF16 = jnp.bfloat16


def split(values):
    first = values.astype(BF16).astype(F32)
    rest = values - first
    second = rest.astype(BF16).astype(F32)
    third = (rest - second).astype(BF16).astype(F32)
    return first, second, third


def split_host(values):
    first = values.astype(jnp.bfloat16).astype(np.float64)
    second = (values - first).astype(jnp.bfloat16).astype(np.float64)
    third = (values - first - second).astype(jnp.bfloat16).astype(np.float64)
    return first, second, third


def trig_tables(cycle_count):
    pitch = -(-cycle_count // 16) * 16
    width = -(-3 * pitch // 128) * 128
    lanes = np.arange(width)
    cycle = lanes % pitch
    piece = lanes // pitch
    inside = (cycle < cycle_count) & (piece < 3)
    polar = np.pi * (cycle + 1.0) / (cycle_count + 1)
    freq = np.arange(FREQS)[:, None]
    polar_table = np.concatenate(
        [np.cos(freq * polar) * inside, -np.sin(freq * polar) * inside], axis=1
    ).astype(np.float32)
    azimuth = 2.0 * np.pi * np.arange(NPH)[:, None] / NPH
    azim_freq = np.arange(FREQS)[None, :] - FREQS // 2
    azim_table = np.concatenate(
        [np.cos(azimuth * azim_freq), np.sin(azimuth * azim_freq)], axis=1
    ).astype(np.float32)
    ring = np.zeros((16, width))
    for row, values in enumerate((np.sin(polar), np.cos(polar))):
        for which, part in enumerate(split_host(values.astype(np.float32).astype(np.float64))):
            ring[row] += part * (inside & (piece == which))
    first_cos = float(np.cos(np.pi / (cycle_count + 1)))
    return pitch, width, polar_table, azim_table, ring.astype(jnp.bfloat16), first_cos


def radius_table(sample, lattice, modes, polar_table, azim_table, width):
    shifts = ((sample * lattice) & (NLAT - 1)).astype(F32) / NLAT - 0.5
    polar_freq = modes[0:1, :]
    azim_freq = modes[1:2, :]
    scale = (1 + polar_freq + jnp.abs(azim_freq)).astype(F32)
    coef = 0.8 * shifts / (scale * scale)
    numbers = lax.broadcasted_iota(jnp.int32, (FREQS, modes.shape[1]), 0)
    at_azim = numbers == azim_freq + FREQS // 2
    at_polar = jnp.where(numbers == polar_freq, 1.0, 0.0).astype(BF16)
    pieces = jnp.concatenate([jnp.where(at_azim, part, 0.0) for part in split(coef)], axis=0)
    grid = lax.dot_general(
        pieces.astype(BF16), at_polar, (((1,), (1,)), ((), ())), preferred_element_type=F32
    )
    grid = grid[:FREQS] + grid[FREQS : 2 * FREQS] + grid[2 * FREQS :]
    both = jnp.dot(grid, polar_table, precision=lax.Precision.HIGHEST, preferred_element_type=F32)
    stacked = jnp.concatenate([both[:, :width], both[:, width:]], axis=0)
    return jnp.exp(
        jnp.dot(azim_table, stacked, precision=lax.Precision.HIGHEST, preferred_element_type=F32)
    )


def azimuth_trig(column):
    quarter = (column + NPH // 8) >> 6
    angle = (column - (quarter << 6)).astype(F32) * (2.0 * math.pi / NPH)
    sq = angle * angle
    sin = angle * (
        1.0 + sq * (-1.0 / 6 + sq * (1.0 / 120 + sq * (-1.0 / 5040 + sq * (1.0 / 362880))))
    )
    cos = 1.0 + sq * (
        -0.5 + sq * (1.0 / 24 + sq * (-1.0 / 720 + sq * (1.0 / 40320 - sq * (1.0 / 3628800))))
    )
    odd = (quarter & 1) == 1
    cos_sign = jnp.where(((quarter + 1) & 2) == 2, -1.0, 1.0)
    sin_sign = jnp.where((quarter & 2) == 2, -1.0, 1.0)
    return jnp.where(odd, sin, cos) * cos_sign, jnp.where(odd, cos, sin) * sin_sign


def lookup(table, cycle, column, pitch, width):
    count = cycle.shape[1]
    hot = jnp.where(
        lax.broadcasted_iota(jnp.int32, (pitch, count), 0) == cycle, 1.0, 0.0
    ).astype(BF16)
    parts = [hot, hot, hot]
    if width > 3 * pitch:
        parts.append(jnp.zeros((width - 3 * pitch, count), BF16))
    found = jnp.dot(table, jnp.concatenate(parts, axis=0), preferred_element_type=F32)
    rows = found[:NPH]
    size = NPH // 2
    while size >= 8:
        rows = jnp.where((column & size) != 0, rows[size:], rows[:size])
        size //= 2
    low = lax.broadcasted_iota(jnp.int32, (8, count), 0) == (column & 7)
    radius = jnp.sum(jnp.where(low, rows, 0.0), axis=0, keepdims=True)
    return radius, found[NPH : NPH + 1], found[NPH + 1 : NPH + 2]


def panels(corners, table, pitch, width):
    column = corners & (NPH - 1)
    cycle = corners >> 8
    cos, sin = azimuth_trig(column)
    points = []
    for c in range(3):
        one = slice(c, c + 1)
        radius, ring_sin, ring_cos = lookup(table, cycle[one], column[one], pitch, width)
        flat = radius * ring_sin
        points.append((flat * cos[one], flat * sin[one], radius * ring_cos))
    centers = [(points[0][d] + points[1][d] + points[2][d]) / 3.0 for d in range(3)]
    one = [points[1][d] - points[0][d] for d in range(3)]
    two = [points[2][d] - points[0][d] for d in range(3)]
    half = 0.5 / (4.0 * math.pi)
    areas = [
        half * (one[(d + 1) % 3] * two[(d + 2) % 3] - one[(d + 2) % 3] * two[(d + 1) % 3])
        for d in range(3)
    ]
    return jnp.concatenate(centers, axis=0), jnp.concatenate(areas, axis=0)


def geometry_kernel(
    row_total, group, sizes, sample_ref, lattice_ref, modes_ref, polar_ref, azim_ref, ring_ref,
    connectivity_ref, dist_ref, flux_ref, target_ref, src_corners, tgt_corners, src_sems, tgt_sems,
):
    pitch, width, first_cos, cycle_count = sizes
    src_total = src_corners.shape[1]
    src_dev = src_total // group
    groups = row_total // group
    row = lax.axis_index("row")
    own_group = row // group
    place = row % group
    copies = []
    for k in range(group):
        first = pl.multiple_of((own_group * group + (place ^ k)) * src_dev, 128)
        copies.append(
            pltpu.make_async_copy(
                connectivity_ref.at[:, pl.ds(first, src_dev)],
                src_corners.at[:, pl.ds(k * src_dev, src_dev)],
                src_sems.at[k],
            )
        )
    for k in range(groups):
        owner = (own_group + k + 1) % groups * group + place
        first = pl.multiple_of(owner * src_dev, 128)
        copies.append(
            pltpu.make_async_copy(
                connectivity_ref.at[:, pl.ds(first, BAND_DEV)],
                tgt_corners.at[:, pl.ds(k * BAND_DEV, BAND_DEV)],
                tgt_sems.at[k],
            )
        )
    for copy in copies:
        copy.start()

    radius = radius_table(
        sample_ref[0], lattice_ref[...], modes_ref[...], polar_ref[...], azim_ref[...], width
    )
    north = jnp.mean(radius[:, 0:1], axis=0, keepdims=True) * first_cos
    south = -jnp.mean(radius[:, cycle_count - 1 : cycle_count], axis=0, keepdims=True) * first_cos
    one, two, three = split(radius)
    lane = lax.broadcasted_iota(jnp.int32, radius.shape, 1)
    radius_pieces = jnp.where(lane < pitch, one, jnp.where(lane < 2 * pitch, two, three))
    table = jnp.concatenate([radius_pieces.astype(BF16), ring_ref[...]], axis=0)
    for copy in copies:
        copy.wait()

    def pieces_of(values):
        return jnp.concatenate(split(values), axis=0)

    def sources(step, carry):
        here = pl.ds(pl.multiple_of(step * CHUNK, CHUNK), CHUNK)
        centers, areas = panels(src_corners[:, here], table, pitch, width)
        upper = centers[2:3] >= 0.0
        offset = centers - jnp.concatenate(
            [jnp.zeros((2, CHUNK), F32), jnp.where(upper, north, south)], axis=0
        )
        square = jnp.sum(offset * offset, axis=0, keepdims=True)
        level = jnp.sum(offset * areas, axis=0, keepdims=True)
        o_one, o_two, o_three = split(-2.0 * offset)
        a_one, a_two, a_three = split(areas)
        ones = jnp.ones((3, CHUNK), F32)
        dist = jnp.concatenate(
            [o_one, o_two, o_three, o_one, o_two, o_one, ones, pieces_of(square)], axis=0
        )
        flux = jnp.concatenate(
            [a_one, a_two, a_three, a_one, a_two, a_one, 0.0 * ones, pieces_of(-level)], axis=0
        )
        for ref, values in ((dist_ref, dist), (flux_ref, flux)):
            both = jnp.concatenate(
                [
                    jnp.where(upper, values, 0.0),
                    jnp.where(upper, 0.0, values),
                    jnp.zeros((FEATS - 2 * HALF, CHUNK), F32),
                ],
                axis=0,
            )
            ref[:, here] = both.astype(BF16)
        return carry

    def targets(step, carry):
        here = pl.ds(pl.multiple_of(step * CHUNK, CHUNK), CHUNK)
        centers, _ = panels(tgt_corners[:, here], table, pitch, width)
        ones = jnp.ones((3, CHUNK), F32)
        rows = []
        for origin in (north, south):
            offset = centers - jnp.concatenate(
                [jnp.zeros((2, CHUNK), F32), jnp.broadcast_to(origin, (1, CHUNK))], axis=0
            )
            square = jnp.sum(offset * offset, axis=0, keepdims=True)
            o_one, o_two, o_three = split(offset)
            rows += [o_one, o_one, o_one, o_two, o_two, o_three, pieces_of(square), ones]
        rows.append(jnp.zeros((FEATS - 2 * HALF, CHUNK), F32))
        target_ref[:, here] = jnp.concatenate(rows, axis=0).astype(BF16)
        return carry

    lax.fori_loop(0, src_total // CHUNK, sources, 0)
    lax.fori_loop(0, tgt_corners.shape[1] // CHUNK, targets, 0)


def geometry(sample_index, lattice_vector, mode_table, connectivity, row_total, group, src_dev):
    cycle_count = src_dev * row_total // (2 * NPH) + 1
    pitch, width, polar_table, azim_table, ring, first_cos = trig_tables(cycle_count)
    groups = row_total // group
    src_total = src_dev * group
    tgt_total = groups * BAND_DEV
    vmem = pl.BlockSpec(memory_space=pltpu.VMEM)

    def kernel(*refs):
        geometry_kernel(row_total, group, (pitch, width, first_cos, cycle_count), *refs)

    return pl.pallas_call(
        kernel,
        out_shape=[
            jax.ShapeDtypeStruct((FEATS, src_total), BF16),
            jax.ShapeDtypeStruct((FEATS, src_total), BF16),
            jax.ShapeDtypeStruct((FEATS, tgt_total), BF16),
        ],
        in_specs=[pl.BlockSpec(memory_space=pltpu.SMEM)] + [vmem] * 5 + [pl.BlockSpec(memory_space=pl.ANY)],
        out_specs=[vmem] * 3,
        scratch_shapes=[
            pltpu.VMEM((3, src_total), jnp.int32),
            pltpu.VMEM((3, tgt_total), jnp.int32),
            pltpu.SemaphoreType.DMA((group,)),
            pltpu.SemaphoreType.DMA((groups,)),
        ],
        compiler_params=pltpu.CompilerParams(vmem_limit_bytes=VMEM),
        name="geometry",
    )(
        sample_index, lattice_vector.reshape(1, -1), mode_table, jnp.asarray(polar_table),
        jnp.asarray(azim_table), jnp.asarray(ring), connectivity,
    )


def pairs_kernel(group, dist_ref, flux_ref, target_ref, *refs):
    density_refs, sums_ref = refs[:group], refs[group]
    src_dev = density_refs[0].shape[1]
    last = pl.program_id(0) == pl.num_programs(0) - 1
    target = target_ref[...]
    diagonal = lax.broadcasted_iota(jnp.int32, (BAND_DEV, BAND_DEV), 0) == lax.broadcasted_iota(
        jnp.int32, (BAND_DEV, BAND_DEV), 1
    )
    sums_ref[...] = jnp.zeros_like(sums_ref)
    for k in range(group):

        def step(turn, carry, k=k):
            inside = pl.multiple_of(turn * SRC_STEP, SRC_STEP)
            here = pl.ds(pl.multiple_of(k * src_dev + turn * SRC_STEP, SRC_STEP), SRC_STEP)
            contract = (((0,), (0,)), ((), ()))
            dist_sq = lax.dot_general(dist_ref[:, here], target, contract, preferred_element_type=F32)
            flux = lax.dot_general(flux_ref[:, here], target, contract, preferred_element_type=F32)
            if k == 0:
                far = jnp.where(last & (turn == 0), 1e30, 0.0)
                apart = jnp.where(diagonal, far, 0.0)
                top = jnp.concatenate(
                    [dist_sq[:BAND_DEV, :-BAND_DEV], dist_sq[:BAND_DEV, -BAND_DEV:] + apart], axis=1
                )
                dist_sq = jnp.concatenate([top, dist_sq[BAND_DEV:]], axis=0)
            inverse = lax.rsqrt(dist_sq)
            tile = (flux * inverse * (inverse * inverse)).astype(BF16)
            sums_ref[...] += jnp.dot(
                density_refs[k][:, pl.ds(inside, SRC_STEP)], tile, preferred_element_type=F32
            )
            return carry

        lax.fori_loop(0, src_dev // SRC_STEP, step, 0)


def pairs(dist, flux, target, densities):
    columns = densities[0].shape[0]
    total = target.shape[1]
    vmem = pl.BlockSpec(memory_space=pltpu.VMEM)

    def kernel(*refs):
        pairs_kernel(len(densities), *refs)

    return pl.pallas_call(
        kernel,
        grid=(total // TGT_STEP,),
        out_shape=jax.ShapeDtypeStruct((columns, total), F32),
        in_specs=[vmem, vmem, pl.BlockSpec((FEATS, TGT_STEP), lambda t: (0, t))]
        + [vmem] * len(densities),
        out_specs=pl.BlockSpec((columns, TGT_STEP), lambda t: (0, t)),
        compiler_params=pltpu.CompilerParams(vmem_limit_bytes=VMEM),
        name="pairs",
    )(dist, flux, target, *densities)


def finish(density, parts):
    def kernel(density_ref, *refs):
        total = 0.5 * density_ref[...].astype(F32)
        for ref in refs[:-1]:
            total = total + ref[...]
        refs[-1][...] = total.T

    columns = density.shape[0]
    block = pl.BlockSpec((columns, BAND_DEV), lambda i: (0, 0))
    return pl.pallas_call(
        kernel,
        grid=(1,),
        out_shape=jax.ShapeDtypeStruct((BAND_DEV, columns), F32),
        in_specs=[block] * (1 + len(parts)),
        out_specs=pl.BlockSpec((BAND_DEV, columns), lambda i: (0, 0)),
        name="finish",
    )(density, *parts)


def per_device(sample_index, lattice_vector, mode_table, connectivity, density):
    src_dev = density.shape[1]
    row_total = lax.axis_size("row")
    group = math.gcd(row_total, 4)
    groups = row_total // group
    densities = [density] + [
        lax.ppermute(density, "row", [(r, r ^ k) for r in range(row_total)])
        for k in range(1, group)
    ]
    dist, flux, target = geometry(
        sample_index, lattice_vector, mode_table, connectivity, row_total, group, src_dev
    )
    sums = pairs(dist, flux, target, densities)
    parts = [sums[:, (groups - 1) * BAND_DEV :]]
    for k in range(1, groups):
        block = sums[:, (k - 1) * BAND_DEV : k * BAND_DEV]
        parts.append(
            lax.ppermute(
                block, "row", [(r, (r + k * group) % row_total) for r in range(row_total)]
            )
        )
    return finish(density, parts)


def solution(mesh):
    placed = (P("sample"), P(), P(), P(), P(None, "row"))
    return jax.shard_map(
        per_device,
        mesh=mesh,
        in_specs=placed,
        out_specs=P(("sample", "row"), None),
        check_vma=False,
    )
```

time: 188 us -> 51.3 us (0.27)
  waiting for transfers between devices: 54.8 us -> 6.63 us
  local copies, waits for them, and re-layouts: 47.3 us -> 4.64 us
  matrix products: 40.1 us -> 0 us
  Pallas kernels: 0 us -> 30.5 us
  blocking collectives: 23.3 us -> 0 us
  between operations: 14.2 us -> 0.7 us
  starting transfers between devices: 0.01 us -> 8.48 us
  other arithmetic: 5.11 us -> 0 us
  loops' own time: 2.73 us -> 0 us
    reduce_scatter x1 -> x0, waiting for transfers between devices: 54.8 us -> none  [per_device(): lax.psum_scatter(blocks.reshape(band_dev * lax.axis_size('row'), columns)...]
    dot_general x6 -> x0, matrix products: 40.1 us -> none  [the longest x4 29.8 us: apply_tile(): lax.dot_general(tile, density_block, (((1,), (1,)), ((), ())), preferred_...]
    pallas_call x0 -> x3, Pallas kernels: none -> 30.5 us  [the longest x1 18.4 us: pairs(): pl.pallas_call(kernel, grid=(total // TGT_STEP,), out_shape=jax.ShapeDtyp...]
    gather x6 -> x0, local copies, waits for them, and re-layouts: 27.6 us -> none  [the longest x2 9.22 us: panel_geometry(): corner_two = vertices[:, corners[1]]]
    all_gather x1 -> x0, blocking collectives: 23.3 us -> none  [per_device(): lax.all_gather(own_centers[:, :band_dev], 'row', axis=1, tiled=True)]
    dynamic_update_slice x8 -> x0, local copies, waits for them, and re-layouts: 9.44 us -> none  [per_device(): lax.map(one_block, jnp.arange(band_dev * lax.axis_size('row') // block, d...]
    ppermute x0 -> x6, starting transfers between devices: none -> 8.48 us  [the longest x3 5.4 us: per_device(): lax.ppermute(block, 'row', [(r, (r + k * group) % row_total) for r in ran...]
    ppermute x0 -> x6, waiting for transfers between devices: none -> 6.63 us  [the longest x3 5.67 us: per_device(): lax.ppermute(block, 'row', [(r, (r + k * group) % row_total) for r in ran...]
  transfers between devices with their start and end apart: 1 -> 6, of which waited for: 1 -> 3; matrix products, arithmetic and copies ran while one was open for 0% -> 0% of each run, Pallas kernels for 0% -> 20%
where the time goes in v1:
time: 51.3 us; the launch traced here: 51 us
  Pallas kernels  30.5 us (59%)
  starting transfers between devices  8.48 us (17%)
  waiting for transfers between devices  6.63 us (13%)
  local copies, waits for them, and re-layouts  4.64 us (9%)
  between operations  0.7 us (1%)
    pallas_call x1, Pallas kernels, pairs(): pl.pallas_call(kernel, grid=(total // TGT_STEP,), out_shape=jax.ShapeDtyp...  18.4 us
    pallas_call x1, Pallas kernels, geometry(): pl.pallas_call(kernel, out_shape=[jax.ShapeDtypeStruct((FEATS, src_total)...  10.4 us
    ppermute x3, waiting for transfers between devices, per_device(): lax.ppermute(block, 'row', [(r, (r + k * group) % row_total) for r in ran...  5.67 us
    ppermute x3, starting transfers between devices, per_device(): lax.ppermute(block, 'row', [(r, (r + k * group) % row_total) for r in ran...  5.4 us
    ppermute x3, starting transfers between devices, per_device(): lax.ppermute(density, 'row', [(r, r ^ k) for r in range(row_total)])  3.08 us
    pallas_call x1, Pallas kernels, finish(): pl.pallas_call(kernel, grid=(1,), out_shape=jax.ShapeDtypeStruct((BAND_DE...  1.71 us
    pallas_call x1, local copies, waits for them, and re-layouts, finish(): pl.pallas_call(kernel, grid=(1,), out_shape=jax.ShapeDtypeStruct((BAND_DE...  1.62 us
    slice x1, local copies, waits for them, and re-layouts, per_device(): block = sums[:, (k - 1) * BAND_DEV:k * BAND_DEV]  1.58 us
  transfers between devices with their start and end apart: 6, of which 3 were waited for; matrix products, arithmetic and copies ran while one was open for 0% of the time, Pallas kernels for 20%

profile of v1, /device:TPU:0, one launch (start us, length us, event | category | flops | bytes accessed | tf_op | source)
XLA Modules:
  0.0 51.0 jit_solution(14049158193113050938)
XLA Ops:
  0.0 2.4 %collective-permute-start.2 = (bf16[64,2048]{1,0:T(8,128)(2,1)}, bf16[64,2048]{1,0:T(8,128)(2,1)S(1)}, u32[]{:S(2)}, u32[]{:S(2)}) collective-permute-start(bf16[64,2048]{1,0:T(8,128)(2,1)} %density_ref.1), channel_id=1, source_target_pairs={{0,3},{1,2},{2,1},{3,0},{4,7},{5,6},{6,5},{7,4},{8,11},{9,10},{10,... | collective-permute-start | bytes 786440 | tf_op jit(solution)/shard_map/ppermute | solution.py:354
  2.4 0.6 %collective-permute-start.1 = (bf16[64,2048]{1,0:T(8,128)(2,1)}, bf16[64,2048]{1,0:T(8,128)(2,1)S(1)}, u32[]{:S(2)}, u32[]{:S(2)}) collective-permute-start(bf16[64,2048]{1,0:T(8,128)(2,1)} %density_ref.1), channel_id=1, source_target_pairs={{0,2},{1,3},{2,0},{3,1},{4,6},{5,7},{6,4},{7,5},{8,10},{9,11},{10,... | collective-permute-start | bytes 786440 | tf_op jit(solution)/shard_map/ppermute | solution.py:354
  3.0 0.1 collective-permute-start
  3.7 10.4 %geometry.1 = (bf16[128,8192]{1,0:T(8,128)(2,1)}, bf16[128,8192]{1,0:T(8,128)(2,1)}, bf16[128,1024]{1,0:T(8,128)(2,1)}) custom-call(s32[1]{0:T(128)S(6)} %copy.10.refs_0_, s32[1,1024]{1,0:T(1,128)} %bitcast.1, s32[2,1024]{1,0:T(2,128)} %refs_2_.1, f32[32,512]{1,0:T(8,128)} %constant.6.clone.refs_3_, f32[256,64]{1,0:T(8,128)} %constant.7.clone.refs_4_, ...), custom_call_target="tpu_custom_call" | custom-call | tf_op jit(solution)/shard_map/geometry/pallas_call | solution.py:252
  14.1 0.0 collective-permute-done.2.refs_6_
  14.1 0.0 copy-start
  14.1 1.0 %collective-permute-done.1.refs_5_ = bf16[64,2048]{1,0:T(8,128)(2,1)S(1)} collective-permute-done((bf16[64,2048]{1,0:T(8,128)(2,1)}, bf16[64,2048]{1,0:T(8,128)(2,1)S(1)}, u32[]{:S(2)}, u32[]{:S(2)}) %collective-permute-start.1) | collective-permute-done | bytes 262176 | tf_op jit(solution)/shard_map/ppermute | solution.py:354
  15.1 0.0 copy-start.1
  15.1 0.0 collective-permute-done.refs_4_
  15.1 0.0 copy-start.2
  15.1 0.0 copy-done
  15.1 0.7 %copy-done.1 = bf16[64,2048]{1,0:T(8,128)(2,1)} copy-done((bf16[64,2048]{1,0:T(8,128)(2,1)}, bf16[64,2048]{1,0:T(8,128)(2,1)S(1)}, u32[]{:S(2)}) %copy-start.1) | copy-done | bytes 262168
  15.8 0.1 copy-done.2
  15.9 18.4 %pairs.1 = f32[64,1024]{1,0:T(8,128)} custom-call(bf16[128,8192]{1,0:T(8,128)(2,1)} %get-tuple-element.8.refs_0_, bf16[128,8192]{1,0:T(8,128)(2,1)} %get-tuple-element.9.refs_1_, bf16[128,1024]{1,0:T(8,128)(2,1)} %get-tuple-element.10.refs_2_, bf16[64,2048]{1,0:T(8,128)(2,1)} %density_ref.1, bf16[64,2048]{1,0:T(8,128)(2,1)} %copy-done.2, ...), custom_call_target="tpu_custom_call" | custom-call | tf_op jit(solution)/shard_map/pairs/pallas_call | solution.py:317
  34.3 1.6 %fusion = (f32[64,256]{1,0:T(8,128)S(1)}, f32[64,256]{1,0:T(8,128)S(1)}, f32[64,256]{1,0:T(8,128)S(1)}, f32[64,256]{1,0:T(8,128)}) fusion(f32[64,1024]{1,0:T(8,128)} %pairs.1), kind=kLoop, calls=%fused_computation | loop fusion | bytes 524288 | tf_op jit(solution)/shard_map/slice | solution.py:363
  35.9 4.4 %collective-permute-start.5 = (f32[64,256]{1,0:T(8,128)S(1)}, f32[64,256]{1,0:T(8,128)S(1)}, u32[]{:S(2)}, u32[]{:S(2)}) collective-permute-start(f32[64,256]{1,0:T(8,128)S(1)} %get-tuple-element.11), channel_id=1, source_target_pairs={{0,12},{1,13},{2,14},{3,15},{4,0},{5,1},{6,2},{7,3},{8,4},{9,5},{1... | collective-permute-start | bytes 196616 | tf_op jit(solution)/shard_map/ppermute | solution.py:365
  40.3 0.0 collective-permute-start.4
  40.3 1.0 %collective-permute-start.3 = (f32[64,256]{1,0:T(8,128)S(1)}, f32[64,256]{1,0:T(8,128)S(1)}, u32[]{:S(2)}, u32[]{:S(2)}) collective-permute-start(f32[64,256]{1,0:T(8,128)S(1)} %get-tuple-element.13), channel_id=1, source_target_pairs={{0,4},{1,5},{2,6},{3,7},{4,8},{5,9},{6,10},{7,11},{8,12},{9,13},{1... | collective-permute-start | bytes 196616 | tf_op jit(solution)/shard_map/ppermute | solution.py:365
  41.3 1.5 %collective-permute-done.5.refs_3_ = f32[64,256]{1,0:T(8,128)S(1)} collective-permute-done((f32[64,256]{1,0:T(8,128)S(1)}, f32[64,256]{1,0:T(8,128)S(1)}, u32[]{:S(2)}, u32[]{:S(2)}) %collective-permute-start.5) | collective-permute-done | bytes 65568 | tf_op jit(solution)/shard_map/ppermute | solution.py:365
  42.8 0.0 copy-start.3
  42.8 4.2 %collective-permute-done.4.refs_2_ = f32[64,256]{1,0:T(8,128)S(1)} collective-permute-done((f32[64,256]{1,0:T(8,128)S(1)}, f32[64,256]{1,0:T(8,128)S(1)}, u32[]{:S(2)}, u32[]{:S(2)}) %collective-permute-start.4) | collective-permute-done | bytes 65568 | tf_op jit(solution)/shard_map/ppermute | solution.py:365
  47.0 0.0 copy-start.4
  47.0 0.0 collective-permute-done.3.refs_1_
  47.0 0.0 copy-start.5
  47.0 0.0 copy-done.3
  47.0 0.6 %copy-done.4 = f32[64,256]{1,0:T(8,128)} copy-done((f32[64,256]{1,0:T(8,128)}, f32[64,256]{1,0:T(8,128)S(1)}, u32[]{:S(2)}) %copy-start.4) | copy-done | bytes 65560
  47.6 0.0 copy-done.5
  47.6 1.7 %finish.1 = f32[256,64]{1,0:T(8,128)} custom-call(bf16[64,2048]{1,0:T(8,128)(2,1)} %density_ref.1, f32[64,256]{1,0:T(8,128)} %get-tuple-element.14.refs_0_, f32[64,256]{1,0:T(8,128)} %copy-done.5, f32[64,256]{1,0:T(8,128)} %copy-done.4, f32[64,256]{1,0:T(8,128)} %copy-done.3), custom_call_target="tpu_custom_call" | custom-call | tf_op jit(solution)/shard_map/finish/pallas_call | solution.py:338
  49.3 1.6 %copy.9 = f32[256,64]{0,1:T(8,128)} copy(f32[256,64]{1,0:T(8,128)} %finish.1) | data formatting | bytes 131072 | tf_op jit(solution)/shard_map/finish/pallas_call | solution.py:338
Async XLA Ops:
  0.0 14.1 %collective-permute-start.2 = (bf16[64,2048]{1,0:T(8,128)(2,1)}, bf16[64,2048]{1,0:T(8,128)(2,1)S(1)}, u32[]{:S(2)}, u32[]{:S(2)}) collective-permute-start(bf16[64,2048]{1,0:T(8,128)(2,1)} %density_ref.1), channel_id=1, source_target_pairs={{0,3},{1,2},{2,1},{3,0},{4,7},{5,6},{6,5},{7,4},{8,11},{9,10},{10,... | collective-permute-start | bytes 786440 | tf_op jit(solution)/shard_map/ppermute | solution.py:354
  2.4 12.7 %collective-permute-start.1 = (bf16[64,2048]{1,0:T(8,128)(2,1)}, bf16[64,2048]{1,0:T(8,128)(2,1)S(1)}, u32[]{:S(2)}, u32[]{:S(2)}) collective-permute-start(bf16[64,2048]{1,0:T(8,128)(2,1)} %density_ref.1), channel_id=1, source_target_pairs={{0,2},{1,3},{2,0},{3,1},{4,6},{5,7},{6,4},{7,5},{8,10},{9,11},{10,... | collective-permute-start | bytes 786440 | tf_op jit(solution)/shard_map/ppermute | solution.py:354
  3.0 12.1 %collective-permute-start = (bf16[64,2048]{1,0:T(8,128)(2,1)}, bf16[64,2048]{1,0:T(8,128)(2,1)S(1)}, u32[]{:S(2)}, u32[]{:S(2)}) collective-permute-start(bf16[64,2048]{1,0:T(8,128)(2,1)} %density_ref.1), channel_id=1, source_target_pairs={{0,1},{1,0},{2,3},{3,2},{4,5},{5,4},{6,7},{7,6},{8,9},{9,8},{10,11... | collective-permute-start | bytes 786440 | tf_op jit(solution)/shard_map/ppermute | solution.py:354
  14.1 1.0 %copy-start = (bf16[64,2048]{1,0:T(8,128)(2,1)}, bf16[64,2048]{1,0:T(8,128)(2,1)S(1)}, u32[]{:S(2)}) copy-start(bf16[64,2048]{1,0:T(8,128)(2,1)S(1)} %collective-permute-done.2.refs_6_) | copy-start | bytes 786436
  15.1 0.7 %copy-start.1 = (bf16[64,2048]{1,0:T(8,128)(2,1)}, bf16[64,2048]{1,0:T(8,128)(2,1)S(1)}, u32[]{:S(2)}) copy-start(bf16[64,2048]{1,0:T(8,128)(2,1)S(1)} %collective-permute-done.1.refs_5_) | copy-start | bytes 786436
  15.1 0.8 %copy-start.2 = (bf16[64,2048]{1,0:T(8,128)(2,1)}, bf16[64,2048]{1,0:T(8,128)(2,1)S(1)}, u32[]{:S(2)}) copy-start(bf16[64,2048]{1,0:T(8,128)(2,1)S(1)} %collective-permute-done.refs_4_) | copy-start | bytes 786436
  35.9 6.9 %collective-permute-start.5 = (f32[64,256]{1,0:T(8,128)S(1)}, f32[64,256]{1,0:T(8,128)S(1)}, u32[]{:S(2)}, u32[]{:S(2)}) collective-permute-start(f32[64,256]{1,0:T(8,128)S(1)} %get-tuple-element.11), channel_id=1, source_target_pairs={{0,12},{1,13},{2,14},{3,15},{4,0},{5,1},{6,2},{7,3},{8,4},{9,5},{1... | collective-permute-start | bytes 196616 | tf_op jit(solution)/shard_map/ppermute | solution.py:365
  40.3 6.7 %collective-permute-start.4 = (f32[64,256]{1,0:T(8,128)S(1)}, f32[64,256]{1,0:T(8,128)S(1)}, u32[]{:S(2)}, u32[]{:S(2)}) collective-permute-start(f32[64,256]{1,0:T(8,128)S(1)} %get-tuple-element.12), channel_id=1, source_target_pairs={{0,8},{1,9},{2,10},{3,11},{4,12},{5,13},{6,14},{7,15},{8,0},{9,1},... | collective-permute-start | bytes 196616 | tf_op jit(solution)/shard_map/ppermute | solution.py:365
  40.3 6.7 %collective-permute-start.3 = (f32[64,256]{1,0:T(8,128)S(1)}, f32[64,256]{1,0:T(8,128)S(1)}, u32[]{:S(2)}, u32[]{:S(2)}) collective-permute-start(f32[64,256]{1,0:T(8,128)S(1)} %get-tuple-element.13), channel_id=1, source_target_pairs={{0,4},{1,5},{2,6},{3,7},{4,8},{5,9},{6,10},{7,11},{8,12},{9,13},{1... | collective-permute-start | bytes 196616 | tf_op jit(solution)/shard_map/ppermute | solution.py:365
  42.8 4.2 %copy-start.3 = (f32[64,256]{1,0:T(8,128)}, f32[64,256]{1,0:T(8,128)S(1)}, u32[]{:S(2)}) copy-start(f32[64,256]{1,0:T(8,128)S(1)} %collective-permute-done.5.refs_3_) | copy-start | bytes 196612
  47.0 0.6 %copy-start.4 = (f32[64,256]{1,0:T(8,128)}, f32[64,256]{1,0:T(8,128)S(1)}, u32[]{:S(2)}) copy-start(f32[64,256]{1,0:T(8,128)S(1)} %collective-permute-done.4.refs_2_) | copy-start | bytes 196612
  47.0 0.6 %copy-start.5 = (f32[64,256]{1,0:T(8,128)}, f32[64,256]{1,0:T(8,128)S(1)}, u32[]{:S(2)}) copy-start(f32[64,256]{1,0:T(8,128)S(1)} %collective-permute-done.3.refs_1_) | copy-start | bytes 196612

commit v2 on v1

--- a/solution.py
+++ b/solution.py
@@ -16,7 +16,7 @@
 FEATS = 128
 CHUNK = 1024
 SRC_STEP = 1024
-TGT_STEP = 1024
+TGT_STEP = 768
 VMEM = 56 << 20
 F32 = jnp.float32
 BF16 = jnp.bfloat16
@@ -141,7 +141,7 @@
 
 def geometry_kernel(
     row_total, group, sizes, sample_ref, lattice_ref, modes_ref, polar_ref, azim_ref, ring_ref,
-    connectivity_ref, dist_ref, flux_ref, target_ref, src_corners, tgt_corners, src_sems, tgt_sems,
+    connectivity_ref, dist_ref, flux_ref, far_ref, own_ref, src_corners, tgt_corners, src_sems, tgt_sems,
 ):
     pitch, width, first_cos, cycle_count = sizes
     src_total = src_corners.shape[1]
@@ -218,24 +218,27 @@
             ref[:, here] = both.astype(BF16)
         return carry
 
-    def targets(step, carry):
-        here = pl.ds(pl.multiple_of(step * CHUNK, CHUNK), CHUNK)
-        centers, _ = panels(tgt_corners[:, here], table, pitch, width)
-        ones = jnp.ones((3, CHUNK), F32)
+    def targets(corners):
+        count = corners.shape[1]
+        centers, _ = panels(corners, table, pitch, width)
+        ones = jnp.ones((3, count), F32)
         rows = []
         for origin in (north, south):
             offset = centers - jnp.concatenate(
-                [jnp.zeros((2, CHUNK), F32), jnp.broadcast_to(origin, (1, CHUNK))], axis=0
+                [jnp.zeros((2, count), F32), jnp.broadcast_to(origin, (1, count))], axis=0
             )
             square = jnp.sum(offset * offset, axis=0, keepdims=True)
             o_one, o_two, o_three = split(offset)
             rows += [o_one, o_one, o_one, o_two, o_two, o_three, pieces_of(square), ones]
-        rows.append(jnp.zeros((FEATS - 2 * HALF, CHUNK), F32))
-        target_ref[:, here] = jnp.concatenate(rows, axis=0).astype(BF16)
-        return carry
-
+        rows.append(jnp.zeros((FEATS - 2 * HALF, count), F32))
+        return jnp.concatenate(rows, axis=0).astype(BF16)
+
+    far_total = far_ref.shape[1]
+    for first in range(0, far_total, TGT_STEP):
+        count = min(TGT_STEP, far_total - first)
+        far_ref[:, first : first + count] = targets(tgt_corners[:, first : first + count])
+    own_ref[...] = targets(tgt_corners[:, far_total:])
     lax.fori_loop(0, src_total // CHUNK, sources, 0)
-    lax.fori_loop(0, tgt_corners.shape[1] // CHUNK, targets, 0)
 
 
 def geometry(sample_index, lattice_vector, mode_table, connectivity, row_total, group, src_dev):
@@ -254,10 +257,11 @@
         out_shape=[
             jax.ShapeDtypeStruct((FEATS, src_total), BF16),
             jax.ShapeDtypeStruct((FEATS, src_total), BF16),
-            jax.ShapeDtypeStruct((FEATS, tgt_total), BF16),
+            jax.ShapeDtypeStruct((FEATS, tgt_total - BAND_DEV), BF16),
+            jax.ShapeDtypeStruct((FEATS, BAND_DEV), BF16),
         ],
         in_specs=[pl.BlockSpec(memory_space=pltpu.SMEM)] + [vmem] * 5 + [pl.BlockSpec(memory_space=pl.ANY)],
-        out_specs=[vmem] * 3,
+        out_specs=[vmem] * 4,
         scratch_shapes=[
             pltpu.VMEM((3, src_total), jnp.int32),
             pltpu.VMEM((3, tgt_total), jnp.int32),
@@ -272,77 +276,71 @@
     )
 
 
-def pairs_kernel(group, dist_ref, flux_ref, target_ref, *refs):
-    density_refs, sums_ref = refs[:group], refs[group]
+def pairs_kernel(group, own, dist_ref, flux_ref, target_ref, *refs):
+    density_refs, sums_refs, total_ref = refs[:group], refs[group:-1], refs[-1]
     src_dev = density_refs[0].shape[1]
-    last = pl.program_id(0) == pl.num_programs(0) - 1
-    target = target_ref[...]
+    tgt_total = target_ref.shape[1]
+    width = min(TGT_STEP, tgt_total)
+    src_step = min(src_dev, SRC_STEP * TGT_STEP // width // 2 * 2)
     diagonal = lax.broadcasted_iota(jnp.int32, (BAND_DEV, BAND_DEV), 0) == lax.broadcasted_iota(
         jnp.int32, (BAND_DEV, BAND_DEV), 1
     )
-    sums_ref[...] = jnp.zeros_like(sums_ref)
-    for k in range(group):
-
-        def step(turn, carry, k=k):
-            inside = pl.multiple_of(turn * SRC_STEP, SRC_STEP)
-            here = pl.ds(pl.multiple_of(k * src_dev + turn * SRC_STEP, SRC_STEP), SRC_STEP)
-            contract = (((0,), (0,)), ((), ()))
-            dist_sq = lax.dot_general(dist_ref[:, here], target, contract, preferred_element_type=F32)
-            flux = lax.dot_general(flux_ref[:, here], target, contract, preferred_element_type=F32)
-            if k == 0:
-                far = jnp.where(last & (turn == 0), 1e30, 0.0)
-                apart = jnp.where(diagonal, far, 0.0)
-                top = jnp.concatenate(
-                    [dist_sq[:BAND_DEV, :-BAND_DEV], dist_sq[:BAND_DEV, -BAND_DEV:] + apart], axis=1
+    contract = (((0,), (0,)), ((), ()))
+    for first in range(0, tgt_total, width):
+        target = target_ref[:, first : first + width]
+        total_ref[...] = jnp.zeros_like(total_ref)
+        for k in range(group):
+
+            def step(turn, carry, k=k, target=target):
+                inside = pl.multiple_of(turn * src_step, src_step)
+                here = pl.ds(pl.multiple_of(k * src_dev + turn * src_step, src_step), src_step)
+                dist_sq = lax.dot_general(
+                    dist_ref[:, here], target, contract, preferred_element_type=F32
                 )
-                dist_sq = jnp.concatenate([top, dist_sq[BAND_DEV:]], axis=0)
-            inverse = lax.rsqrt(dist_sq)
-            tile = (flux * inverse * (inverse * inverse)).astype(BF16)
-            sums_ref[...] += jnp.dot(
-                density_refs[k][:, pl.ds(inside, SRC_STEP)], tile, preferred_element_type=F32
-            )
-            return carry
-
-        lax.fori_loop(0, src_dev // SRC_STEP, step, 0)
-
-
-def pairs(dist, flux, target, densities):
+                flux = lax.dot_general(
+                    flux_ref[:, here], target, contract, preferred_element_type=F32
+                )
+                if own and k == 0:
+                    far = jnp.where(turn == 0, 1e30, 0.0)
+                    apart = jnp.where(diagonal, far, 0.0)
+                    dist_sq = jnp.concatenate(
+                        [dist_sq[:BAND_DEV] + apart, dist_sq[BAND_DEV:]], axis=0
+                    )
+                inverse = lax.rsqrt(dist_sq)
+                tile = (flux * inverse * (inverse * inverse)).astype(BF16)
+                total_ref[...] += jnp.dot(
+                    density_refs[k][:, pl.ds(inside, src_step)], tile, preferred_element_type=F32
+                )
+                return carry
+
+            lax.fori_loop(0, src_dev // src_step, step, 0)
+        for block in range(width // BAND_DEV):
+            sums_refs[first // BAND_DEV + block][...] = total_ref[
+                :, block * BAND_DEV : (block + 1) * BAND_DEV
+            ]
+
+
+def pairs(dist, flux, target, densities, own):
     columns = densities[0].shape[0]
     total = target.shape[1]
     vmem = pl.BlockSpec(memory_space=pltpu.VMEM)
+    blocks = total // BAND_DEV
 
     def kernel(*refs):
-        pairs_kernel(len(densities), *refs)
+        pairs_kernel(len(densities), own, *refs)
 
     return pl.pallas_call(
         kernel,
-        grid=(total // TGT_STEP,),
-        out_shape=jax.ShapeDtypeStruct((columns, total), F32),
-        in_specs=[vmem, vmem, pl.BlockSpec((FEATS, TGT_STEP), lambda t: (0, t))]
-        + [vmem] * len(densities),
-        out_specs=pl.BlockSpec((columns, TGT_STEP), lambda t: (0, t)),
+        out_shape=[jax.ShapeDtypeStruct((columns, BAND_DEV), F32)] * blocks,
+        in_specs=[vmem] * (3 + len(densities)),
+        out_specs=[vmem] * blocks,
+        scratch_shapes=[pltpu.VMEM((columns, min(TGT_STEP, total)), F32)],
         compiler_params=pltpu.CompilerParams(vmem_limit_bytes=VMEM),
-        name="pairs",
+        cost_estimate=pl.CostEstimate(
+            flops=2 * total * dist.shape[1] * 256, bytes_accessed=1 << 20, transcendentals=0
+        ),
+        name="pairs_own" if own else "pairs_far",
     )(dist, flux, target, *densities)
-
-
-def finish(density, parts):
-    def kernel(density_ref, *refs):
-        total = 0.5 * density_ref[...].astype(F32)
-        for ref in refs[:-1]:
-            total = total + ref[...]
-        refs[-1][...] = total.T
-
-    columns = density.shape[0]
-    block = pl.BlockSpec((columns, BAND_DEV), lambda i: (0, 0))
-    return pl.pallas_call(
-        kernel,
-        grid=(1,),
-        out_shape=jax.ShapeDtypeStruct((BAND_DEV, columns), F32),
-        in_specs=[block] * (1 + len(parts)),
-        out_specs=pl.BlockSpec((BAND_DEV, columns), lambda i: (0, 0)),
-        name="finish",
-    )(density, *parts)
 
 
 def per_device(sample_index, lattice_vector, mode_table, connectivity, density):
@@ -354,19 +352,21 @@
         lax.ppermute(density, "row", [(r, r ^ k) for r in range(row_total)])
         for k in range(1, group)
     ]
-    dist, flux, target = geometry(
+    dist, flux, target_far, target_own = geometry(
         sample_index, lattice_vector, mode_table, connectivity, row_total, group, src_dev
     )
-    sums = pairs(dist, flux, target, densities)
-    parts = [sums[:, (groups - 1) * BAND_DEV :]]
-    for k in range(1, groups):
-        block = sums[:, (k - 1) * BAND_DEV : k * BAND_DEV]
-        parts.append(
-            lax.ppermute(
-                block, "row", [(r, (r + k * group) % row_total) for r in range(row_total)]
-            )
-        )
-    return finish(density, parts)
+    sums = pairs(dist, flux, target_far, densities, False)
+    parts = [
+        lax.ppermute(
+            block, "row", [(r, (r + (k + 1) * group) % row_total) for r in range(row_total)]
+        )
+        for k, block in enumerate(sums)
+    ]
+    total = 0.5 * density[:, :BAND_DEV].astype(F32)
+    total = total + pairs(dist, flux, target_own, densities, True)[0]
+    for part in parts:
+        total = total + part
+    return total.T
 
 
 def solution(mesh):

time: 51.3 us -> 44 us (0.86)
  waiting for transfers between devices: 6.63 us -> 0.02 us
  local copies, waits for them, and re-layouts: 4.64 us -> 0.86 us
  other arithmetic: 0 us -> 1.49 us
  Pallas kernels: 30.5 us -> 31.4 us
  starting transfers between devices: 8.48 us -> 9.31 us
    ppermute x3, waiting for transfers between devices: 5.67 us -> 0.01 us  [per_device(): lax.ppermute(block, 'row', [(r, (r + (k + 1) * group) % row_total) for r...]
    pallas_call x1 -> x0, local copies, waits for them, and re-layouts: 1.62 us -> none  [finish(): pl.pallas_call(kernel, grid=(1,), out_shape=jax.ShapeDtypeStruct((BAND_DE...]
    slice x1 -> x0, local copies, waits for them, and re-layouts: 1.58 us -> none  [per_device(): block = sums[:, (k - 1) * BAND_DEV:k * BAND_DEV]]
    transpose x0 -> x1, other arithmetic: none -> 1.49 us  [per_device(): return total.T]
    ppermute x3, waiting for transfers between devices: 0.97 us -> 0.01 us  [per_device(): lax.ppermute(density, 'row', [(r, r ^ k) for r in range(row_total)])]
    pallas_call x1, Pallas kernels: 10.4 us -> 11.3 us  [geometry(): pl.pallas_call(kernel, out_shape=[jax.ShapeDtypeStruct((FEATS, src_total)...]
    ppermute x3, starting transfers between devices: 5.4 us -> 6.23 us  [per_device(): lax.ppermute(block, 'row', [(r, (r + (k + 1) * group) % row_total) for r...]
    unnamed x12 -> x6, local copies, waits for them, and re-layouts: 1.44 us -> 0.86 us
  transfers between devices with their start and end apart: 6 -> 6, of which waited for: 3 -> 0; matrix products, arithmetic and copies ran while one was open for 0% -> 0% of each run, Pallas kernels for 20% -> 40%
where the time goes in v2:
time: 44 us; the launch traced here: 43.9 us
  Pallas kernels  31.4 us (71%)
  starting transfers between devices  9.31 us (21%)
  other arithmetic  1.49 us (3%)
  local copies, waits for them, and re-layouts  0.86 us (2%)
  between operations  0.72 us (2%)
    pallas_call x2, Pallas kernels, pairs(): pl.pallas_call(kernel, out_shape=[jax.ShapeDtypeStruct((columns, BAND_DEV...  20.1 us
    pallas_call x1, Pallas kernels, geometry(): pl.pallas_call(kernel, out_shape=[jax.ShapeDtypeStruct((FEATS, src_total)...  11.3 us
    ppermute x3, starting transfers between devices, per_device(): lax.ppermute(block, 'row', [(r, (r + (k + 1) * group) % row_total) for r...  6.23 us
    ppermute x3, starting transfers between devices, per_device(): lax.ppermute(density, 'row', [(r, r ^ k) for r in range(row_total)])  3.08 us
    transpose x1, other arithmetic, per_device(): return total.T  1.49 us
  transfers between devices with their start and end apart: 6, of which 0 were waited for; matrix products, arithmetic and copies ran while one was open for 0% of the time, Pallas kernels for 40%

profile of v2, /device:TPU:0, one launch (start us, length us, event | category | flops | bytes accessed | tf_op | source)
XLA Modules:
  0.0 43.9 jit_solution(13382251879546717641)
XLA Ops:
  0.0 2.4 %collective-permute-start.2 = (bf16[64,2048]{1,0:T(8,128)(2,1)}, bf16[64,2048]{1,0:T(8,128)(2,1)S(1)}, u32[]{:S(2)}, u32[]{:S(2)}) collective-permute-start(bf16[64,2048]{1,0:T(8,128)(2,1)} %refs_3_.4), channel_id=1, source_target_pairs={{0,3},{1,2},{2,1},{3,0},{4,7},{5,6},{6,5},{7,4},{8,11},{9,10},{10,... | collective-permute-start | bytes 786440 | tf_op jit(solution)/shard_map/ppermute | solution.py:352
  2.4 0.6 %collective-permute-start.1 = (bf16[64,2048]{1,0:T(8,128)(2,1)}, bf16[64,2048]{1,0:T(8,128)(2,1)S(1)}, u32[]{:S(2)}, u32[]{:S(2)}) collective-permute-start(bf16[64,2048]{1,0:T(8,128)(2,1)} %refs_3_.4), channel_id=1, source_target_pairs={{0,2},{1,3},{2,0},{3,1},{4,6},{5,7},{6,4},{7,5},{8,10},{9,11},{10,... | collective-permute-start | bytes 786440 | tf_op jit(solution)/shard_map/ppermute | solution.py:352
  3.0 0.1 collective-permute-start
  3.7 11.3 %geometry.1 = (bf16[128,8192]{1,0:T(8,128)(2,1)}, bf16[128,8192]{1,0:T(8,128)(2,1)}, bf16[128,768]{1,0:T(8,128)(2,1)}, bf16[128,256]{1,0:T(8,128)(2,1)}) custom-call(s32[1]{0:T(128)S(6)} %copy.9.refs_0_, s32[1,1024]{1,0:T(1,128)} %bitcast.3, s32[2,1024]{1,0:T(2,128)} %refs_2_.1, f32[32,512]{1,0:T(8,128)} %constant.8.clone.refs_3_, ...), custom_call_target="tpu_custom_call" | custom-call | tf_op jit(solution)/shard_map/geometry/pallas_call | solution.py:255
  15.1 0.0 collective-permute-done.2.refs_6_
  15.1 0.0 copy-start
  15.1 0.0 collective-permute-done.1.refs_5_
  15.1 0.0 copy-start.1
  15.1 0.0 collective-permute-done.refs_4_
  15.1 0.0 copy-start.2
  15.1 0.7 %copy-done = bf16[64,2048]{1,0:T(8,128)(2,1)} copy-done((bf16[64,2048]{1,0:T(8,128)(2,1)}, bf16[64,2048]{1,0:T(8,128)(2,1)S(1)}, u32[]{:S(2)}) %copy-start) | copy-done | bytes 262168
  15.8 0.1 copy-done.1
  15.9 0.1 copy-done.2
  16.0 13.8 %pairs_far.1 = (f32[64,256]{1,0:T(8,128)}, f32[64,256]{1,0:T(8,128)}, f32[64,256]{1,0:T(8,128)}) custom-call(bf16[128,8192]{1,0:T(8,128)(2,1)} %get-tuple-element.12.refs_0_, bf16[128,8192]{1,0:T(8,128)(2,1)} %get-tuple-element.13.refs_1_, bf16[128,768]{1,0:T(8,128)(2,1)} %get-tuple-element.15.refs_2_, bf16[64,2048]{1,0:T(8,128)(2,1)} %refs_3_.4, ...), custom_call_target="tpu_custom_call" | custom-call | flops 3221225472 | bytes 1048576 | tf_op jit(solution)/shard_map/pairs_far/pallas_call | solution.py:332
  29.8 2.3 %collective-permute-start.3 = (f32[64,256]{1,0:T(8,128)}, f32[64,256]{1,0:T(8,128)S(1)}, u32[]{:S(2)}, u32[]{:S(2)}) collective-permute-start(f32[64,256]{1,0:T(8,128)} %get-tuple-element.16), channel_id=1, source_target_pairs={{0,4},{1,5},{2,6},{3,7},{4,8},{5,9},{6,10},{7,11},{8,12},{9,13},{1... | collective-permute-start | bytes 196616 | tf_op jit(solution)/shard_map/ppermute | solution.py:360
  32.1 2.6 %collective-permute-start.4 = (f32[64,256]{1,0:T(8,128)}, f32[64,256]{1,0:T(8,128)S(1)}, u32[]{:S(2)}, u32[]{:S(2)}) collective-permute-start(f32[64,256]{1,0:T(8,128)} %get-tuple-element.17), channel_id=1, source_target_pairs={{0,8},{1,9},{2,10},{3,11},{4,12},{5,13},{6,14},{7,15},{8,0},{9,1},... | collective-permute-start | bytes 196616 | tf_op jit(solution)/shard_map/ppermute | solution.py:360
  34.7 1.4 %collective-permute-start.5 = (f32[64,256]{1,0:T(8,128)}, f32[64,256]{1,0:T(8,128)S(1)}, u32[]{:S(2)}, u32[]{:S(2)}) collective-permute-start(f32[64,256]{1,0:T(8,128)} %get-tuple-element.18), channel_id=1, source_target_pairs={{0,12},{1,13},{2,14},{3,15},{4,0},{5,1},{6,2},{7,3},{8,4},{9,5},{1... | collective-permute-start | bytes 196616 | tf_op jit(solution)/shard_map/ppermute | solution.py:360
  36.0 6.3 %pairs_own.1 = f32[64,256]{1,0:T(8,128)} custom-call(bf16[128,8192]{1,0:T(8,128)(2,1)} %get-tuple-element.12.refs_0_, bf16[128,8192]{1,0:T(8,128)(2,1)} %get-tuple-element.13.refs_1_, bf16[128,256]{1,0:T(8,128)(2,1)} %get-tuple-element.14.refs_2_, bf16[64,2048]{1,0:T(8,128)(2,1)} %refs_3_.4, bf16[64,2048]{1,0:T(8,128)(2,1)} %copy-done.2, ...), custom_call_target="tpu_custom_call" | custom-call | flops 1073741824 | bytes 1048576 | tf_op jit(solution)/shard_map/pairs_own/pallas_call | solution.py:332
  42.3 0.0 collective-permute-done.3
  42.3 0.0 collective-permute-done.4
  42.3 0.0 collective-permute-done.5
  42.4 1.5 %add_bitcast_fusion = f32[256,64]{0,1:T(8,128)} fusion(f32[64,256]{1,0:T(8,128)S(1)} %collective-permute-done.5, f32[64,256]{1,0:T(8,128)S(1)} %collective-permute-done.4, f32[64,256]{1,0:T(8,128)S(1)} %collective-permute-done.3, f32[64,256]{1,0:T(8,128)} %pairs_own.1, bf16[64,2048]{1,0:T(8,128)(2,1)} %refs_3_.4), kind=kLoop, calls=%fused_computation | loop fusion | flops 98304 | bytes 360448 | tf_op jit(solution)/shard_map/transpose | solution.py:369
Async XLA Ops:
  0.0 15.1 %collective-permute-start.2 = (bf16[64,2048]{1,0:T(8,128)(2,1)}, bf16[64,2048]{1,0:T(8,128)(2,1)S(1)}, u32[]{:S(2)}, u32[]{:S(2)}) collective-permute-start(bf16[64,2048]{1,0:T(8,128)(2,1)} %refs_3_.4), channel_id=1, source_target_pairs={{0,3},{1,2},{2,1},{3,0},{4,7},{5,6},{6,5},{7,4},{8,11},{9,10},{10,... | collective-permute-start | bytes 786440 | tf_op jit(solution)/shard_map/ppermute | solution.py:352
  2.4 12.7 %collective-permute-start.1 = (bf16[64,2048]{1,0:T(8,128)(2,1)}, bf16[64,2048]{1,0:T(8,128)(2,1)S(1)}, u32[]{:S(2)}, u32[]{:S(2)}) collective-permute-start(bf16[64,2048]{1,0:T(8,128)(2,1)} %refs_3_.4), channel_id=1, source_target_pairs={{0,2},{1,3},{2,0},{3,1},{4,6},{5,7},{6,4},{7,5},{8,10},{9,11},{10,... | collective-permute-start | bytes 786440 | tf_op jit(solution)/shard_map/ppermute | solution.py:352
  3.0 12.1 %collective-permute-start = (bf16[64,2048]{1,0:T(8,128)(2,1)}, bf16[64,2048]{1,0:T(8,128)(2,1)S(1)}, u32[]{:S(2)}, u32[]{:S(2)}) collective-permute-start(bf16[64,2048]{1,0:T(8,128)(2,1)} %refs_3_.4), channel_id=1, source_target_pairs={{0,1},{1,0},{2,3},{3,2},{4,5},{5,4},{6,7},{7,6},{8,9},{9,8},{10,11... | collective-permute-start | bytes 786440 | tf_op jit(solution)/shard_map/ppermute | solution.py:352
  15.1 0.7 %copy-start = (bf16[64,2048]{1,0:T(8,128)(2,1)}, bf16[64,2048]{1,0:T(8,128)(2,1)S(1)}, u32[]{:S(2)}) copy-start(bf16[64,2048]{1,0:T(8,128)(2,1)S(1)} %collective-permute-done.2.refs_6_) | copy-start | bytes 786436
  15.1 0.8 %copy-start.1 = (bf16[64,2048]{1,0:T(8,128)(2,1)}, bf16[64,2048]{1,0:T(8,128)(2,1)S(1)}, u32[]{:S(2)}) copy-start(bf16[64,2048]{1,0:T(8,128)(2,1)S(1)} %collective-permute-done.1.refs_5_) | copy-start | bytes 786436
  15.1 0.9 %copy-start.2 = (bf16[64,2048]{1,0:T(8,128)(2,1)}, bf16[64,2048]{1,0:T(8,128)(2,1)S(1)}, u32[]{:S(2)}) copy-start(bf16[64,2048]{1,0:T(8,128)(2,1)S(1)} %collective-permute-done.refs_4_) | copy-start | bytes 786436
  29.8 12.5 %collective-permute-start.3 = (f32[64,256]{1,0:T(8,128)}, f32[64,256]{1,0:T(8,128)S(1)}, u32[]{:S(2)}, u32[]{:S(2)}) collective-permute-start(f32[64,256]{1,0:T(8,128)} %get-tuple-element.16), channel_id=1, source_target_pairs={{0,4},{1,5},{2,6},{3,7},{4,8},{5,9},{6,10},{7,11},{8,12},{9,13},{1... | collective-permute-start | bytes 196616 | tf_op jit(solution)/shard_map/ppermute | solution.py:360
  32.1 10.2 %collective-permute-start.4 = (f32[64,256]{1,0:T(8,128)}, f32[64,256]{1,0:T(8,128)S(1)}, u32[]{:S(2)}, u32[]{:S(2)}) collective-permute-start(f32[64,256]{1,0:T(8,128)} %get-tuple-element.17), channel_id=1, source_target_pairs={{0,8},{1,9},{2,10},{3,11},{4,12},{5,13},{6,14},{7,15},{8,0},{9,1},... | collective-permute-start | bytes 196616 | tf_op jit(solution)/shard_map/ppermute | solution.py:360
  34.7 7.7 %collective-permute-start.5 = (f32[64,256]{1,0:T(8,128)}, f32[64,256]{1,0:T(8,128)S(1)}, u32[]{:S(2)}, u32[]{:S(2)}) collective-permute-start(f32[64,256]{1,0:T(8,128)} %get-tuple-element.18), channel_id=1, source_target_pairs={{0,12},{1,13},{2,14},{3,15},{4,0},{5,1},{6,2},{7,3},{8,4},{9,5},{1... | collective-permute-start | bytes 196616 | tf_op jit(solution)/shard_map/ppermute | solution.py:360

commit v3 on v2

v3 whole, which is shorter than its diff:
```python
import math

import jax
import jax.numpy as jnp
import numpy as np
from jax import lax
from jax.experimental import pallas as pl
from jax.experimental.pallas import tpu as pltpu
from jax.sharding import PartitionSpec as P

NLAT = 32768
NPH = 256
BAND_DEV = 256
FREQS = 32
HALF = 24
FEATS = 2 * HALF
CHUNK = 1024
TGT_STEP = 768
VMEM = 30 << 20
F32 = jnp.float32
BF16 = jnp.bfloat16


def split(values):
    first = values.astype(BF16).astype(F32)
    rest = values - first
    second = rest.astype(BF16).astype(F32)
    third = (rest - second).astype(BF16).astype(F32)
    return first, second, third


def split_host(values):
    first = values.astype(jnp.bfloat16).astype(np.float64)
    second = (values - first).astype(jnp.bfloat16).astype(np.float64)
    third = (values - first - second).astype(jnp.bfloat16).astype(np.float64)
    return first, second, third


def trig_tables(cycle_count):
    pitch = -(-cycle_count // 16) * 16
    width = -(-3 * pitch // 128) * 128
    lanes = np.arange(width)
    cycle = lanes % pitch
    piece = lanes // pitch
    inside = (cycle < cycle_count) & (piece < 3)
    polar = np.pi * (cycle + 1.0) / (cycle_count + 1)
    freq = np.arange(FREQS)[:, None]
    polar_table = np.concatenate(
        [np.cos(freq * polar) * inside, -np.sin(freq * polar) * inside], axis=1
    ).astype(np.float32)
    azimuth = 2.0 * np.pi * np.arange(NPH)[:, None] / NPH
    azim_freq = np.arange(FREQS)[None, :] - FREQS // 2
    azim_table = np.concatenate(
        [np.cos(azimuth * azim_freq), np.sin(azimuth * azim_freq)], axis=1
    ).astype(np.float32)
    ring = np.zeros((16, width))
    for row, values in enumerate((np.sin(polar), np.cos(polar))):
        for which, part in enumerate(split_host(values.astype(np.float32).astype(np.float64))):
            ring[row] += part * (inside & (piece == which))
    first_cos = float(np.cos(np.pi / (cycle_count + 1)))
    return pitch, width, polar_table, azim_table, ring.astype(jnp.bfloat16), first_cos


def radius_table(sample, lattice, modes, polar_table, azim_table, width):
    shifts = ((sample * lattice) & (NLAT - 1)).astype(F32) / NLAT - 0.5
    polar_freq = modes[0:1, :]
    azim_freq = modes[1:2, :]
    scale = (1 + polar_freq + jnp.abs(azim_freq)).astype(F32)
    coef = 0.8 * shifts / (scale * scale)
    numbers = lax.broadcasted_iota(jnp.int32, (FREQS, modes.shape[1]), 0)
    at_azim = numbers == azim_freq + FREQS // 2
    at_polar = jnp.where(numbers == polar_freq, 1.0, 0.0).astype(BF16)
    pieces = jnp.concatenate([jnp.where(at_azim, part, 0.0) for part in split(coef)], axis=0)
    grid = lax.dot_general(
        pieces.astype(BF16), at_polar, (((1,), (1,)), ((), ())), preferred_element_type=F32
    )
    grid = grid[:FREQS] + grid[FREQS : 2 * FREQS] + grid[2 * FREQS :]
    both = jnp.dot(grid, polar_table, precision=lax.Precision.HIGHEST, preferred_element_type=F32)
    stacked = jnp.concatenate([both[:, :width], both[:, width:]], axis=0)
    return jnp.exp(
        jnp.dot(azim_table, stacked, precision=lax.Precision.HIGHEST, preferred_element_type=F32)
    )


def azimuth_trig(column):
    quarter = (column + NPH // 8) >> 6
    angle = (column - (quarter << 6)).astype(F32) * (2.0 * math.pi / NPH)
    sq = angle * angle
    sin = angle * (
        1.0 + sq * (-1.0 / 6 + sq * (1.0 / 120 + sq * (-1.0 / 5040 + sq * (1.0 / 362880))))
    )
    cos = 1.0 + sq * (
        -0.5 + sq * (1.0 / 24 + sq * (-1.0 / 720 + sq * (1.0 / 40320 - sq * (1.0 / 3628800))))
    )
    odd = (quarter & 1) == 1
    cos_sign = jnp.where(((quarter + 1) & 2) == 2, -1.0, 1.0)
    sin_sign = jnp.where((quarter & 2) == 2, -1.0, 1.0)
    return jnp.where(odd, sin, cos) * cos_sign, jnp.where(odd, cos, sin) * sin_sign


def lookup(table, cycle, column, pitch, width):
    count = cycle.shape[1]
    hot = jnp.where(
        lax.broadcasted_iota(jnp.int32, (pitch, count), 0) == cycle, 1.0, 0.0
    ).astype(BF16)
    parts = [hot, hot, hot]
    if width > 3 * pitch:
        parts.append(jnp.zeros((width - 3 * pitch, count), BF16))
    found = jnp.dot(table, jnp.concatenate(parts, axis=0), preferred_element_type=F32)
    rows = found[:NPH]
    size = NPH // 2
    while size >= 8:
        rows = jnp.where((column & size) != 0, rows[size:], rows[:size])
        size //= 2
    low = lax.broadcasted_iota(jnp.int32, (8, count), 0) == (column & 7)
    radius = jnp.sum(jnp.where(low, rows, 0.0), axis=0, keepdims=True)
    return radius, found[NPH : NPH + 1], found[NPH + 1 : NPH + 2]


def panels(corners, table, pitch, width):
    column = corners & (NPH - 1)
    cycle = corners >> 8
    cos, sin = azimuth_trig(column)
    points = []
    for c in range(3):
        one = slice(c, c + 1)
        radius, ring_sin, ring_cos = lookup(table, cycle[one], column[one], pitch, width)
        flat = radius * ring_sin
        points.append((flat * cos[one], flat * sin[one], radius * ring_cos))
    centers = [(points[0][d] + points[1][d] + points[2][d]) / 3.0 for d in range(3)]
    one = [points[1][d] - points[0][d] for d in range(3)]
    two = [points[2][d] - points[0][d] for d in range(3)]
    half = 0.5 / (4.0 * math.pi)
    areas = [
        half * (one[(d + 1) % 3] * two[(d + 2) % 3] - one[(d + 2) % 3] * two[(d + 1) % 3])
        for d in range(3)
    ]
    return jnp.concatenate(centers, axis=0), jnp.concatenate(areas, axis=0)


def pieces_of(values):
    return jnp.concatenate(split(values), axis=0)


def target_features(corners, table, north, south, pitch, width):
    count = corners.shape[1]
    centers, _ = panels(corners, table, pitch, width)
    ones = jnp.ones((3, count), F32)
    rows = []
    for origin in (north, south):
        offset = centers - jnp.concatenate(
            [jnp.zeros((2, count), F32), jnp.broadcast_to(origin, (1, count))], axis=0
        )
        square = jnp.sum(offset * offset, axis=0, keepdims=True)
        one, two, three = split(offset)
        rows += [one, one, one, two, two, three, pieces_of(square), ones]
    return jnp.concatenate(rows, axis=0).astype(BF16)


def source_features(corners, table, north, south, pitch, width):
    count = corners.shape[1]
    centers, areas = panels(corners, table, pitch, width)
    upper = centers[2:3] >= 0.0
    offset = centers - jnp.concatenate(
        [jnp.zeros((2, count), F32), jnp.where(upper, north, south)], axis=0
    )
    square = jnp.sum(offset * offset, axis=0, keepdims=True)
    level = jnp.sum(offset * areas, axis=0, keepdims=True)
    ones = jnp.ones((3, count), F32)
    found = []
    for (one, two, three), flat, last in (
        (split(-2.0 * offset), ones, square),
        (split(areas), 0.0 * ones, -level),
    ):
        values = jnp.concatenate([one, two, three, one, two, one, flat, pieces_of(last)], axis=0)
        both = jnp.concatenate(
            [jnp.where(upper, values, 0.0), jnp.where(upper, 0.0, values)], axis=0
        )
        found.append(both.astype(BF16))
    return found


def pair_sums(dist, flux, target, density, apart=None):
    contract = (((0,), (0,)), ((), ()))
    dist_sq = lax.dot_general(dist, target, contract, preferred_element_type=F32)
    flow = lax.dot_general(flux, target, contract, preferred_element_type=F32)
    if apart is not None:
        dist_sq = jnp.concatenate([dist_sq[:BAND_DEV] + apart, dist_sq[BAND_DEV:]], axis=0)
    inverse = lax.rsqrt(dist_sq)
    tile = (flow * inverse * (inverse * inverse)).astype(BF16)
    return jnp.dot(density, tile, preferred_element_type=F32)


def far_steps(corners_ref, density_ref, target_ref, total_ref, dist_ref, flux_ref, features):
    src_total = corners_ref.shape[1]
    tgt_total = target_ref.shape[1]
    chunk = min(CHUNK, src_total)
    steps = src_total // chunk
    tgt_steps = tgt_total // TGT_STEP if tgt_total % TGT_STEP == 0 else tgt_total // BAND_DEV
    tgt_step = tgt_total // tgt_steps

    def make(turn):
        here = pl.ds(pl.multiple_of(turn * chunk, chunk), chunk)
        dist, flux = features(corners_ref[:, here])
        dist_ref[:, here] = dist
        flux_ref[:, here] = flux
        return dist, flux

    def apply(turn, dist, flux):
        here = pl.ds(pl.multiple_of(turn * chunk, chunk), chunk)
        density = density_ref[:, here]

        def some(step):
            cols = pl.ds(pl.multiple_of(step * tgt_step, 128), tgt_step)
            total_ref[:, cols] += pair_sums(dist, flux, target_ref[:, cols], density)

        if tgt_steps == 1:
            some(0)
        else:
            pl.loop(0, tgt_steps)(some)

    def both(turn, carry):
        apply(turn, *carry)
        return tuple(make(turn + 1))

    apply(steps - 1, *lax.fori_loop(0, steps - 1, both, tuple(make(0))))


def partner(own, k, groups):
    return own ^ (groups - k) if groups & (groups - 1) == 0 else (own + groups - k) % groups


def start_corners(connectivity_ref, corners_ref, sems, firsts, count):
    copies = []
    for k, first in enumerate(firsts):
        copy = pltpu.make_async_copy(
            connectivity_ref.at[:, pl.ds(pl.multiple_of(first, 128), count)],
            corners_ref.at[:, pl.ds(k * count, count)],
            sems.at[k],
        )
        copy.start()
        copies.append(copy)
    return copies


def start_density(density_refs, held_ref, sems):
    copies = []
    for k, ref in enumerate(density_refs):
        count = ref.shape[1]
        copy = pltpu.make_async_copy(ref, held_ref.at[:, pl.ds(k * count, count)], sems.at[k])
        copy.start()
        copies.append(copy)
    return copies


def first_kernel(near, row_total, group, sizes, sample_ref, *refs):
    small_refs, connectivity_ref, density_refs, refs = refs[:5], refs[5], refs[6 : 6 + near], refs[6 + near :]
    (table_ref, origin_ref, far_ref, own_ref, total_ref, dist_ref, flux_ref, rest_ref), refs = refs[:8], refs[8:]
    small, (src_corners, tgt_corners, held_ref, small_sems, src_sems, rest_sems, tgt_sems, density_sems) = (
        refs[:5], refs[5:],
    )
    lattice_ref, modes_ref, polar_ref, azim_ref, ring_ref = small
    pitch, width, first_cos, cycle_count = sizes
    src_dev = src_corners.shape[1] // near
    groups = row_total // group
    row = lax.axis_index("row")
    own_group = row // group
    place = row % group
    first_copies = []
    for k in range(5):
        first_copies.append(pltpu.make_async_copy(small_refs[k], small[k], small_sems.at[k]))
        first_copies[k].start()
    copies = start_corners(
        connectivity_ref, tgt_corners, tgt_sems,
        [(partner(own_group, k + 1, groups) * group + place) * src_dev for k in range(groups)], BAND_DEV,
    )
    copies += start_corners(
        connectivity_ref, src_corners, src_sems,
        [(own_group * group + (place ^ k)) * src_dev for k in range(near)], src_dev,
    )
    copies += start_density(density_refs, held_ref, density_sems)
    rest_copies = start_corners(
        connectivity_ref, rest_ref, rest_sems,
        [(own_group * group + (place ^ k)) * src_dev for k in range(near, group)], src_dev,
    )

    for copy in first_copies:
        copy.wait()
    radius = radius_table(
        sample_ref[0], lattice_ref[...], modes_ref[...], polar_ref[...], azim_ref[...], width
    )
    north = jnp.mean(radius[:, 0:1], axis=0, keepdims=True) * first_cos
    south = -jnp.mean(radius[:, cycle_count - 1 : cycle_count], axis=0, keepdims=True) * first_cos
    origin_ref[0:1] = jnp.broadcast_to(north, (1, 128))
    origin_ref[1:2] = jnp.broadcast_to(south, (1, 128))
    one, two, three = split(radius)
    lane = lax.broadcasted_iota(jnp.int32, radius.shape, 1)
    radius_pieces = jnp.where(lane < pitch, one, jnp.where(lane < 2 * pitch, two, three))
    table_ref[...] = jnp.concatenate([radius_pieces.astype(BF16), ring_ref[...]], axis=0)
    for copy in copies:
        copy.wait()

    far_total = far_ref.shape[1]
    for first in range(0, far_total, TGT_STEP):
        last = min(first + TGT_STEP, far_total)
        far_ref[:, first:last] = target_features(
            tgt_corners[:, first:last], table_ref[...], north, south, pitch, width
        )
    own_ref[...] = target_features(
        tgt_corners[:, far_total:], table_ref[...], north, south, pitch, width
    )
    total_ref[...] = jnp.zeros_like(total_ref)

    def features(corners):
        return source_features(corners, table_ref[...], north, south, pitch, width)

    far_steps(src_corners, held_ref, far_ref, total_ref, dist_ref, flux_ref, features)
    for copy in rest_copies:
        copy.wait()


def second_kernel(near, group, sizes, corners_ref, table_ref, origin_ref, far_ref, part_ref, *refs):
    rest = group - near
    density_refs, refs = refs[:rest], refs[rest:]
    (*sums_refs, dist_ref, flux_ref, held_ref, total_ref, density_sems) = refs
    pitch, width = sizes[:2]
    copies = start_density(density_refs, held_ref, density_sems)
    north = origin_ref[0:1, 0:1]
    south = origin_ref[1:2, 0:1]
    total_ref[...] = part_ref[...]
    for copy in copies:
        copy.wait()

    def features(corners):
        return source_features(corners, table_ref[...], north, south, pitch, width)

    far_steps(corners_ref, held_ref, far_ref, total_ref, dist_ref, flux_ref, features)
    for k, ref in enumerate(sums_refs):
        ref[...] = total_ref[:, k * BAND_DEV : (k + 1) * BAND_DEV]


def own_kernel(group, target_ref, *refs):
    halves, density_refs, (sums_ref, total_ref) = refs[:-2 - group], refs[-2 - group : -2], refs[-2:]
    src_dev = density_refs[0].shape[1]
    target = target_ref[...]
    diagonal = lax.broadcasted_iota(jnp.int32, (BAND_DEV, BAND_DEV), 0) == lax.broadcasted_iota(
        jnp.int32, (BAND_DEV, BAND_DEV), 1
    )
    apart = jnp.where(diagonal, 1e30, 0.0)
    near = halves[0].shape[1] // src_dev
    total = None
    for k in range(group):
        dist_ref, flux_ref = halves[0:2] if k < near else halves[2:4]
        here = slice(k % near * src_dev, (k % near + 1) * src_dev)
        part = pair_sums(
            dist_ref[:, here], flux_ref[:, here], target, density_refs[k][...],
            apart if k == 0 else None,
        )
        total = part if total is None else total + part
    sums_ref[...] = total


def per_device(sample_index, lattice_vector, mode_table, connectivity, density):
    columns, src_dev = density.shape
    row_total = lax.axis_size("row")
    group = 4
    near = 2
    groups = row_total // group
    cycle_count = src_dev * row_total // (2 * NPH) + 1
    pitch, width, polar_table, azim_table, ring, first_cos = trig_tables(cycle_count)
    sizes = (pitch, width, first_cos, cycle_count)
    far_total = (groups - 1) * BAND_DEV
    vmem = pl.BlockSpec(memory_space=pltpu.VMEM)
    hbm = pl.BlockSpec(memory_space=pltpu.HBM)
    anywhere = pl.BlockSpec(memory_space=pl.ANY)
    params = pltpu.CompilerParams(vmem_limit_bytes=VMEM)
    densities = [density] + [
        lax.ppermute(density, "row", [(r, r ^ k) for r in range(row_total)])
        for k in range(1, group)
    ]

    def shape(*dims, dtype=BF16):
        return jax.ShapeDtypeStruct(dims, dtype)

    def in_hbm(array):
        return pltpu.with_memory_space_constraint(array, pltpu.HBM)

    def cost(sources, targets):
        return pl.CostEstimate(
            flops=2 * sources * targets * 256 * 3, bytes_accessed=1 << 20, transcendentals=0
        )

    small = [
        lattice_vector.reshape(1, -1), mode_table, jnp.asarray(polar_table),
        jnp.asarray(azim_table), jnp.asarray(ring),
    ]
    table, origins, far, own, part, dist_near, flux_near, corners = pl.pallas_call(
        lambda *refs: first_kernel(near, row_total, group, sizes, *refs),
        out_shape=[
            shape(NPH + 16, width),
            shape(8, 128, dtype=F32),
            shape(FEATS, far_total),
            shape(FEATS, BAND_DEV),
            shape(columns, far_total, dtype=F32),
            shape(FEATS, near * src_dev),
            shape(FEATS, near * src_dev),
            shape(3, (group - near) * src_dev, dtype=jnp.int32),
        ],
        in_specs=[pl.BlockSpec(memory_space=pltpu.SMEM)] + [hbm] * 7 + [anywhere] * (near - 1),
        out_specs=[vmem] * 8,
        scratch_shapes=[pltpu.VMEM(array.shape, array.dtype) for array in small]
        + [
            pltpu.VMEM((3, near * src_dev), jnp.int32),
            pltpu.VMEM((3, groups * BAND_DEV), jnp.int32),
            pltpu.VMEM((columns, near * src_dev), BF16),
            pltpu.SemaphoreType.DMA((5,)),
            pltpu.SemaphoreType.DMA((near,)),
            pltpu.SemaphoreType.DMA((group - near,)),
            pltpu.SemaphoreType.DMA((groups,)),
            pltpu.SemaphoreType.DMA((near,)),
        ],
        compiler_params=params,
        cost_estimate=cost(near * src_dev, far_total),
        name="first_half",
    )(sample_index, *[in_hbm(array) for array in (*small, connectivity, density)], *densities[1:near])

    rest = group - near
    *sums, dist_rest, flux_rest = pl.pallas_call(
        lambda *refs: second_kernel(near, group, sizes, *refs),
        out_shape=[shape(columns, BAND_DEV, dtype=F32)] * (groups - 1)
        + [shape(FEATS, rest * src_dev)] * 2,
        in_specs=[vmem] * 5 + [anywhere] * rest,
        out_specs=[vmem] * (groups + 1),
        scratch_shapes=[
            pltpu.VMEM((columns, rest * src_dev), BF16),
            pltpu.VMEM((columns, far_total), F32),
            pltpu.SemaphoreType.DMA((rest,)),
        ],
        compiler_params=params,
        cost_estimate=cost(rest * src_dev, far_total),
        name="second_half",
    )(corners, table, origins, far, part, *densities[near:])

    parts = [
        lax.ppermute(
            block,
            "row",
            [
                (r, partner(r // group, k + 1, groups) * group + r % group)
                for r in range(row_total)
            ],
        )
        for k, block in enumerate(sums)
    ]
    own_sums = pl.pallas_call(
        lambda *refs: own_kernel(group, *refs),
        out_shape=shape(columns, BAND_DEV, dtype=F32),
        in_specs=[vmem] * (5 + group),
        out_specs=vmem,
        scratch_shapes=[pltpu.VMEM((columns, BAND_DEV), F32)],
        compiler_params=params,
        cost_estimate=cost(group * src_dev, BAND_DEV),
        name="own_targets",
    )(own, dist_near, flux_near, dist_rest, flux_rest, *densities)
    total = 0.5 * density[:, :BAND_DEV].astype(F32) + own_sums
    for other in parts:
        total = total + other
    return total.T


def solution(mesh):
    placed = (P("sample"), P(), P(), P(), P(None, "row"))
    return jax.shard_map(
        per_device,
        mesh=mesh,
        in_specs=placed,
        out_specs=P(("sample", "row"), None),
        check_vma=False,
    )
```

time: 44 us -> 34 us (0.77)
  Pallas kernels: 31.4 us -> 22 us
  waiting for transfers between devices: 0.02 us -> 2.87 us
  starting transfers between devices: 9.31 us -> 7.57 us
  local copies, waits for them, and re-layouts: 0.86 us -> 0.01 us
  other arithmetic: 1.49 us -> 0.65 us
    pallas_call x3, Pallas kernels: 31.4 us -> 22 us  [the longest x1 10.9 us: per_device(): pl.pallas_call(lambda *refs: first_kernel(near, row_total, group, sizes,...]
    ppermute x3, waiting for transfers between devices: 0.01 us -> 1.93 us  [per_device(): lax.ppermute(block, 'row', [(r, partner(r // group, k + 1, groups) * grou...]
    ppermute x3, starting transfers between devices: 6.23 us -> 4.45 us  [per_device(): lax.ppermute(block, 'row', [(r, partner(r // group, k + 1, groups) * grou...]
    ppermute x3, waiting for transfers between devices: 0.01 us -> 0.94 us  [per_device(): lax.ppermute(density, 'row', [(r, r ^ k) for r in range(row_total)])]
    unnamed x6 -> x2, local copies, waits for them, and re-layouts: 0.86 us -> 0.01 us
    transpose x1, other arithmetic: 1.49 us -> 0.65 us  [per_device(): return total.T]
  transfers between devices with their start and end apart: 6 -> 6, of which waited for: 0 -> 2; matrix products, arithmetic and copies ran while one was open for 0% -> 0% of each run, Pallas kernels for 40% -> 42%
where the time goes in v3:
time: 34 us; the launch traced here: 33.8 us
  Pallas kernels  22 us (65%)
  starting transfers between devices  7.57 us (22%)
  waiting for transfers between devices  2.87 us (8%)
  between operations  0.71 us (2%)
  other arithmetic  0.65 us (2%)
    pallas_call x1, Pallas kernels, per_device(): pl.pallas_call(lambda *refs: first_kernel(near, row_total, group, sizes,...  10.9 us
    pallas_call x1, Pallas kernels, per_device(): pl.pallas_call(lambda *refs: second_kernel(near, group, sizes, *refs), ou...  7.97 us
    ppermute x3, starting transfers between devices, per_device(): lax.ppermute(block, 'row', [(r, partner(r // group, k + 1, groups) * grou...  4.45 us
    pallas_call x1, Pallas kernels, per_device(): pl.pallas_call(lambda *refs: own_kernel(group, *refs), out_shape=shape(co...  3.2 us
    ppermute x3, starting transfers between devices, per_device(): lax.ppermute(density, 'row', [(r, r ^ k) for r in range(row_total)])  3.11 us
    ppermute x3, waiting for transfers between devices, per_device(): lax.ppermute(block, 'row', [(r, partner(r // group, k + 1, groups) * grou...  1.93 us
    ppermute x3, waiting for transfers between devices, per_device(): lax.ppermute(density, 'row', [(r, r ^ k) for r in range(row_total)])  0.94 us
  transfers between devices with their start and end apart: 6, of which 2 were waited for; matrix products, arithmetic and copies ran while one was open for 0% of the time, Pallas kernels for 42%

profile of v3, /device:TPU:0, one launch (start us, length us, event | category | flops | bytes accessed | tf_op | source)
XLA Modules:
  0.0 33.8 jit_solution(7384023267547560815)
XLA Ops:
  0.0 0.5 %collective-permute-start = (bf16[64,2048]{1,0:T(8,128)(2,1)}, bf16[64,2048]{1,0:T(8,128)(2,1)S(1)}, u32[]{:S(2)}, u32[]{:S(2)}) collective-permute-start(bf16[64,2048]{1,0:T(8,128)(2,1)} %refs_5_.2), channel_id=1, source_target_pairs={{0,1},{1,0},{2,3},{3,2},{4,5},{5,4},{6,7},{7,6},{8,9},{9,8},{10,11... | collective-permute-start | bytes 786440 | tf_op jit(solution)/shard_map/ppermute | solution.py:378
  0.5 2.5 %collective-permute-start.1 = (bf16[64,2048]{1,0:T(8,128)(2,1)}, bf16[64,2048]{1,0:T(8,128)(2,1)S(1)}, u32[]{:S(2)}, u32[]{:S(2)}) collective-permute-start(bf16[64,2048]{1,0:T(8,128)(2,1)} %refs_5_.2), channel_id=1, source_target_pairs={{0,2},{1,3},{2,0},{3,1},{4,6},{5,7},{6,4},{7,5},{8,10},{9,11},{10,... | collective-permute-start | bytes 786440 | tf_op jit(solution)/shard_map/ppermute | solution.py:378
  3.0 0.1 collective-permute-start.2
  3.8 0.0 collective-permute-done.refs_8_.refs_6_
  3.8 10.9 %first_half.1 = (bf16[272,256]{1,0:T(8,128)(2,1)S(1)}, f32[8,128]{1,0:T(8,128)S(1)}, bf16[48,768]{1,0:T(8,128)(2,1)S(1)}, bf16[48,256]{1,0:T(8,128)(2,1)S(1)}, f...) custom-call(s32[1]{0:T(128)S(6)} %copy.9.refs_0_, ...), custom_call_target="tpu_custom_call" | custom-call | flops 4831838208 | bytes 1048576 | tf_op jit(solution)/shard_map/first_half/pallas_call | solution.py:397
  14.6 0.0 collective-permute-done.1.refs_5_.refs_7_
  14.7 0.9 %collective-permute-done.2.refs_6_.refs_8_ = bf16[64,2048]{1,0:T(8,128)(2,1)S(1)} collective-permute-done((bf16[64,2048]{1,0:T(8,128)(2,1)}, bf16[64,2048]{1,0:T(8,128)(2,1)S(1)}, u32[]{:S(2)}, u32[]{:S(2)}) %collective-permute-start.2) | collective-permute-done | bytes 262176 | tf_op jit(solution)/shard_map/ppermute | solution.py:378
  15.6 0.0 copy-start
  15.6 8.0 %second_half.1 = (f32[64,256]{1,0:T(8,128)S(1)}, f32[64,256]{1,0:T(8,128)S(1)}, f32[64,256]{1,0:T(8,128)S(1)}, bf16[48,4096]{1,0:T(8,128)(2,1)S(1)}, bf16[48,4096]{1,0:T(8,128)(2,1)S(1)}) custom-call(s32[3,4096]{1,0:T(4,128)S(1)} %get-tuple-element.21.refs_0_, bf16[272,256]{1,0:T(8,128)(2,1)S(1)} %get-tuple-element.22.refs_1_, ...), custom_call_target="tpu_custom_call" | custom-call | flops 4831838208 | bytes 1048576 | tf_op jit(solution)/shard_map/second_half/pallas_call | solution.py:428
  23.6 3.7 %collective-permute-start.3 = (f32[64,256]{1,0:T(8,128)S(1)}, f32[64,256]{1,0:T(8,128)S(1)}, u32[]{:S(2)}, u32[]{:S(2)}) collective-permute-start(f32[64,256]{1,0:T(8,128)S(1)} %get-tuple-element.28), channel_id=1, source_target_pairs={{0,12},{1,13},{2,14},{3,15},{4,8},{5,9},{6,10},{7,11},{8,4},{9,5},... | collective-permute-start | bytes 196616 | tf_op jit(solution)/shard_map/ppermute | solution.py:445
  27.3 0.0 collective-permute-start.4
  27.3 0.8 %collective-permute-start.5 = (f32[64,256]{1,0:T(8,128)S(1)}, f32[64,256]{1,0:T(8,128)S(1)}, u32[]{:S(2)}, u32[]{:S(2)}) collective-permute-start(f32[64,256]{1,0:T(8,128)S(1)} %get-tuple-element.30), channel_id=1, source_target_pairs={{0,4},{1,5},{2,6},{3,7},{4,0},{5,1},{6,2},{7,3},{8,12},{9,13},{10,... | collective-permute-start | bytes 196616 | tf_op jit(solution)/shard_map/ppermute | solution.py:445
  28.0 0.0 copy-done
  28.0 3.2 %own_targets.1 = f32[64,256]{1,0:T(8,128)S(1)} custom-call(bf16[48,256]{1,0:T(8,128)(2,1)S(1)} %get-tuple-element.18.refs_0_, bf16[48,4096]{1,0:T(8,128)(2,1)S(1)} %get-tuple-element.19.refs_1_, bf16[48,4096]{1,0:T(8,128)(2,1)S(1)} %get-tuple-element.20.refs_2_, bf16[48,4096]{1,0:T(8,128)(2,1)S(1)} %get-tuple-element.26.refs_3_, ...), custom_call_target="tpu_custom_call" | custom-call | flops 3221225472 | bytes 1048576 | tf_op jit(solution)/shard_map/own_targets/pallas_call | solution.py:455
  31.2 0.0 collective-permute-done.3
  31.2 1.9 %collective-permute-done.4 = f32[64,256]{1,0:T(8,128)S(1)} collective-permute-done((f32[64,256]{1,0:T(8,128)S(1)}, f32[64,256]{1,0:T(8,128)S(1)}, u32[]{:S(2)}, u32[]{:S(2)}) %collective-permute-start.4) | collective-permute-done | bytes 65568 | tf_op jit(solution)/shard_map/ppermute | solution.py:445
  33.2 0.0 collective-permute-done.5
  33.2 0.7 %add_bitcast_fusion = f32[256,64]{0,1:T(8,128)} fusion(f32[64,256]{1,0:T(8,128)S(1)} %collective-permute-done.5, f32[64,256]{1,0:T(8,128)S(1)} %collective-permute-done.4, f32[64,256]{1,0:T(8,128)S(1)} %collective-permute-done.3, f32[64,256]{1,0:T(8,128)S(1)} %own_targets.1, bf16[64,2048]{1,0:T(8,128)(2,1)S(1)} %copy-done), kind=kLoop, calls=%fused_computation | loop fusion | flops 98304 | bytes 360448 | tf_op jit(solution)/shard_map/transpose | solution.py:468
Async XLA Ops:
  0.0 3.8 %collective-permute-start = (bf16[64,2048]{1,0:T(8,128)(2,1)}, bf16[64,2048]{1,0:T(8,128)(2,1)S(1)}, u32[]{:S(2)}, u32[]{:S(2)}) collective-permute-start(bf16[64,2048]{1,0:T(8,128)(2,1)} %refs_5_.2), channel_id=1, source_target_pairs={{0,1},{1,0},{2,3},{3,2},{4,5},{5,4},{6,7},{7,6},{8,9},{9,8},{10,11... | collective-permute-start | bytes 786440 | tf_op jit(solution)/shard_map/ppermute | solution.py:378
  0.5 14.2 %collective-permute-start.1 = (bf16[64,2048]{1,0:T(8,128)(2,1)}, bf16[64,2048]{1,0:T(8,128)(2,1)S(1)}, u32[]{:S(2)}, u32[]{:S(2)}) collective-permute-start(bf16[64,2048]{1,0:T(8,128)(2,1)} %refs_5_.2), channel_id=1, source_target_pairs={{0,2},{1,3},{2,0},{3,1},{4,6},{5,7},{6,4},{7,5},{8,10},{9,11},{10,... | collective-permute-start | bytes 786440 | tf_op jit(solution)/shard_map/ppermute | solution.py:378
  3.0 12.6 %collective-permute-start.2 = (bf16[64,2048]{1,0:T(8,128)(2,1)}, bf16[64,2048]{1,0:T(8,128)(2,1)S(1)}, u32[]{:S(2)}, u32[]{:S(2)}) collective-permute-start(bf16[64,2048]{1,0:T(8,128)(2,1)} %refs_5_.2), channel_id=1, source_target_pairs={{0,3},{1,2},{2,1},{3,0},{4,7},{5,6},{6,5},{7,4},{8,11},{9,10},{10,... | collective-permute-start | bytes 786440 | tf_op jit(solution)/shard_map/ppermute | solution.py:378
  15.6 12.4 %copy-start = (bf16[64,2048]{1,0:T(8,128)(2,1)S(1)}, bf16[64,2048]{1,0:T(8,128)(2,1)}, u32[]{:S(2)}) copy-start(bf16[64,2048]{1,0:T(8,128)(2,1)} %refs_5_.2) | copy-start | bytes 786436
  23.6 7.7 %collective-permute-start.3 = (f32[64,256]{1,0:T(8,128)S(1)}, f32[64,256]{1,0:T(8,128)S(1)}, u32[]{:S(2)}, u32[]{:S(2)}) collective-permute-start(f32[64,256]{1,0:T(8,128)S(1)} %get-tuple-element.28), channel_id=1, source_target_pairs={{0,12},{1,13},{2,14},{3,15},{4,8},{5,9},{6,10},{7,11},{8,4},{9,5},... | collective-permute-start | bytes 196616 | tf_op jit(solution)/shard_map/ppermute | solution.py:445
  27.3 5.9 %collective-permute-start.4 = (f32[64,256]{1,0:T(8,128)S(1)}, f32[64,256]{1,0:T(8,128)S(1)}, u32[]{:S(2)}, u32[]{:S(2)}) collective-permute-start(f32[64,256]{1,0:T(8,128)S(1)} %get-tuple-element.29), channel_id=1, source_target_pairs={{0,8},{1,9},{2,10},{3,11},{4,12},{5,13},{6,14},{7,15},{8,0},{9,1},... | collective-permute-start | bytes 196616 | tf_op jit(solution)/shard_map/ppermute | solution.py:445
  27.3 5.9 %collective-permute-start.5 = (f32[64,256]{1,0:T(8,128)S(1)}, f32[64,256]{1,0:T(8,128)S(1)}, u32[]{:S(2)}, u32[]{:S(2)}) collective-permute-start(f32[64,256]{1,0:T(8,128)S(1)} %get-tuple-element.30), channel_id=1, source_target_pairs={{0,4},{1,5},{2,6},{3,7},{4,0},{5,1},{6,2},{7,3},{8,12},{9,13},{10,... | collective-permute-start | bytes 196616 | tf_op jit(solution)/shard_map/ppermute | solution.py:445

commit v4 on v3

v4 whole, which is shorter than its diff:
```python
import math

import jax
import jax.numpy as jnp
import numpy as np
from jax import lax
from jax.experimental import pallas as pl
from jax.experimental.pallas import tpu as pltpu
from jax.sharding import PartitionSpec as P

NLAT = 32768
NPH = 256
BAND_DEV = 256
FREQS = 32
HALF = 24
FEATS = 2 * HALF
BLOCK = 1024
CHUNK = 1024
TGT_STEP = 768
VMEM = 30 << 20
F32 = jnp.float32
BF16 = jnp.bfloat16


def split(values):
    first = values.astype(BF16).astype(F32)
    rest = values - first
    second = rest.astype(BF16).astype(F32)
    third = (rest - second).astype(BF16).astype(F32)
    return [first, second, third]


def trig_tables(cycle_count):
    pitch = -(-cycle_count // 8) * 8
    cycle = np.arange(pitch)[:, None]
    polar = np.pi * (cycle + 1.0) / (cycle_count + 1) * (cycle < cycle_count)
    freq = np.arange(FREQS)[None, :]
    polar_table = np.concatenate([np.cos(freq * polar), -np.sin(freq * polar)], axis=0)
    azimuth = 2.0 * np.pi * np.arange(NPH)[None, :] / NPH
    azim_freq = np.arange(FREQS)[:, None] - FREQS // 2
    azim_table = np.concatenate([np.cos(azimuth * azim_freq), np.sin(azimuth * azim_freq)], axis=0)
    rows = -(-cycle_count // 128)
    ring = np.zeros((2, rows * 128))
    ring[0, :cycle_count] = np.sin(polar[:cycle_count, 0])
    ring[1, :cycle_count] = np.cos(polar[:cycle_count, 0])
    angles = np.concatenate(
        [ring.reshape(-1, 128), np.cos(azimuth).reshape(-1, 128), np.sin(azimuth).reshape(-1, 128)]
    )
    angles = np.concatenate([angles, np.zeros((-len(angles) % 8, 128))])
    first_cos = float(np.cos(np.pi / (cycle_count + 1)))
    tables = [polar_table, azim_table, angles]
    return pitch, first_cos, [table.astype(np.float32) for table in tables]


def radius_table(sample, lattice, modes, polar_table, azim_table, pitch):
    shifts = ((sample * lattice) & (NLAT - 1)).astype(F32) / NLAT - 0.5
    polar_freq = modes[0:1, :]
    azim_freq = modes[1:2, :]
    scale = (1 + polar_freq + jnp.abs(azim_freq)).astype(F32)
    coef = 0.8 * shifts / (scale * scale)
    numbers = lax.broadcasted_iota(jnp.int32, (FREQS, modes.shape[1]), 0)
    at_azim = numbers == azim_freq + FREQS // 2
    at_polar = jnp.where(numbers == polar_freq, 1.0, 0.0).astype(BF16)
    grid = None
    for part in split(coef):
        placed = lax.dot_general(
            at_polar,
            jnp.where(at_azim, part, 0.0).astype(BF16),
            (((1,), (1,)), ((), ())),
            preferred_element_type=F32,
        )
        grid = placed if grid is None else grid + placed
    exact = dict(precision=lax.Precision.HIGHEST, preferred_element_type=F32)
    both = jnp.dot(polar_table, grid, **exact)
    return jnp.exp(
        jnp.dot(both[:pitch], azim_table[:FREQS], **exact)
        + jnp.dot(both[pitch:], azim_table[FREQS:], **exact)
    )


def at_lanes(ref, row, first, lanes):
    values = jnp.broadcast_to(ref[row : row + 1, first : first + 128], lanes.shape)
    return jnp.take_along_axis(values, lanes, axis=1)


def radii(table_ref, column, cycles, cycle_count):
    lanes = column & 127
    right = column >= 128
    levels = (cycle_count - 1).bit_length()
    bits = [[(cycle & (1 << level)) != 0 for level in range(levels)] for cycle in cycles]

    def among(low, level):
        if level == 0:
            left = at_lanes(table_ref, low, 0, lanes)
            return [jnp.where(right, at_lanes(table_ref, low, 128, lanes), left)] * len(cycles)
        half = 1 << (level - 1)
        below = among(low, level - 1)
        if low + half >= cycle_count:
            return below
        above = among(low + half, level - 1)
        return [jnp.where(bit[level - 1], y, x) for bit, x, y in zip(bits, below, above)]

    return among(0, levels)


def angle_of(angles_ref, first, rows, index):
    lanes = index & 127
    found = at_lanes(angles_ref, first, 0, lanes)
    for row in range(1, rows):
        found = jnp.where(index >= 128 * row, at_lanes(angles_ref, first + row, 0, lanes), found)
    return found


def panels(corners, table_ref, angles_ref, cycle_count):
    zero, one, two = [
        jnp.concatenate([corners[c : c + 1, k * 128 : (k + 1) * 128] for k in range(8)], axis=0)
        for c in range(3)
    ]
    last = ((zero ^ one) & (NPH - 1)) == 0
    middle = ((zero ^ two) & (NPH - 1)) == 0
    turned = (
        jnp.where(last, two, jnp.where(middle, one, zero)),
        jnp.where(last, zero, jnp.where(middle, two, one)),
        jnp.where(last, one, jnp.where(middle, zero, two)),
    )
    cycles = [corner >> 8 for corner in turned]
    columns = [turned[0] & (NPH - 1), turned[1] & (NPH - 1)]
    radius = radii(table_ref, columns[0], cycles[:1], cycle_count) + radii(
        table_ref, columns[1], cycles[1:], cycle_count
    )
    rows = -(-cycle_count // 128)
    cos = [angle_of(angles_ref, 2 * rows, 2, column) for column in columns]
    sin = [angle_of(angles_ref, 2 * rows + 2, 2, column) for column in columns]
    points = []
    for c in range(3):
        flat = radius[c] * angle_of(angles_ref, 0, rows, cycles[c])
        side = min(c, 1)
        points.append(
            (flat * cos[side], flat * sin[side], radius[c] * angle_of(angles_ref, rows, rows, cycles[c]))
        )
    centers = [(points[0][d] + points[1][d] + points[2][d]) / 3.0 for d in range(3)]
    one = [points[1][d] - points[0][d] for d in range(3)]
    two = [points[2][d] - points[0][d] for d in range(3)]
    half = 0.5 / (4.0 * math.pi)
    areas = [
        half * (one[(d + 1) % 3] * two[(d + 2) % 3] - one[(d + 2) % 3] * two[(d + 1) % 3])
        for d in range(3)
    ]
    return centers, areas


def as_rows(values, stage_ref):
    for k, value in enumerate(values):
        stage_ref[k * 8 : (k + 1) * 8, :] = value
    blocks = [stage_ref[pl.ds(k, len(values), stride=8), :].astype(BF16) for k in range(8)]
    return jnp.concatenate(blocks, axis=1)


def pieces_of(vector):
    parts = [split(coordinate) for coordinate in vector]
    return [[part[k] for part in parts] for k in range(3)]


def target_features(corners, geometry, stage_ref):
    centers, _ = panels(corners, *geometry[:3])
    ones = jnp.ones((8, 128), F32)
    rows = []
    for origin in geometry[3:]:
        offset = centers[:2] + [centers[2] - origin]
        square = offset[0] * offset[0] + offset[1] * offset[1] + offset[2] * offset[2]
        one, two, three = pieces_of(offset)
        rows += one + one + one + two + two + three + split(square) + [ones] * 3
    return as_rows(rows, stage_ref)


def source_features(corners, geometry, stage_refs):
    centers, areas = panels(corners, *geometry[:3])
    north, south = geometry[3:]
    upper = centers[2] >= 0.0
    offset = centers[:2] + [centers[2] - jnp.where(upper, north, south)]
    square = offset[0] * offset[0] + offset[1] * offset[1] + offset[2] * offset[2]
    level = offset[0] * areas[0] + offset[1] * areas[1] + offset[2] * areas[2]
    zeros = jnp.zeros((8, 128), F32)
    found = []
    for vector, flat, last, stage_ref in (
        ([-2.0 * x for x in offset], zeros + 1.0, square, stage_refs[0]),
        (areas, zeros, -level, stage_refs[1]),
    ):
        one, two, three = pieces_of(vector)
        rows = one + two + three + one + two + one + [flat] * 3 + split(last)
        rows = [jnp.where(upper, x, 0.0) for x in rows] + [jnp.where(upper, 0.0, x) for x in rows]
        found.append(as_rows(rows, stage_ref))
    return found


def pair_sums(dist, flux, target, density, apart=None):
    contract = (((0,), (0,)), ((), ()))
    dist_sq = lax.dot_general(dist, target, contract, preferred_element_type=F32)
    flow = lax.dot_general(flux, target, contract, preferred_element_type=F32)
    if apart is not None:
        dist_sq = jnp.concatenate([dist_sq[:BAND_DEV] + apart, dist_sq[BAND_DEV:]], axis=0)
    inverse = lax.rsqrt(dist_sq)
    tile = (flow * inverse * (inverse * inverse)).astype(BF16)
    return jnp.dot(density, tile, preferred_element_type=F32)


def far_steps(
    corners_ref, density_ref, target_ref, total_ref, dist_ref, flux_ref, geometry, stage_ref
):
    src_total = corners_ref.shape[1]
    tgt_total = target_ref.shape[1]
    chunk = min(CHUNK, src_total)
    steps = src_total // chunk
    tgt_step = max(
        step for step in range(BAND_DEV, TGT_STEP + 1, BAND_DEV) if tgt_total % step == 0
    )
    tgt_steps = tgt_total // tgt_step

    def make(turn):
        here = pl.ds(turn * chunk, chunk)
        corners = corners_ref[:, here]
        blocks = [
            source_features(
                corners[:, k * BLOCK : (k + 1) * BLOCK],
                geometry,
                (stage_ref.at[2 * k], stage_ref.at[2 * k + 1]),
            )
            for k in range(chunk // BLOCK)
        ]
        dist, flux = [jnp.concatenate([block[k] for block in blocks], axis=1) for k in range(2)]
        dist_ref[:, here] = dist
        flux_ref[:, here] = flux
        return dist, flux

    def apply(turn, dist, flux):
        here = pl.ds(turn * chunk, chunk)
        density = density_ref[:, here]

        def some(step):
            cols = pl.ds(pl.multiple_of(step * tgt_step, 128), tgt_step)
            total_ref[:, cols] += pair_sums(dist, flux, target_ref[:, cols], density)

        if tgt_steps == 1:
            some(0)
        else:
            pl.loop(0, tgt_steps)(some)

    kept = make(0)
    for turn in range(steps):
        following = make(turn + 1) if turn + 1 < steps else None
        apply(turn, *kept)
        kept = following


def partner(own, k, groups):
    return own ^ (groups - k) if groups & (groups - 1) == 0 else (own + groups - k) % groups


def start_corners(connectivity_ref, corners_ref, sems, firsts, count):
    copies = []
    for k, first in enumerate(firsts):
        copy = pltpu.make_async_copy(
            connectivity_ref.at[:, pl.ds(pl.multiple_of(first, 128), count)],
            corners_ref.at[:, pl.ds(k * count, count)],
            sems.at[k],
        )
        copy.start()
        copies.append(copy)
    return copies


def start_density(density_refs, held_ref, sems):
    copies = []
    for k, ref in enumerate(density_refs):
        count = ref.shape[1]
        copy = pltpu.make_async_copy(ref, held_ref.at[:, pl.ds(k * count, count)], sems.at[k])
        copy.start()
        copies.append(copy)
    return copies


def first_kernel(near, row_total, group, sizes, sample_ref, *refs):
    small_refs, connectivity_ref, density_refs, refs = refs[:5], refs[5], refs[6 : 6 + near], refs[6 + near :]
    (table_ref, origin_ref, *tgt_refs, dist_ref, flux_ref, rest_ref), refs = refs[:10], refs[10:]
    feature_refs, part_refs = tgt_refs[:3], tgt_refs[3:]
    small, (src_corners, tgt_corners, held_ref, stage_ref, far_ref, total_ref, small_sems, src_sems, rest_sems, tgt_sems, density_sems) = (
        refs[:5], refs[5:],
    )
    lattice_ref, modes_ref, polar_ref, azim_ref, angles_ref = small
    pitch, first_cos, cycle_count = sizes
    src_dev = src_corners.shape[1] // near
    groups = row_total // group
    row = lax.axis_index("row")
    own_group = row // group
    place = row % group
    first_copies = []
    for k in range(5):
        first_copies.append(pltpu.make_async_copy(small_refs[k], small[k], small_sems.at[k]))
        first_copies[k].start()
    copies = start_corners(
        connectivity_ref, tgt_corners, tgt_sems,
        [(partner(own_group, k + 1, groups) * group + place) * src_dev for k in range(groups)], BAND_DEV,
    )
    copies += start_corners(
        connectivity_ref, src_corners, src_sems,
        [(own_group * group + (place ^ k)) * src_dev for k in range(near)], src_dev,
    )
    copies += start_density(density_refs, held_ref, density_sems)
    rest_copies = start_corners(
        connectivity_ref, rest_ref, rest_sems,
        [(own_group * group + (place ^ k)) * src_dev for k in range(near, group)], src_dev,
    )

    for copy in first_copies:
        copy.wait()
    radius = radius_table(
        sample_ref[0], lattice_ref[...], modes_ref[...], polar_ref[...], azim_ref[...], pitch
    )
    north = jnp.mean(radius[0:1], axis=1, keepdims=True) * first_cos
    south = -jnp.mean(radius[cycle_count - 1 : cycle_count], axis=1, keepdims=True) * first_cos
    origin_ref[0:1] = jnp.broadcast_to(north, (1, 128))
    origin_ref[1:2] = jnp.broadcast_to(south, (1, 128))
    table_ref[...] = radius
    for copy in copies:
        copy.wait()

    geometry = (table_ref, angles_ref, cycle_count, north, south)
    found = [
        target_features(tgt_corners[:, first : first + BLOCK], geometry, stage_ref.at[0])
        for first in range(0, tgt_corners.shape[1], BLOCK)
    ]
    found = jnp.concatenate(found, axis=1)
    far_ref[...] = found[:, :-BAND_DEV]
    first = 0
    for ref in feature_refs:
        ref[...] = found[:, first : first + ref.shape[1]]
        first += ref.shape[1]
    total_ref[...] = jnp.zeros_like(total_ref)
    far_steps(
        src_corners, held_ref, far_ref, total_ref, dist_ref, flux_ref, geometry, stage_ref
    )
    first = 0
    for ref in part_refs:
        ref[...] = total_ref[:, first : first + ref.shape[1]]
        first += ref.shape[1]
    for copy in rest_copies:
        copy.wait()


def second_kernel(
    near, group, cycle_count, corners_ref, table_ref, angles_ref, origin_ref, far_ref, part_ref, *refs
):
    rest = group - near
    density_refs, refs = refs[:rest], refs[rest:]
    (*sums_refs, dist_ref, flux_ref, held_ref, total_ref, stage_ref, density_sems) = refs
    copies = start_density(density_refs, held_ref, density_sems)
    geometry = (table_ref, angles_ref, cycle_count, origin_ref[0:1, 0:1], origin_ref[1:2, 0:1])
    total_ref[...] = part_ref[...]
    for copy in copies:
        copy.wait()
    far_steps(corners_ref, held_ref, far_ref, total_ref, dist_ref, flux_ref, geometry, stage_ref)
    for k, ref in enumerate(sums_refs):
        ref[...] = total_ref[:, k * BAND_DEV : (k + 1) * BAND_DEV]


def kept_kernel(own, count, dist_ref, flux_ref, target_ref, *refs):
    density_refs, (*part_refs, sums_ref) = refs[:count], refs[count:]
    src_dev = density_refs[0].shape[1]
    target = target_ref[...]
    apart = None
    if own:
        diagonal = lax.broadcasted_iota(
            jnp.int32, (BAND_DEV, BAND_DEV), 0
        ) == lax.broadcasted_iota(jnp.int32, (BAND_DEV, BAND_DEV), 1)
        apart = jnp.where(diagonal, 1e30, 0.0)
    total = part_refs[0][...] if part_refs else None
    for k in range(count):
        here = slice(k * src_dev, (k + 1) * src_dev)
        sums = pair_sums(
            dist_ref[:, here], flux_ref[:, here], target, density_refs[k][...], None if k else apart
        )
        total = sums if total is None else total + sums
    sums_ref[...] = total


def per_device(sample_index, lattice_vector, mode_table, connectivity, density):
    columns, src_dev = density.shape
    row_total = lax.axis_size("row")
    group = 4
    near = 2
    groups = row_total // group
    cycle_count = src_dev * row_total // (2 * NPH) + 1
    pitch, first_cos, tables = trig_tables(cycle_count)
    sizes = (pitch, first_cos, cycle_count)
    far_total = (groups - 1) * BAND_DEV
    vmem = pl.BlockSpec(memory_space=pltpu.VMEM)
    hbm = pl.BlockSpec(memory_space=pltpu.HBM)
    anywhere = pl.BlockSpec(memory_space=pl.ANY)
    params = pltpu.CompilerParams(vmem_limit_bytes=VMEM)
    def moved(array, target_of):
        return lax.ppermute(array, "row", [(r, target_of(r)) for r in range(row_total)])

    densities = [density, moved(density, lambda r: r ^ 1), moved(density, lambda r: r ^ 2)]

    def shape(*dims, dtype=BF16):
        return jax.ShapeDtypeStruct(dims, dtype)

    def in_hbm(array):
        return pltpu.with_memory_space_constraint(array, pltpu.HBM)

    def cost(sources, targets):
        return pl.CostEstimate(
            flops=2 * sources * targets * 256 * 3, bytes_accessed=1 << 20, transcendentals=0
        )

    small = [lattice_vector.reshape(1, -1), mode_table, *map(jnp.asarray, tables)]
    stage = pltpu.VMEM((2 * min(CHUNK, src_dev) // BLOCK, 8 * FEATS, 128), F32)
    early = far_total - BAND_DEV
    table, origins, tgt_early, tgt_late, tgt_own, part_early, part_late, *near_features, corners = (
        pl.pallas_call(
            lambda *refs: first_kernel(near, row_total, group, sizes, *refs),
            out_shape=[
                shape(pitch, NPH, dtype=F32),
                shape(8, 128, dtype=F32),
                shape(FEATS, early),
                shape(FEATS, BAND_DEV),
                shape(FEATS, BAND_DEV),
                shape(columns, early, dtype=F32),
                shape(columns, BAND_DEV, dtype=F32),
                shape(FEATS, near * src_dev),
                shape(FEATS, near * src_dev),
                shape(3, (group - near) * src_dev, dtype=jnp.int32),
            ],
            in_specs=[pl.BlockSpec(memory_space=pltpu.SMEM)] + [hbm] * 7 + [anywhere] * (near - 1),
            out_specs=[vmem] * 10,
            scratch_shapes=[pltpu.VMEM(array.shape, array.dtype) for array in small]
            + [
                pltpu.VMEM((3, near * src_dev), jnp.int32),
                pltpu.VMEM((3, groups * BAND_DEV), jnp.int32),
                pltpu.VMEM((columns, near * src_dev), BF16),
                stage,
                pltpu.VMEM((FEATS, far_total), BF16),
                pltpu.VMEM((columns, far_total), F32),
                pltpu.SemaphoreType.DMA((5,)),
                pltpu.SemaphoreType.DMA((near,)),
                pltpu.SemaphoreType.DMA((group - near,)),
                pltpu.SemaphoreType.DMA((groups,)),
                pltpu.SemaphoreType.DMA((near,)),
            ],
            compiler_params=params,
            cost_estimate=cost(near * src_dev, far_total),
            name="near_sources",
        )(
            sample_index,
            *[in_hbm(array) for array in (*small, connectivity, density)],
            *densities[1:near],
        )
    )

    relay, origins = lax.optimization_barrier((densities[2], origins))
    densities.append(moved(relay, lambda r: r ^ 1))
    rest = group - near
    *sums, dist_rest, flux_rest = pl.pallas_call(
        lambda *refs: second_kernel(near, group, cycle_count, *refs),
        out_shape=[shape(columns, BAND_DEV, dtype=F32)] * (groups - 2)
        + [shape(FEATS, rest * src_dev)] * 2,
        in_specs=[vmem] * 6 + [anywhere] * rest,
        out_specs=[vmem] * groups,
        scratch_shapes=[
            pltpu.VMEM((columns, rest * src_dev), BF16),
            pltpu.VMEM((columns, early), F32),
            stage,
            pltpu.SemaphoreType.DMA((rest,)),
        ],
        compiler_params=params,
        cost_estimate=cost(rest * src_dev, early),
        name="other_sources",
    )(corners, table, small[4], origins, tgt_early, part_early, *densities[near:])

    def kept(features, target, blocks, own, part):
        return pl.pallas_call(
            lambda *refs: kept_kernel(own, len(blocks), *refs),
            out_shape=shape(columns, BAND_DEV, dtype=F32),
            in_specs=[vmem] * (3 + len(blocks) + len(part)),
            out_specs=vmem,
            compiler_params=params,
            cost_estimate=cost(len(blocks) * src_dev, BAND_DEV),
            name="own_targets" if own else "late_targets",
        )(*features, target, *blocks, *part)

    rest_features = (dist_rest, flux_rest)
    own_sums = kept(near_features, tgt_own, densities[:near], True, [])
    sums.append(kept(rest_features, tgt_late, densities[near:], False, [part_late]))
    own_sums = kept(rest_features, tgt_own, densities[near:], False, [own_sums])
    total = 0.5 * density[:, :BAND_DEV].astype(F32) + own_sums
    for k, block in enumerate(sums):
        total = total + moved(
            block, lambda r, k=k: partner(r // group, k + 1, groups) * group + r % group
        )
    return total.T


def solution(mesh):
    placed = (P("sample"), P(), P(), P(), P(None, "row"))
    return jax.shard_map(
        per_device,
        mesh=mesh,
        in_specs=placed,
        out_specs=P(("sample", "row"), None),
        check_vma=False,
    )
```

time: 34 us -> 31.3 us (0.921)
  Pallas kernels: 22 us -> 18.9 us
  local copies, waits for them, and re-layouts: 0.01 us -> 0.68 us
  waiting for transfers between devices: 2.87 us -> 2.36 us
    pallas_call x1, Pallas kernels: 10.9 us -> 8.25 us  [per_device(): pl.pallas_call(lambda *refs: first_kernel(near, row_total, group, sizes,...]
    unnamed x2 -> x4, local copies, waits for them, and re-layouts: 0.01 us -> 0.68 us
    pallas_call x2 -> x4, Pallas kernels: 11.2 us -> 10.6 us  [the longest x3 5.98 us: kept(): pl.pallas_call(lambda *refs: kept_kernel(own, len(blocks), *refs), out_sh...]
    ppermute x6, waiting for transfers between devices: 2.87 us -> 2.36 us  [moved(): lax.ppermute(array, 'row', [(r, target_of(r)) for r in range(row_total)])]
  transfers between devices with their start and end apart: 6 -> 6, of which waited for: 2 -> 2; matrix products, arithmetic and copies ran while one was open for 0% -> 0% of each run, Pallas kernels for 42% -> 46%
where the time goes in v4:
time: 31.3 us; the launch traced here: 31.1 us
  Pallas kernels  18.9 us (60%)
  starting transfers between devices  7.78 us (25%)
  waiting for transfers between devices  2.36 us (8%)
  between operations  0.74 us (2%)
  local copies, waits for them, and re-layouts  0.68 us (2%)
  other arithmetic  0.66 us (2%)
    pallas_call x1, Pallas kernels, per_device(): pl.pallas_call(lambda *refs: first_kernel(near, row_total, group, sizes,...  8.25 us
    ppermute x6, starting transfers between devices, moved(): lax.ppermute(array, 'row', [(r, target_of(r)) for r in range(row_total)])  7.78 us
    pallas_call x3, Pallas kernels, kept(): pl.pallas_call(lambda *refs: kept_kernel(own, len(blocks), *refs), out_sh...  5.98 us
    pallas_call x1, Pallas kernels, per_device(): pl.pallas_call(lambda *refs: second_kernel(near, group, cycle_count, *ref...  4.64 us
    ppermute x6, waiting for transfers between devices, moved(): lax.ppermute(array, 'row', [(r, target_of(r)) for r in range(row_total)])  2.36 us
    unnamed x4, local copies, waits for them, and re-layouts  0.68 us
    transpose x1, other arithmetic, per_device(): return total.T  0.66 us
  transfers between devices with their start and end apart: 6, of which 2 were waited for; matrix products, arithmetic and copies ran while one was open for 0% of the time, Pallas kernels for 46%

profile of v4, /device:TPU:0, one launch (start us, length us, event | category | flops | bytes accessed | tf_op | source)
XLA Modules:
  0.0 31.1 jit_solution(11099234331799902309)
XLA Ops:
  0.0 0.5 %collective-permute-start = (bf16[64,2048]{1,0:T(8,128)(2,1)}, bf16[64,2048]{1,0:T(8,128)(2,1)S(1)}, u32[]{:S(2)}, u32[]{:S(2)}) collective-permute-start(bf16[64,2048]{1,0:T(8,128)(2,1)} %refs_3_.2), channel_id=1, source_target_pairs={{0,1},{1,0},{2,3},{3,2},{4,5},{5,4},{6,7},{7,6},{8,9},{9,8},{10,11... | collective-permute-start | bytes 786440 | tf_op jit(solution)/shard_map/ppermute | solution.py:401
  0.5 2.5 %collective-permute-start.1 = (bf16[64,2048]{1,0:T(8,128)(2,1)}, bf16[64,2048]{1,0:T(8,128)(2,1)S(1)}, u32[]{:S(2)}, u32[]{:S(2)}) collective-permute-start(bf16[64,2048]{1,0:T(8,128)(2,1)} %refs_3_.2), channel_id=1, source_target_pairs={{0,2},{1,3},{2,0},{3,1},{4,6},{5,7},{6,4},{7,5},{8,10},{9,11},{10,... | collective-permute-start | bytes 786440 | tf_op jit(solution)/shard_map/ppermute | solution.py:401
  3.6 0.0 collective-permute-done.refs_8_.refs_4_
  3.6 0.0 copy-start
  3.6 8.3 %near_sources.1 = (f32[72,256]{1,0:T(8,128)S(1)}, f32[8,128]{1,0:T(8,128)S(1)}, bf16[48,512]{1,0:T(8,128)(2,1)S(1)}, bf16[48,256]{1,0:T(8,128)(2,1)S(1)}, bf16[4...) custom-call(s32[1]{0:T(128)S(6)} %copy.9.refs_0_, ...), custom_call_target="tpu_custom_call" | custom-call | flops 4831838208 | bytes 1048576 | tf_op jit(solution)/shard_map/near_sources/pallas_call | solution.py:420
  11.9 0.0 collective-permute-done.1.refs_6_.refs_3_
  11.9 0.3 collective-permute-start.2
  12.2 0.0 copy-done
  12.2 2.0 %own_targets.1.refs_5_ = f32[64,256]{1,0:T(8,128)S(1)} custom-call(bf16[48,4096]{1,0:T(8,128)(2,1)S(1)} %get-tuple-element.31.refs_0_, bf16[48,4096]{1,0:T(8,128)(2,1)S(1)} %get-tuple-element.32.refs_1_, bf16[48,256]{1,0:T(8,128)(2,1)S(1)} %get-tuple-element.30.refs_2_, bf16[64,2048]{1,0:T(8,128)(2,1)S(1)} %copy-done, ...), custom_call_target="tpu_custom_call" | custom-call | flops 1610612736 | bytes 1048576 | tf_op jit(solution)/shard_map/own_targets/pallas_call | solution.py:481
  14.2 0.0 copy-start.1
  14.2 0.0 collective-permute-done.2.refs_7_.refs_4_
  14.2 0.7 %copy-done.1 = f32[8,128]{1,0:T(8,128)S(1)} copy-done((f32[8,128]{1,0:T(8,128)S(1)}, f32[8,128]{1,0:T(8,128)}, u32[]{:S(2)}) %copy-start.1) | copy-done | bytes 4120
  14.9 4.6 %other_sources.1 = (f32[64,256]{1,0:T(8,128)S(1)}, f32[64,256]{1,0:T(8,128)S(1)}, bf16[48,4096]{1,0:T(8,128)(2,1)S(1)}, bf16[48,4096]{1,0:T(8,128)(2,1)S(1)}) custom-call(s32[3,4096]{1,0:T(4,128)S(1)} %get-tuple-element.21.refs_0_, f32[72,256]{1,0:T(8,128)S(1)} %get-tuple-element.22.refs_1_, f32[8,128]{1,0:T(8,128)S(1)} %copy-done.1, ...), custom_call_target="tpu_custom_call" | custom-call | flops 3221225472 | bytes 1048576 | tf_op jit(solution)/shard_map/other_sources/pallas_call | solution.py:463
  19.6 3.7 %collective-permute-start.3 = (f32[64,256]{1,0:T(8,128)S(1)}, f32[64,256]{1,0:T(8,128)S(1)}, u32[]{:S(2)}, u32[]{:S(2)}) collective-permute-start(f32[64,256]{1,0:T(8,128)S(1)} %get-tuple-element.33), channel_id=1, source_target_pairs={{0,12},{1,13},{2,14},{3,15},{4,8},{5,9},{6,10},{7,11},{8,4},{9,5},... | collective-permute-start | bytes 196616 | tf_op jit(solution)/shard_map/ppermute | solution.py:401
  23.2 0.0 collective-permute-start.4
  23.2 2.0 %late_targets.3 = f32[64,256]{1,0:T(8,128)S(1)} custom-call(bf16[48,4096]{1,0:T(8,128)(2,1)S(1)} %get-tuple-element.28.refs_0_, bf16[48,4096]{1,0:T(8,128)(2,1)S(1)} %get-tuple-element.29.refs_1_, bf16[48,256]{1,0:T(8,128)(2,1)S(1)} %get-tuple-element.35.refs_2_, bf16[64,2048]{1,0:T(8,128)(2,1)S(1)} %collective-permute-done.1.refs_6_.refs_3_, ...), custom_call_target="tpu_custom_call" | custom-call | flops 1610612736 | bytes 1048576 | tf_op jit(solution)/shard_map/late_targets/pallas_call | solution.py:481
  25.2 0.8 %collective-permute-start.5 = (f32[64,256]{1,0:T(8,128)S(1)}, f32[64,256]{1,0:T(8,128)S(1)}, u32[]{:S(2)}, u32[]{:S(2)}) collective-permute-start(f32[64,256]{1,0:T(8,128)S(1)} %late_targets.3), channel_id=1, source_target_pairs={{0,4},{1,5},{2,6},{3,7},{4,0},{5,1},{6,2},{7,3},{8,12},{9,13},{10,... | collective-permute-start | bytes 196616 | tf_op jit(solution)/shard_map/ppermute | solution.py:401
  26.1 2.0 %late_targets.2 = f32[64,256]{1,0:T(8,128)S(1)} custom-call(bf16[48,4096]{1,0:T(8,128)(2,1)S(1)} %get-tuple-element.28.refs_0_, bf16[48,4096]{1,0:T(8,128)(2,1)S(1)} %get-tuple-element.29.refs_1_, bf16[48,256]{1,0:T(8,128)(2,1)S(1)} %get-tuple-element.30.refs_2_, bf16[64,2048]{1,0:T(8,128)(2,1)S(1)} %collective-permute-done.1.refs_6_.refs_3_, ...), custom_call_target="tpu_custom_call" | custom-call | flops 1610612736 | bytes 1048576 | tf_op jit(solution)/shard_map/late_targets/pallas_call | solution.py:481
  28.1 0.0 collective-permute-done.3
  28.1 1.2 %collective-permute-done.4 = f32[64,256]{1,0:T(8,128)S(1)} collective-permute-done((f32[64,256]{1,0:T(8,128)S(1)}, f32[64,256]{1,0:T(8,128)S(1)}, u32[]{:S(2)}, u32[]{:S(2)}) %collective-permute-start.4) | collective-permute-done | bytes 65568 | tf_op jit(solution)/shard_map/ppermute | solution.py:401
  29.2 1.2 %collective-permute-done.5 = f32[64,256]{1,0:T(8,128)S(1)} collective-permute-done((f32[64,256]{1,0:T(8,128)S(1)}, f32[64,256]{1,0:T(8,128)S(1)}, u32[]{:S(2)}, u32[]{:S(2)}) %collective-permute-start.5) | collective-permute-done | bytes 65568 | tf_op jit(solution)/shard_map/ppermute | solution.py:401
  30.4 0.7 %add_bitcast_fusion = f32[256,64]{0,1:T(8,128)} fusion(f32[64,256]{1,0:T(8,128)S(1)} %collective-permute-done.5, f32[64,256]{1,0:T(8,128)S(1)} %collective-permute-done.4, f32[64,256]{1,0:T(8,128)S(1)} %collective-permute-done.3, f32[64,256]{1,0:T(8,128)S(1)} %late_targets.2, bf16[64,2048]{1,0:T(8,128)(2,1)S(1)} %copy-done), kind=kLoop, calls=%fused_computation | loop fusion | flops 98304 | bytes 360448 | tf_op jit(solution)/shard_map/transpose | solution.py:500
Async XLA Ops:
  0.0 3.6 %collective-permute-start = (bf16[64,2048]{1,0:T(8,128)(2,1)}, bf16[64,2048]{1,0:T(8,128)(2,1)S(1)}, u32[]{:S(2)}, u32[]{:S(2)}) collective-permute-start(bf16[64,2048]{1,0:T(8,128)(2,1)} %refs_3_.2), channel_id=1, source_target_pairs={{0,1},{1,0},{2,3},{3,2},{4,5},{5,4},{6,7},{7,6},{8,9},{9,8},{10,11... | collective-permute-start | bytes 786440 | tf_op jit(solution)/shard_map/ppermute | solution.py:401
  0.5 11.5 %collective-permute-start.1 = (bf16[64,2048]{1,0:T(8,128)(2,1)}, bf16[64,2048]{1,0:T(8,128)(2,1)S(1)}, u32[]{:S(2)}, u32[]{:S(2)}) collective-permute-start(bf16[64,2048]{1,0:T(8,128)(2,1)} %refs_3_.2), channel_id=1, source_target_pairs={{0,2},{1,3},{2,0},{3,1},{4,6},{5,7},{6,4},{7,5},{8,10},{9,11},{10,... | collective-permute-start | bytes 786440 | tf_op jit(solution)/shard_map/ppermute | solution.py:401
  3.6 8.6 %copy-start = (bf16[64,2048]{1,0:T(8,128)(2,1)S(1)}, bf16[64,2048]{1,0:T(8,128)(2,1)}, u32[]{:S(2)}) copy-start(bf16[64,2048]{1,0:T(8,128)(2,1)} %refs_3_.2) | copy-start | bytes 786436
  11.9 2.3 %collective-permute-start.2 = (bf16[64,2048]{1,0:T(8,128)(2,1)S(1)}, bf16[64,2048]{1,0:T(8,128)(2,1)S(1)}, u32[]{:S(2)}, u32[]{:S(2)}) collective-permute-start(bf16[64,2048]{1,0:T(8,128)(2,1)S(1)} %collective-permute-done.1.refs_6_.refs_3_), channel_id=1, source_target_pairs={{0,1},{1,0},{2,3},{3,2},{4,5},{5,4},{6,7},{7,6},{8,9},{9,8},{10,11... | collective-permute-start | bytes 786440 | tf_op jit(solution)/shard_map/ppermute | solution.py:401
  14.2 0.7 %copy-start.1 = (f32[8,128]{1,0:T(8,128)S(1)}, f32[8,128]{1,0:T(8,128)}, u32[]{:S(2)}) copy-start(f32[8,128]{1,0:T(8,128)} %constant.10.clone.refs_5_.refs_2_) | copy-start | bytes 12292
  19.6 8.5 %collective-permute-start.3 = (f32[64,256]{1,0:T(8,128)S(1)}, f32[64,256]{1,0:T(8,128)S(1)}, u32[]{:S(2)}, u32[]{:S(2)}) collective-permute-start(f32[64,256]{1,0:T(8,128)S(1)} %get-tuple-element.33), channel_id=1, source_target_pairs={{0,12},{1,13},{2,14},{3,15},{4,8},{5,9},{6,10},{7,11},{8,4},{9,5},... | collective-permute-start | bytes 196616 | tf_op jit(solution)/shard_map/ppermute | solution.py:401
  23.2 6.0 %collective-permute-start.4 = (f32[64,256]{1,0:T(8,128)S(1)}, f32[64,256]{1,0:T(8,128)S(1)}, u32[]{:S(2)}, u32[]{:S(2)}) collective-permute-start(f32[64,256]{1,0:T(8,128)S(1)} %get-tuple-element.34), channel_id=1, source_target_pairs={{0,8},{1,9},{2,10},{3,11},{4,12},{5,13},{6,14},{7,15},{8,0},{9,1},... | collective-permute-start | bytes 196616 | tf_op jit(solution)/shard_map/ppermute | solution.py:401
  25.2 5.2 %collective-permute-start.5 = (f32[64,256]{1,0:T(8,128)S(1)}, f32[64,256]{1,0:T(8,128)S(1)}, u32[]{:S(2)}, u32[]{:S(2)}) collective-permute-start(f32[64,256]{1,0:T(8,128)S(1)} %late_targets.3), channel_id=1, source_target_pairs={{0,4},{1,5},{2,6},{3,7},{4,0},{5,1},{6,2},{7,3},{8,12},{9,13},{10,... | collective-permute-start | bytes 196616 | tf_op jit(solution)/shard_map/ppermute | solution.py:401

commit v5 on v4

--- a/solution.py
+++ b/solution.py
@@ -12,8 +12,7 @@
 NPH = 256
 BAND_DEV = 256
 FREQS = 32
-HALF = 24
-FEATS = 2 * HALF
+FEATS = 64
 BLOCK = 1024
 CHUNK = 1024
 TGT_STEP = 768
@@ -78,6 +77,16 @@
     )
 
 
+def heights(first, last, first_cos):
+    found, limits = [], []
+    for ring, sign in ((first, first_cos), (last, -first_cos)):
+        low = jnp.min(ring, axis=1, keepdims=True) * sign
+        high = jnp.max(ring, axis=1, keepdims=True) * sign
+        found += [0.25 * low + 0.75 * high, 0.75 * low + 0.25 * high]
+        limits.append(0.5 * (low + high))
+    return found + limits
+
+
 def at_lanes(ref, row, first, lanes):
     values = jnp.broadcast_to(ref[row : row + 1, first : first + 128], lanes.shape)
     return jnp.take_along_axis(values, lanes, axis=1)
@@ -156,40 +165,52 @@
     return jnp.concatenate(blocks, axis=1)
 
 
-def pieces_of(vector):
-    parts = [split(coordinate) for coordinate in vector]
-    return [[part[k] for part in parts] for k in range(3)]
+def left_pieces(value):
+    one, two, three = split(value)
+    return [one, one, one, two, two, three]
+
+
+def right_pieces(value):
+    one, two, three = split(value)
+    return [one, two, three, one, two, one]
+
+
+def padded(rows):
+    return rows + [jnp.zeros((8, 128), F32)] * (FEATS - len(rows))
 
 
 def target_features(corners, geometry, stage_ref):
-    centers, _ = panels(corners, *geometry[:3])
-    ones = jnp.ones((8, 128), F32)
-    rows = []
-    for origin in geometry[3:]:
-        offset = centers[:2] + [centers[2] - origin]
-        square = offset[0] * offset[0] + offset[1] * offset[1] + offset[2] * offset[2]
-        one, two, three = pieces_of(offset)
-        rows += one + one + one + two + two + three + split(square) + [ones] * 3
-    return as_rows(rows, stage_ref)
+    (x, y, z), _ = panels(corners, *geometry[:3])
+    ones = [jnp.ones((8, 128), F32)] * 3
+    rows = left_pieces(x) + left_pieces(y) + split(x * x + y * y) + ones
+    for height in geometry[3][:4]:
+        rise = z - height
+        rows += left_pieces(rise) + split(rise * rise)
+    return as_rows(padded(rows), stage_ref)
 
 
 def source_features(corners, geometry, stage_refs):
-    centers, areas = panels(corners, *geometry[:3])
-    north, south = geometry[3:]
-    upper = centers[2] >= 0.0
-    offset = centers[:2] + [centers[2] - jnp.where(upper, north, south)]
-    square = offset[0] * offset[0] + offset[1] * offset[1] + offset[2] * offset[2]
-    level = offset[0] * areas[0] + offset[1] * areas[1] + offset[2] * areas[2]
+    (x, y, z), areas = panels(corners, *geometry[:3])
+    *levels, north, south = geometry[3]
+    upper = z >= 0.0
+    places = [z >= north, upper & (z < north), z <= south, ~upper & (z > south)]
+    height = jnp.where(
+        upper, jnp.where(places[0], levels[0], levels[1]), jnp.where(places[2], levels[2], levels[3])
+    )
+    rise = z - height
     zeros = jnp.zeros((8, 128), F32)
+    square = x * x + y * y + rise * rise
+    level = x * areas[0] + y * areas[1] + rise * areas[2]
     found = []
-    for vector, flat, last, stage_ref in (
-        ([-2.0 * x for x in offset], zeros + 1.0, square, stage_refs[0]),
+    for (a, b, c), flat, last, stage_ref in (
+        ((-2.0 * x, -2.0 * y, -2.0 * rise), zeros + 1.0, square, stage_refs[0]),
         (areas, zeros, -level, stage_refs[1]),
     ):
-        one, two, three = pieces_of(vector)
-        rows = one + two + three + one + two + one + [flat] * 3 + split(last)
-        rows = [jnp.where(upper, x, 0.0) for x in rows] + [jnp.where(upper, 0.0, x) for x in rows]
-        found.append(as_rows(rows, stage_ref))
+        rows = right_pieces(a) + right_pieces(b) + [flat] * 3 + split(last)
+        along = right_pieces(c) + [flat] * 3
+        for place in places:
+            rows += [jnp.where(place, row, 0.0) for row in along]
+        found.append(as_rows(padded(rows), stage_ref))
     return found
 
 
@@ -199,8 +220,7 @@
     flow = lax.dot_general(flux, target, contract, preferred_element_type=F32)
     if apart is not None:
         dist_sq = jnp.concatenate([dist_sq[:BAND_DEV] + apart, dist_sq[BAND_DEV:]], axis=0)
-    inverse = lax.rsqrt(dist_sq)
-    tile = (flow * inverse * (inverse * inverse)).astype(BF16)
+    tile = (flow * lax.rsqrt(dist_sq * dist_sq * dist_sq)).astype(BF16)
     return jnp.dot(density, tile, preferred_element_type=F32)
 
 
@@ -316,15 +336,16 @@
     radius = radius_table(
         sample_ref[0], lattice_ref[...], modes_ref[...], polar_ref[...], azim_ref[...], pitch
     )
-    north = jnp.mean(radius[0:1], axis=1, keepdims=True) * first_cos
-    south = -jnp.mean(radius[cycle_count - 1 : cycle_count], axis=1, keepdims=True) * first_cos
-    origin_ref[0:1] = jnp.broadcast_to(north, (1, 128))
-    origin_ref[1:2] = jnp.broadcast_to(south, (1, 128))
+    rows = angles_ref.shape[0]
+    origin_ref[0:rows] = angles_ref[...]
+    levels = heights(radius[0:1], radius[cycle_count - 1 : cycle_count], first_cos)
+    for k, level in enumerate(levels):
+        origin_ref[rows + k : rows + k + 1] = jnp.broadcast_to(level, (1, 128))
     table_ref[...] = radius
     for copy in copies:
         copy.wait()
 
-    geometry = (table_ref, angles_ref, cycle_count, north, south)
+    geometry = (table_ref, angles_ref, cycle_count, levels)
     found = [
         target_features(tgt_corners[:, first : first + BLOCK], geometry, stage_ref.at[0])
         for first in range(0, tgt_corners.shape[1], BLOCK)
@@ -348,19 +369,21 @@
 
 
 def second_kernel(
-    near, group, cycle_count, corners_ref, table_ref, angles_ref, origin_ref, far_ref, part_ref, *refs
+    near, group, cycle_count, corners_ref, table_ref, origin_ref, far_ref, part_ref, *refs
 ):
     rest = group - near
     density_refs, refs = refs[:rest], refs[rest:]
     (*sums_refs, dist_ref, flux_ref, held_ref, total_ref, stage_ref, density_sems) = refs
     copies = start_density(density_refs, held_ref, density_sems)
-    geometry = (table_ref, angles_ref, cycle_count, origin_ref[0:1, 0:1], origin_ref[1:2, 0:1])
+    rows = origin_ref.shape[0] - 8
+    levels = [origin_ref[rows + k : rows + k + 1, 0:1] for k in range(6)]
+    geometry = (table_ref, origin_ref, cycle_count, levels)
     total_ref[...] = part_ref[...]
     for copy in copies:
         copy.wait()
     far_steps(corners_ref, held_ref, far_ref, total_ref, dist_ref, flux_ref, geometry, stage_ref)
     for k, ref in enumerate(sums_refs):
-        ref[...] = total_ref[:, k * BAND_DEV : (k + 1) * BAND_DEV]
+        ref[...] = total_ref[:, k * BAND_DEV : (k + 1) * BAND_DEV].astype(BF16)
 
 
 def kept_kernel(own, count, dist_ref, flux_ref, target_ref, *refs):
@@ -380,7 +403,7 @@
             dist_ref[:, here], flux_ref[:, here], target, density_refs[k][...], None if k else apart
         )
         total = sums if total is None else total + sums
-    sums_ref[...] = total
+    sums_ref[...] = total.astype(sums_ref.dtype)
 
 
 def per_device(sample_index, lattice_vector, mode_table, connectivity, density):
@@ -421,7 +444,7 @@
             lambda *refs: first_kernel(near, row_total, group, sizes, *refs),
             out_shape=[
                 shape(pitch, NPH, dtype=F32),
-                shape(8, 128, dtype=F32),
+                shape(tables[2].shape[0] + 8, 128, dtype=F32),
                 shape(FEATS, early),
                 shape(FEATS, BAND_DEV),
                 shape(FEATS, BAND_DEV),
@@ -462,9 +485,9 @@
     rest = group - near
     *sums, dist_rest, flux_rest = pl.pallas_call(
         lambda *refs: second_kernel(near, group, cycle_count, *refs),
-        out_shape=[shape(columns, BAND_DEV, dtype=F32)] * (groups - 2)
+        out_shape=[shape(columns, BAND_DEV)] * (groups - 2)
         + [shape(FEATS, rest * src_dev)] * 2,
-        in_specs=[vmem] * 6 + [anywhere] * rest,
+        in_specs=[vmem] * 5 + [anywhere] * rest,
         out_specs=[vmem] * groups,
         scratch_shapes=[
             pltpu.VMEM((columns, rest * src_dev), BF16),
@@ -475,28 +498,28 @@
         compiler_params=params,
         cost_estimate=cost(rest * src_dev, early),
         name="other_sources",
-    )(corners, table, small[4], origins, tgt_early, part_early, *densities[near:])
-
-    def kept(features, target, blocks, own, part):
+    )(corners, table, origins, tgt_early, part_early, *densities[near:])
+
+    def kept(features, target, blocks, own, part, dtype=F32):
         return pl.pallas_call(
             lambda *refs: kept_kernel(own, len(blocks), *refs),
-            out_shape=shape(columns, BAND_DEV, dtype=F32),
+            out_shape=shape(columns, BAND_DEV, dtype=dtype),
             in_specs=[vmem] * (3 + len(blocks) + len(part)),
             out_specs=vmem,
             compiler_params=params,
             cost_estimate=cost(len(blocks) * src_dev, BAND_DEV),
-            name="own_targets" if own else "late_targets",
+            name="own_first" if own else "late_targets" if dtype == BF16 else "own_last",
         )(*features, target, *blocks, *part)
 
     rest_features = (dist_rest, flux_rest)
     own_sums = kept(near_features, tgt_own, densities[:near], True, [])
-    sums.append(kept(rest_features, tgt_late, densities[near:], False, [part_late]))
+    sums.append(kept(rest_features, tgt_late, densities[near:], False, [part_late], BF16))
     own_sums = kept(rest_features, tgt_own, densities[near:], False, [own_sums])
     total = 0.5 * density[:, :BAND_DEV].astype(F32) + own_sums
     for k, block in enumerate(sums):
         total = total + moved(
             block, lambda r, k=k: partner(r // group, k + 1, groups) * group + r % group
-        )
+        ).astype(F32)
     return total.T
 
 

time: 31.3 us -> 28.6 us (0.914)
  waiting for transfers between devices: 2.36 us -> 1.14 us
  Pallas kernels: 18.9 us -> 18.2 us
  local copies, waits for them, and re-layouts: 0.68 us -> 0.01 us
    ppermute x6, waiting for transfers between devices: 2.36 us -> 1.14 us  [moved(): lax.ppermute(array, 'row', [(r, target_of(r)) for r in range(row_total)])]
    unnamed x4 -> x2, local copies, waits for them, and re-layouts: 0.68 us -> 0.01 us
    pallas_call x1, Pallas kernels: 8.25 us -> 7.88 us  [per_device(): pl.pallas_call(lambda *refs: first_kernel(near, row_total, group, sizes,...]
    pallas_call x1, Pallas kernels: 4.64 us -> 4.3 us  [per_device(): pl.pallas_call(lambda *refs: second_kernel(near, group, cycle_count, *ref...]
  transfers between devices with their start and end apart: 6 -> 6, of which waited for: 2 -> 1; matrix products, arithmetic and copies ran while one was open for 0% -> 0% of each run, Pallas kernels for 46% -> 49%
where the time goes in v5:
time: 28.6 us; the launch traced here: 28.5 us
  Pallas kernels  18.2 us (64%)
  starting transfers between devices  7.77 us (27%)
  waiting for transfers between devices  1.14 us (4%)
  between operations  0.74 us (3%)
  other arithmetic  0.65 us (2%)
    pallas_call x1, Pallas kernels, per_device(): pl.pallas_call(lambda *refs: first_kernel(near, row_total, group, sizes,...  7.88 us
    ppermute x6, starting transfers between devices, moved(): lax.ppermute(array, 'row', [(r, target_of(r)) for r in range(row_total)])  7.77 us
    pallas_call x3, Pallas kernels, kept(): pl.pallas_call(lambda *refs: kept_kernel(own, len(blocks), *refs), out_sh...  5.97 us
    pallas_call x1, Pallas kernels, per_device(): pl.pallas_call(lambda *refs: second_kernel(near, group, cycle_count, *ref...  4.3 us
    ppermute x6, waiting for transfers between devices, moved(): lax.ppermute(array, 'row', [(r, target_of(r)) for r in range(row_total)])  1.14 us
    transpose x1, other arithmetic, per_device(): return total.T  0.65 us
  transfers between devices with their start and end apart: 6, of which 1 were waited for; matrix products, arithmetic and copies ran while one was open for 0% of the time, Pallas kernels for 49%

profile of v5, /device:TPU:0, one launch (start us, length us, event | category | flops | bytes accessed | tf_op | source)
XLA Modules:
  0.0 28.5 jit_solution(2338212238385553142)
XLA Ops:
  0.0 0.5 %collective-permute-start = (bf16[64,2048]{1,0:T(8,128)(2,1)}, bf16[64,2048]{1,0:T(8,128)(2,1)S(1)}, u32[]{:S(2)}, u32[]{:S(2)}) collective-permute-start(bf16[64,2048]{1,0:T(8,128)(2,1)} %refs_3_.2), channel_id=1, source_target_pairs={{0,1},{1,0},{2,3},{3,2},{4,5},{5,4},{6,7},{7,6},{8,9},{9,8},{10,11... | collective-permute-start | bytes 786440 | tf_op jit(solution)/shard_map/ppermute | solution.py:424
  0.5 2.5 %collective-permute-start.1 = (bf16[64,2048]{1,0:T(8,128)(2,1)}, bf16[64,2048]{1,0:T(8,128)(2,1)S(1)}, u32[]{:S(2)}, u32[]{:S(2)}) collective-permute-start(bf16[64,2048]{1,0:T(8,128)(2,1)} %refs_3_.2), channel_id=1, source_target_pairs={{0,2},{1,3},{2,0},{3,1},{4,6},{5,7},{6,4},{7,5},{8,10},{9,11},{10,... | collective-permute-start | bytes 786440 | tf_op jit(solution)/shard_map/ppermute | solution.py:424
  3.6 0.0 collective-permute-done.refs_8_.refs_4_
  3.6 0.0 copy-start
  3.6 7.9 %near_sources.1 = (f32[72,256]{1,0:T(8,128)S(1)}, f32[16,128]{1,0:T(8,128)S(1)}, bf16[64,512]{1,0:T(8,128)(2,1)S(1)}, bf16[64,256]{1,0:T(8,128)(2,1)S(1)}, bf16[...) custom-call(s32[1]{0:T(128)S(6)} %copy.9.refs_0_, ...), custom_call_target="tpu_custom_call" | custom-call | flops 4831838208 | bytes 1048576 | tf_op jit(solution)/shard_map/near_sources/pallas_call | solution.py:443
  11.5 0.0 collective-permute-done.1.refs_5_.refs_3_
  11.5 0.3 collective-permute-start.2
  11.8 0.0 copy-done
  11.8 2.0 %own_first.1.refs_5_ = f32[64,256]{1,0:T(8,128)S(1)} custom-call(bf16[64,4096]{1,0:T(8,128)(2,1)S(1)} %get-tuple-element.31.refs_0_, bf16[64,4096]{1,0:T(8,128)(2,1)S(1)} %get-tuple-element.32.refs_1_, bf16[64,256]{1,0:T(8,128)(2,1)S(1)} %get-tuple-element.30.refs_2_, bf16[64,2048]{1,0:T(8,128)(2,1)S(1)} %copy-done, ...), custom_call_target="tpu_custom_call" | custom-call | flops 1610612736 | bytes 1048576 | tf_op jit(solution)/shard_map/own_first/pallas_call | solution.py:504
  13.8 0.0 collective-permute-done.2.refs_6_.refs_4_
  13.8 4.3 %other_sources.1 = (bf16[64,256]{1,0:T(8,128)(2,1)S(1)}, bf16[64,256]{1,0:T(8,128)(2,1)S(1)}, bf16[64,4096]{1,0:T(8,128)(2,1)S(1)}, bf16[64,4096]{1,0:T(8,128)(2,1)S(1)}) custom-call(s32[3,4096]{1,0:T(4,128)S(1)} %get-tuple-element.21.refs_0_, f32[72,256]{1,0:T(8,128)S(1)} %get-tuple-element.22.refs_1_, f32[16,128]{1,0:T(8,128)S(1)} %get-tuple-element.24.refs_2_, ...), custom_call_target="tpu_custom_call" | custom-call | flops 3221225472 | bytes 1048576 | tf_op jit(solution)/shard_map/other_sources/pallas_call | solution.py:486
  18.2 3.7 %collective-permute-start.3 = (bf16[64,256]{1,0:T(8,128)(2,1)S(1)}, bf16[64,256]{1,0:T(8,128)(2,1)S(1)}, u32[]{:S(2)}, u32[]{:S(2)}) collective-permute-start(bf16[64,256]{1,0:T(8,128)(2,1)S(1)} %get-tuple-element.33), channel_id=1, source_target_pairs={{0,12},{1,13},{2,14},{3,15},{4,8},{5,9},{6,10},{7,11},{8,4},{9,5},... | collective-permute-start | bytes 98312 | tf_op jit(solution)/shard_map/ppermute | solution.py:424
  21.8 0.0 collective-permute-start.4
  21.8 2.0 %late_targets.1 = bf16[64,256]{1,0:T(8,128)(2,1)S(1)} custom-call(bf16[64,4096]{1,0:T(8,128)(2,1)S(1)} %get-tuple-element.28.refs_0_, bf16[64,4096]{1,0:T(8,128)(2,1)S(1)} %get-tuple-element.29.refs_1_, bf16[64,256]{1,0:T(8,128)(2,1)S(1)} %get-tuple-element.35.refs_2_, bf16[64,2048]{1,0:T(8,128)(2,1)S(1)} %collective-permute-done.1.refs_5_.refs_3_, ...), custom_call_target="tpu_custom_call" | custom-call | flops 1610612736 | bytes 1048576 | tf_op jit(solution)/shard_map/late_targets/pallas_call | solution.py:504
  23.8 0.8 %collective-permute-start.5 = (bf16[64,256]{1,0:T(8,128)(2,1)S(1)}, bf16[64,256]{1,0:T(8,128)(2,1)S(1)}, u32[]{:S(2)}, u32[]{:S(2)}) collective-permute-start(bf16[64,256]{1,0:T(8,128)(2,1)S(1)} %late_targets.1), channel_id=1, source_target_pairs={{0,4},{1,5},{2,6},{3,7},{4,0},{5,1},{6,2},{7,3},{8,12},{9,13},{10,... | collective-permute-start | bytes 98312 | tf_op jit(solution)/shard_map/ppermute | solution.py:424
  24.7 2.0 %own_last.1 = f32[64,256]{1,0:T(8,128)S(1)} custom-call(bf16[64,4096]{1,0:T(8,128)(2,1)S(1)} %get-tuple-element.28.refs_0_, bf16[64,4096]{1,0:T(8,128)(2,1)S(1)} %get-tuple-element.29.refs_1_, bf16[64,256]{1,0:T(8,128)(2,1)S(1)} %get-tuple-element.30.refs_2_, bf16[64,2048]{1,0:T(8,128)(2,1)S(1)} %collective-permute-done.1.refs_5_.refs_3_, ...), custom_call_target="tpu_custom_call" | custom-call | flops 1610612736 | bytes 1048576 | tf_op jit(solution)/shard_map/own_last/pallas_call | solution.py:504
  26.7 0.0 collective-permute-done.3
  26.7 0.0 collective-permute-done.4
  26.7 1.1 %collective-permute-done.5 = bf16[64,256]{1,0:T(8,128)(2,1)S(1)} collective-permute-done((bf16[64,256]{1,0:T(8,128)(2,1)S(1)}, bf16[64,256]{1,0:T(8,128)(2,1)S(1)}, u32[]{:S(2)}, u32[]{:S(2)}) %collective-permute-start.5) | collective-permute-done | bytes 32800 | tf_op jit(solution)/shard_map/ppermute | solution.py:424
  27.8 0.7 %add_bitcast_fusion = f32[256,64]{0,1:T(8,128)} fusion(bf16[64,256]{1,0:T(8,128)(2,1)S(1)} %collective-permute-done.5, bf16[64,256]{1,0:T(8,128)(2,1)S(1)} %collective-permute-done.4, bf16[64,256]{1,0:T(8,128)(2,1)S(1)} %collective-permute-done.3, f32[64,256]{1,0:T(8,128)S(1)} %own_last.1, bf16[64,2048]{1,0:T(8,128)(2,1)S(1)} %copy-done), kind=kLoop, calls=%fused_computation | loop fusion | flops 147456 | bytes 262144 | tf_op jit(solution)/shard_map/transpose | solution.py:523
Async XLA Ops:
  0.0 3.6 %collective-permute-start = (bf16[64,2048]{1,0:T(8,128)(2,1)}, bf16[64,2048]{1,0:T(8,128)(2,1)S(1)}, u32[]{:S(2)}, u32[]{:S(2)}) collective-permute-start(bf16[64,2048]{1,0:T(8,128)(2,1)} %refs_3_.2), channel_id=1, source_target_pairs={{0,1},{1,0},{2,3},{3,2},{4,5},{5,4},{6,7},{7,6},{8,9},{9,8},{10,11... | collective-permute-start | bytes 786440 | tf_op jit(solution)/shard_map/ppermute | solution.py:424
  0.5 11.1 %collective-permute-start.1 = (bf16[64,2048]{1,0:T(8,128)(2,1)}, bf16[64,2048]{1,0:T(8,128)(2,1)S(1)}, u32[]{:S(2)}, u32[]{:S(2)}) collective-permute-start(bf16[64,2048]{1,0:T(8,128)(2,1)} %refs_3_.2), channel_id=1, source_target_pairs={{0,2},{1,3},{2,0},{3,1},{4,6},{5,7},{6,4},{7,5},{8,10},{9,11},{10,... | collective-permute-start | bytes 786440 | tf_op jit(solution)/shard_map/ppermute | solution.py:424
  3.6 8.2 %copy-start = (bf16[64,2048]{1,0:T(8,128)(2,1)S(1)}, bf16[64,2048]{1,0:T(8,128)(2,1)}, u32[]{:S(2)}) copy-start(bf16[64,2048]{1,0:T(8,128)(2,1)} %refs_3_.2) | copy-start | bytes 786436
  11.5 2.3 %collective-permute-start.2 = (bf16[64,2048]{1,0:T(8,128)(2,1)S(1)}, bf16[64,2048]{1,0:T(8,128)(2,1)S(1)}, u32[]{:S(2)}, u32[]{:S(2)}) collective-permute-start(bf16[64,2048]{1,0:T(8,128)(2,1)S(1)} %collective-permute-done.1.refs_5_.refs_3_), channel_id=1, source_target_pairs={{0,1},{1,0},{2,3},{3,2},{4,5},{5,4},{6,7},{7,6},{8,9},{9,8},{10,11... | collective-permute-start | bytes 786440 | tf_op jit(solution)/shard_map/ppermute | solution.py:424
  18.2 8.5 %collective-permute-start.3 = (bf16[64,256]{1,0:T(8,128)(2,1)S(1)}, bf16[64,256]{1,0:T(8,128)(2,1)S(1)}, u32[]{:S(2)}, u32[]{:S(2)}) collective-permute-start(bf16[64,256]{1,0:T(8,128)(2,1)S(1)} %get-tuple-element.33), channel_id=1, source_target_pairs={{0,12},{1,13},{2,14},{3,15},{4,8},{5,9},{6,10},{7,11},{8,4},{9,5},... | collective-permute-start | bytes 98312 | tf_op jit(solution)/shard_map/ppermute | solution.py:424
  21.8 4.8 %collective-permute-start.4 = (bf16[64,256]{1,0:T(8,128)(2,1)S(1)}, bf16[64,256]{1,0:T(8,128)(2,1)S(1)}, u32[]{:S(2)}, u32[]{:S(2)}) collective-permute-start(bf16[64,256]{1,0:T(8,128)(2,1)S(1)} %get-tuple-element.34), channel_id=1, source_target_pairs={{0,8},{1,9},{2,10},{3,11},{4,12},{5,13},{6,14},{7,15},{8,0},{9,1},... | collective-permute-start | bytes 98312 | tf_op jit(solution)/shard_map/ppermute | solution.py:424
  23.8 4.0 %collective-permute-start.5 = (bf16[64,256]{1,0:T(8,128)(2,1)S(1)}, bf16[64,256]{1,0:T(8,128)(2,1)S(1)}, u32[]{:S(2)}, u32[]{:S(2)}) collective-permute-start(bf16[64,256]{1,0:T(8,128)(2,1)S(1)} %late_targets.1), channel_id=1, source_target_pairs={{0,4},{1,5},{2,6},{3,7},{4,0},{5,1},{6,2},{7,3},{8,12},{9,13},{10,... | collective-permute-start | bytes 98312 | tf_op jit(solution)/shard_map/ppermute | solution.py:424

commit v6 on v5

--- a/solution.py
+++ b/solution.py
@@ -16,6 +16,7 @@
 BLOCK = 1024
 CHUNK = 1024
 TGT_STEP = 768
+KEPT_STEP = 1024
 VMEM = 30 << 20
 F32 = jnp.float32
 BF16 = jnp.bfloat16
@@ -225,11 +226,12 @@
 
 
 def far_steps(
-    corners_ref, density_ref, target_ref, total_ref, dist_ref, flux_ref, geometry, stage_ref
+    corners_ref, density_refs, target_ref, total_ref, dist_ref, flux_ref, geometry, stage_ref
 ):
     src_total = corners_ref.shape[1]
+    src_dev = density_refs[0].shape[1]
     tgt_total = target_ref.shape[1]
-    chunk = min(CHUNK, src_total)
+    chunk = min(CHUNK, src_dev)
     steps = src_total // chunk
     tgt_step = max(
         step for step in range(BAND_DEV, TGT_STEP + 1, BAND_DEV) if tgt_total % step == 0
@@ -254,7 +256,8 @@
 
     def apply(turn, dist, flux):
         here = pl.ds(turn * chunk, chunk)
-        density = density_ref[:, here]
+        first = turn * chunk % src_dev
+        density = density_refs[turn * chunk // src_dev][:, first : first + chunk]
 
         def some(step):
             cols = pl.ds(pl.multiple_of(step * tgt_step, 128), tgt_step)
@@ -289,21 +292,11 @@
     return copies
 
 
-def start_density(density_refs, held_ref, sems):
-    copies = []
-    for k, ref in enumerate(density_refs):
-        count = ref.shape[1]
-        copy = pltpu.make_async_copy(ref, held_ref.at[:, pl.ds(k * count, count)], sems.at[k])
-        copy.start()
-        copies.append(copy)
-    return copies
-
-
 def first_kernel(near, row_total, group, sizes, sample_ref, *refs):
     small_refs, connectivity_ref, density_refs, refs = refs[:5], refs[5], refs[6 : 6 + near], refs[6 + near :]
     (table_ref, origin_ref, *tgt_refs, dist_ref, flux_ref, rest_ref), refs = refs[:10], refs[10:]
     feature_refs, part_refs = tgt_refs[:3], tgt_refs[3:]
-    small, (src_corners, tgt_corners, held_ref, stage_ref, far_ref, total_ref, small_sems, src_sems, rest_sems, tgt_sems, density_sems) = (
+    small, (src_corners, tgt_corners, held_ref, stage_ref, far_ref, total_ref, small_sems, src_sems, rest_sems, tgt_sems, density_sem) = (
         refs[:5], refs[5:],
     )
     lattice_ref, modes_ref, polar_ref, azim_ref, angles_ref = small
@@ -325,7 +318,9 @@
         connectivity_ref, src_corners, src_sems,
         [(own_group * group + (place ^ k)) * src_dev for k in range(near)], src_dev,
     )
-    copies += start_density(density_refs, held_ref, density_sems)
+    held_copy = pltpu.make_async_copy(density_refs[0], held_ref, density_sem)
+    held_copy.start()
+    copies.append(held_copy)
     rest_copies = start_corners(
         connectivity_ref, rest_ref, rest_sems,
         [(own_group * group + (place ^ k)) * src_dev for k in range(near, group)], src_dev,
@@ -358,7 +353,9 @@
         first += ref.shape[1]
     total_ref[...] = jnp.zeros_like(total_ref)
     far_steps(
-        src_corners, held_ref, far_ref, total_ref, dist_ref, flux_ref, geometry, stage_ref
+        src_corners,
+        (held_ref, *density_refs[1:]),
+        far_ref, total_ref, dist_ref, flux_ref, geometry, stage_ref,
     )
     first = 0
     for ref in part_refs:
@@ -373,15 +370,14 @@
 ):
     rest = group - near
     density_refs, refs = refs[:rest], refs[rest:]
-    (*sums_refs, dist_ref, flux_ref, held_ref, total_ref, stage_ref, density_sems) = refs
-    copies = start_density(density_refs, held_ref, density_sems)
+    (*sums_refs, dist_ref, flux_ref, total_ref, stage_ref) = refs
     rows = origin_ref.shape[0] - 8
     levels = [origin_ref[rows + k : rows + k + 1, 0:1] for k in range(6)]
     geometry = (table_ref, origin_ref, cycle_count, levels)
     total_ref[...] = part_ref[...]
-    for copy in copies:
-        copy.wait()
-    far_steps(corners_ref, held_ref, far_ref, total_ref, dist_ref, flux_ref, geometry, stage_ref)
+    far_steps(
+        corners_ref, density_refs, far_ref, total_ref, dist_ref, flux_ref, geometry, stage_ref
+    )
     for k, ref in enumerate(sums_refs):
         ref[...] = total_ref[:, k * BAND_DEV : (k + 1) * BAND_DEV].astype(BF16)
 
@@ -397,10 +393,13 @@
         ) == lax.broadcasted_iota(jnp.int32, (BAND_DEV, BAND_DEV), 1)
         apart = jnp.where(diagonal, 1e30, 0.0)
     total = part_refs[0][...] if part_refs else None
-    for k in range(count):
-        here = slice(k * src_dev, (k + 1) * src_dev)
+    step = KEPT_STEP
+    for first in range(0, count * src_dev, step):
+        here = slice(first, first + step)
+        inside = slice(first % src_dev, first % src_dev + step)
         sums = pair_sums(
-            dist_ref[:, here], flux_ref[:, here], target, density_refs[k][...], None if k else apart
+            dist_ref[:, here], flux_ref[:, here], target, density_refs[first // src_dev][:, inside],
+            None if first else apart,
         )
         total = sums if total is None else total + sums
     sums_ref[...] = total.astype(sums_ref.dtype)
@@ -418,7 +417,6 @@
     far_total = (groups - 1) * BAND_DEV
     vmem = pl.BlockSpec(memory_space=pltpu.VMEM)
     hbm = pl.BlockSpec(memory_space=pltpu.HBM)
-    anywhere = pl.BlockSpec(memory_space=pl.ANY)
     params = pltpu.CompilerParams(vmem_limit_bytes=VMEM)
     def moved(array, target_of):
         return lax.ppermute(array, "row", [(r, target_of(r)) for r in range(row_total)])
@@ -454,13 +452,13 @@
                 shape(FEATS, near * src_dev),
                 shape(3, (group - near) * src_dev, dtype=jnp.int32),
             ],
-            in_specs=[pl.BlockSpec(memory_space=pltpu.SMEM)] + [hbm] * 7 + [anywhere] * (near - 1),
+            in_specs=[pl.BlockSpec(memory_space=pltpu.SMEM)] + [hbm] * 7 + [vmem] * (near - 1),
             out_specs=[vmem] * 10,
             scratch_shapes=[pltpu.VMEM(array.shape, array.dtype) for array in small]
             + [
                 pltpu.VMEM((3, near * src_dev), jnp.int32),
                 pltpu.VMEM((3, groups * BAND_DEV), jnp.int32),
-                pltpu.VMEM((columns, near * src_dev), BF16),
+                pltpu.VMEM((columns, src_dev), BF16),
                 stage,
                 pltpu.VMEM((FEATS, far_total), BF16),
                 pltpu.VMEM((columns, far_total), F32),
@@ -468,7 +466,7 @@
                 pltpu.SemaphoreType.DMA((near,)),
                 pltpu.SemaphoreType.DMA((group - near,)),
                 pltpu.SemaphoreType.DMA((groups,)),
-                pltpu.SemaphoreType.DMA((near,)),
+                pltpu.SemaphoreType.DMA,
             ],
             compiler_params=params,
             cost_estimate=cost(near * src_dev, far_total),
@@ -487,13 +485,11 @@
         lambda *refs: second_kernel(near, group, cycle_count, *refs),
         out_shape=[shape(columns, BAND_DEV)] * (groups - 2)
         + [shape(FEATS, rest * src_dev)] * 2,
-        in_specs=[vmem] * 5 + [anywhere] * rest,
+        in_specs=[vmem] * (5 + rest),
         out_specs=[vmem] * groups,
         scratch_shapes=[
-            pltpu.VMEM((columns, rest * src_dev), BF16),
             pltpu.VMEM((columns, early), F32),
             stage,
-            pltpu.SemaphoreType.DMA((rest,)),
         ],
         compiler_params=params,
         cost_estimate=cost(rest * src_dev, early),

time: 28.6 us -> 28.1 us (0.983)
  Pallas kernels: 18.2 us -> 17.4 us
    pallas_call x3, Pallas kernels: 5.97 us -> 5.48 us  [kept(): pl.pallas_call(lambda *refs: kept_kernel(own, len(blocks), *refs), out_sh...]
  transfers between devices with their start and end apart: 6 -> 6, of which waited for: 1 -> 2; matrix products, arithmetic and copies ran while one was open for 0% -> 0% of each run, Pallas kernels for 49% -> 48%
where the time goes in v6:
time: 28.1 us; the launch traced here: 27.9 us
  Pallas kernels  17.4 us (62%)
  starting transfers between devices  7.79 us (28%)
  waiting for transfers between devices  1.35 us (5%)
  between operations  0.73 us (3%)
  other arithmetic  0.65 us (2%)
    pallas_call x1, Pallas kernels, per_device(): pl.pallas_call(lambda *refs: first_kernel(near, row_total, group, sizes,...  7.86 us
    ppermute x6, starting transfers between devices, moved(): lax.ppermute(array, 'row', [(r, target_of(r)) for r in range(row_total)])  7.79 us
    pallas_call x3, Pallas kernels, kept(): pl.pallas_call(lambda *refs: kept_kernel(own, len(blocks), *refs), out_sh...  5.48 us
    pallas_call x1, Pallas kernels, per_device(): pl.pallas_call(lambda *refs: second_kernel(near, group, cycle_count, *ref...  4.04 us
    ppermute x6, waiting for transfers between devices, moved(): lax.ppermute(array, 'row', [(r, target_of(r)) for r in range(row_total)])  1.35 us
    transpose x1, other arithmetic, per_device(): return total.T  0.65 us
  transfers between devices with their start and end apart: 6, of which 2 were waited for; matrix products, arithmetic and copies ran while one was open for 0% of the time, Pallas kernels for 48%

profile of v6, /device:TPU:0, one launch (start us, length us, event | category | flops | bytes accessed | tf_op | source)
XLA Modules:
  0.0 27.9 jit_solution(9248195416317096720)
XLA Ops:
  0.0 0.5 %collective-permute-start = (bf16[64,2048]{1,0:T(8,128)(2,1)}, bf16[64,2048]{1,0:T(8,128)(2,1)S(1)}, u32[]{:S(2)}, u32[]{:S(2)}) collective-permute-start(bf16[64,2048]{1,0:T(8,128)(2,1)} %refs_3_.2), channel_id=1, source_target_pairs={{0,1},{1,0},{2,3},{3,2},{4,5},{5,4},{6,7},{7,6},{8,9},{9,8},{10,11... | collective-permute-start | bytes 786440 | tf_op jit(solution)/shard_map/ppermute | solution.py:422
  0.5 2.5 %collective-permute-start.1 = (bf16[64,2048]{1,0:T(8,128)(2,1)}, bf16[64,2048]{1,0:T(8,128)(2,1)S(1)}, u32[]{:S(2)}, u32[]{:S(2)}) collective-permute-start(bf16[64,2048]{1,0:T(8,128)(2,1)} %refs_3_.2), channel_id=1, source_target_pairs={{0,2},{1,3},{2,0},{3,1},{4,6},{5,7},{6,4},{7,5},{8,10},{9,11},{10,... | collective-permute-start | bytes 786440 | tf_op jit(solution)/shard_map/ppermute | solution.py:422
  3.6 0.0 collective-permute-done.refs_8_.refs_4_
  3.6 0.0 copy-start
  3.6 7.9 %near_sources.1 = (f32[72,256]{1,0:T(8,128)S(1)}, f32[16,128]{1,0:T(8,128)S(1)}, bf16[64,512]{1,0:T(8,128)(2,1)S(1)}, bf16[64,256]{1,0:T(8,128)(2,1)S(1)}, bf16[...) custom-call(s32[1]{0:T(128)S(6)} %copy.9.refs_0_, ...), custom_call_target="tpu_custom_call" | custom-call | flops 4831838208 | bytes 1048576 | tf_op jit(solution)/shard_map/near_sources/pallas_call | solution.py:441
  11.5 0.0 collective-permute-done.1.refs_5_.refs_3_
  11.5 0.3 %collective-permute-start.2 = (bf16[64,2048]{1,0:T(8,128)(2,1)S(1)}, bf16[64,2048]{1,0:T(8,128)(2,1)S(1)}, u32[]{:S(2)}, u32[]{:S(2)}) collective-permute-start(bf16[64,2048]{1,0:T(8,128)(2,1)S(1)} %collective-permute-done.1.refs_5_.refs_3_), channel_id=1, source_target_pairs={{0,1},{1,0},{2,3},{3,2},{4,5},{5,4},{6,7},{7,6},{8,9},{9,8},{10,11... | collective-permute-start | bytes 786440 | tf_op jit(solution)/shard_map/ppermute | solution.py:422
  11.8 0.0 copy-done
  11.8 1.8 %own_first.1.refs_5_ = f32[64,256]{1,0:T(8,128)S(1)} custom-call(bf16[64,4096]{1,0:T(8,128)(2,1)S(1)} %get-tuple-element.31.refs_0_, bf16[64,4096]{1,0:T(8,128)(2,1)S(1)} %get-tuple-element.32.refs_1_, bf16[64,256]{1,0:T(8,128)(2,1)S(1)} %get-tuple-element.30.refs_2_, bf16[64,2048]{1,0:T(8,128)(2,1)S(1)} %copy-done, ...), custom_call_target="tpu_custom_call" | custom-call | flops 1610612736 | bytes 1048576 | tf_op jit(solution)/shard_map/own_first/pallas_call | solution.py:500
  13.6 0.0 collective-permute-done.2.refs_6_.refs_4_
  13.6 4.0 %other_sources.1 = (bf16[64,256]{1,0:T(8,128)(2,1)S(1)}, bf16[64,256]{1,0:T(8,128)(2,1)S(1)}, bf16[64,4096]{1,0:T(8,128)(2,1)S(1)}, bf16[64,4096]{1,0:T(8,128)(2,1)S(1)}) custom-call(s32[3,4096]{1,0:T(4,128)S(1)} %get-tuple-element.21.refs_0_, f32[72,256]{1,0:T(8,128)S(1)} %get-tuple-element.22.refs_1_, f32[16,128]{1,0:T(8,128)S(1)} %get-tuple-element.24.refs_2_, ...), custom_call_target="tpu_custom_call" | custom-call | flops 3221225472 | bytes 1048576 | tf_op jit(solution)/shard_map/other_sources/pallas_call | solution.py:484
  17.6 3.7 %collective-permute-start.3 = (bf16[64,256]{1,0:T(8,128)(2,1)S(1)}, bf16[64,256]{1,0:T(8,128)(2,1)S(1)}, u32[]{:S(2)}, u32[]{:S(2)}) collective-permute-start(bf16[64,256]{1,0:T(8,128)(2,1)S(1)} %get-tuple-element.33), channel_id=1, source_target_pairs={{0,12},{1,13},{2,14},{3,15},{4,8},{5,9},{6,10},{7,11},{8,4},{9,5},... | collective-permute-start | bytes 98312 | tf_op jit(solution)/shard_map/ppermute | solution.py:422
  21.3 0.0 collective-permute-start.4
  21.3 2.0 %late_targets.1 = bf16[64,256]{1,0:T(8,128)(2,1)S(1)} custom-call(bf16[64,4096]{1,0:T(8,128)(2,1)S(1)} %get-tuple-element.28.refs_0_, bf16[64,4096]{1,0:T(8,128)(2,1)S(1)} %get-tuple-element.29.refs_1_, bf16[64,256]{1,0:T(8,128)(2,1)S(1)} %get-tuple-element.35.refs_2_, bf16[64,2048]{1,0:T(8,128)(2,1)S(1)} %collective-permute-done.1.refs_5_.refs_3_, ...), custom_call_target="tpu_custom_call" | custom-call | flops 1610612736 | bytes 1048576 | tf_op jit(solution)/shard_map/late_targets/pallas_call | solution.py:500
  23.3 0.9 %collective-permute-start.5 = (bf16[64,256]{1,0:T(8,128)(2,1)S(1)}, bf16[64,256]{1,0:T(8,128)(2,1)S(1)}, u32[]{:S(2)}, u32[]{:S(2)}) collective-permute-start(bf16[64,256]{1,0:T(8,128)(2,1)S(1)} %late_targets.1), channel_id=1, source_target_pairs={{0,4},{1,5},{2,6},{3,7},{4,0},{5,1},{6,2},{7,3},{8,12},{9,13},{10,... | collective-permute-start | bytes 98312 | tf_op jit(solution)/shard_map/ppermute | solution.py:422
  24.1 1.8 %own_last.1 = f32[64,256]{1,0:T(8,128)S(1)} custom-call(bf16[64,4096]{1,0:T(8,128)(2,1)S(1)} %get-tuple-element.28.refs_0_, bf16[64,4096]{1,0:T(8,128)(2,1)S(1)} %get-tuple-element.29.refs_1_, bf16[64,256]{1,0:T(8,128)(2,1)S(1)} %get-tuple-element.30.refs_2_, bf16[64,2048]{1,0:T(8,128)(2,1)S(1)} %collective-permute-done.1.refs_5_.refs_3_, ...), custom_call_target="tpu_custom_call" | custom-call | flops 1610612736 | bytes 1048576 | tf_op jit(solution)/shard_map/own_last/pallas_call | solution.py:500
  25.9 0.0 collective-permute-done.3
  25.9 0.2 collective-permute-done.4
  26.1 1.1 %collective-permute-done.5 = bf16[64,256]{1,0:T(8,128)(2,1)S(1)} collective-permute-done((bf16[64,256]{1,0:T(8,128)(2,1)S(1)}, bf16[64,256]{1,0:T(8,128)(2,1)S(1)}, u32[]{:S(2)}, u32[]{:S(2)}) %collective-permute-start.5) | collective-permute-done | bytes 32800 | tf_op jit(solution)/shard_map/ppermute | solution.py:422
  27.2 0.7 %add_bitcast_fusion = f32[256,64]{0,1:T(8,128)} fusion(bf16[64,256]{1,0:T(8,128)(2,1)S(1)} %collective-permute-done.5, bf16[64,256]{1,0:T(8,128)(2,1)S(1)} %collective-permute-done.4, bf16[64,256]{1,0:T(8,128)(2,1)S(1)} %collective-permute-done.3, f32[64,256]{1,0:T(8,128)S(1)} %own_last.1, bf16[64,2048]{1,0:T(8,128)(2,1)S(1)} %copy-done), kind=kLoop, calls=%fused_computation | loop fusion | flops 147456 | bytes 262144 | tf_op jit(solution)/shard_map/transpose | solution.py:519
Async XLA Ops:
  0.0 3.6 %collective-permute-start = (bf16[64,2048]{1,0:T(8,128)(2,1)}, bf16[64,2048]{1,0:T(8,128)(2,1)S(1)}, u32[]{:S(2)}, u32[]{:S(2)}) collective-permute-start(bf16[64,2048]{1,0:T(8,128)(2,1)} %refs_3_.2), channel_id=1, source_target_pairs={{0,1},{1,0},{2,3},{3,2},{4,5},{5,4},{6,7},{7,6},{8,9},{9,8},{10,11... | collective-permute-start | bytes 786440 | tf_op jit(solution)/shard_map/ppermute | solution.py:422
  0.5 11.1 %collective-permute-start.1 = (bf16[64,2048]{1,0:T(8,128)(2,1)}, bf16[64,2048]{1,0:T(8,128)(2,1)S(1)}, u32[]{:S(2)}, u32[]{:S(2)}) collective-permute-start(bf16[64,2048]{1,0:T(8,128)(2,1)} %refs_3_.2), channel_id=1, source_target_pairs={{0,2},{1,3},{2,0},{3,1},{4,6},{5,7},{6,4},{7,5},{8,10},{9,11},{10,... | collective-permute-start | bytes 786440 | tf_op jit(solution)/shard_map/ppermute | solution.py:422
  3.6 8.2 %copy-start = (bf16[64,2048]{1,0:T(8,128)(2,1)S(1)}, bf16[64,2048]{1,0:T(8,128)(2,1)}, u32[]{:S(2)}) copy-start(bf16[64,2048]{1,0:T(8,128)(2,1)} %refs_3_.2) | copy-start | bytes 786436
  11.5 2.1 %collective-permute-start.2 = (bf16[64,2048]{1,0:T(8,128)(2,1)S(1)}, bf16[64,2048]{1,0:T(8,128)(2,1)S(1)}, u32[]{:S(2)}, u32[]{:S(2)}) collective-permute-start(bf16[64,2048]{1,0:T(8,128)(2,1)S(1)} %collective-permute-done.1.refs_5_.refs_3_), channel_id=1, source_target_pairs={{0,1},{1,0},{2,3},{3,2},{4,5},{5,4},{6,7},{7,6},{8,9},{9,8},{10,11... | collective-permute-start | bytes 786440 | tf_op jit(solution)/shard_map/ppermute | solution.py:422
  17.6 8.3 %collective-permute-start.3 = (bf16[64,256]{1,0:T(8,128)(2,1)S(1)}, bf16[64,256]{1,0:T(8,128)(2,1)S(1)}, u32[]{:S(2)}, u32[]{:S(2)}) collective-permute-start(bf16[64,256]{1,0:T(8,128)(2,1)S(1)} %get-tuple-element.33), channel_id=1, source_target_pairs={{0,12},{1,13},{2,14},{3,15},{4,8},{5,9},{6,10},{7,11},{8,4},{9,5},... | collective-permute-start | bytes 98312 | tf_op jit(solution)/shard_map/ppermute | solution.py:422
  21.3 4.8 %collective-permute-start.4 = (bf16[64,256]{1,0:T(8,128)(2,1)S(1)}, bf16[64,256]{1,0:T(8,128)(2,1)S(1)}, u32[]{:S(2)}, u32[]{:S(2)}) collective-permute-start(bf16[64,256]{1,0:T(8,128)(2,1)S(1)} %get-tuple-element.34), channel_id=1, source_target_pairs={{0,8},{1,9},{2,10},{3,11},{4,12},{5,13},{6,14},{7,15},{8,0},{9,1},... | collective-permute-start | bytes 98312 | tf_op jit(solution)/shard_map/ppermute | solution.py:422
  23.3 4.0 %collective-permute-start.5 = (bf16[64,256]{1,0:T(8,128)(2,1)S(1)}, bf16[64,256]{1,0:T(8,128)(2,1)S(1)}, u32[]{:S(2)}, u32[]{:S(2)}) collective-permute-start(bf16[64,256]{1,0:T(8,128)(2,1)S(1)} %late_targets.1), channel_id=1, source_target_pairs={{0,4},{1,5},{2,6},{3,7},{4,0},{5,1},{6,2},{7,3},{8,12},{9,13},{10,... | collective-permute-start | bytes 98312 | tf_op jit(solution)/shard_map/ppermute | solution.py:422

commit v7 on v6

--- a/solution.py
+++ b/solution.py
@@ -225,12 +225,25 @@
     return jnp.dot(density, tile, preferred_element_type=F32)
 
 
-def far_steps(
-    corners_ref, density_refs, target_ref, total_ref, dist_ref, flux_ref, geometry, stage_ref
+def chunk_features(corners, geometry, stage_ref):
+    blocks = [
+        source_features(
+            corners[:, k * BLOCK : (k + 1) * BLOCK],
+            geometry,
+            (stage_ref.at[2 * k], stage_ref.at[2 * k + 1]),
+        )
+        for k in range(corners.shape[1] // BLOCK)
+    ]
+    return [jnp.concatenate([block[k] for block in blocks], axis=1) for k in range(2)]
+
+
+def source_steps(
+    corners_ref, first, density_refs, target_ref, total_ref, ready_refs, kept_refs, next_refs,
+    geometry, stage_ref,
 ):
-    src_total = corners_ref.shape[1]
     src_dev = density_refs[0].shape[1]
-    tgt_total = target_ref.shape[1]
+    src_total = src_dev * len(density_refs)
+    tgt_total = total_ref.shape[1]
     chunk = min(CHUNK, src_dev)
     steps = src_total // chunk
     tgt_step = max(
@@ -239,20 +252,8 @@
     tgt_steps = tgt_total // tgt_step
 
     def make(turn):
-        here = pl.ds(turn * chunk, chunk)
-        corners = corners_ref[:, here]
-        blocks = [
-            source_features(
-                corners[:, k * BLOCK : (k + 1) * BLOCK],
-                geometry,
-                (stage_ref.at[2 * k], stage_ref.at[2 * k + 1]),
-            )
-            for k in range(chunk // BLOCK)
-        ]
-        dist, flux = [jnp.concatenate([block[k] for block in blocks], axis=1) for k in range(2)]
-        dist_ref[:, here] = dist
-        flux_ref[:, here] = flux
-        return dist, flux
+        start = first * src_dev + turn * chunk
+        return chunk_features(corners_ref[:, start : start + chunk], geometry, stage_ref)
 
     def apply(turn, dist, flux):
         here = pl.ds(turn * chunk, chunk)
@@ -268,11 +269,15 @@
         else:
             pl.loop(0, tgt_steps)(some)
 
-    kept = make(0)
+    kept = [ref[...] for ref in ready_refs] if ready_refs else make(0)
     for turn in range(steps):
-        following = make(turn + 1) if turn + 1 < steps else None
+        for ref, values in zip(kept_refs, kept):
+            ref[:, turn * chunk : (turn + 1) * chunk] = values
+        following = make(turn + 1) if turn + 1 < steps or next_refs else None
         apply(turn, *kept)
         kept = following
+    for ref, values in zip(next_refs, kept or ()):
+        ref[...] = values
 
 
 def partner(own, k, groups):
@@ -292,41 +297,30 @@
     return copies
 
 
-def first_kernel(near, row_total, group, sizes, sample_ref, *refs):
-    small_refs, connectivity_ref, density_refs, refs = refs[:5], refs[5], refs[6 : 6 + near], refs[6 + near :]
-    (table_ref, origin_ref, *tgt_refs, dist_ref, flux_ref, rest_ref), refs = refs[:10], refs[10:]
-    feature_refs, part_refs = tgt_refs[:3], tgt_refs[3:]
-    small, (src_corners, tgt_corners, held_ref, stage_ref, far_ref, total_ref, small_sems, src_sems, rest_sems, tgt_sems, density_sem) = (
-        refs[:5], refs[5:],
-    )
+def prepare_kernel(row_total, group, sizes, sample_ref, *refs):
+    small_refs, connectivity_ref, refs = refs[:5], refs[5], refs[6:]
+    (table_ref, origin_ref, far_ref, own_ref, src_corners), refs = refs[:5], refs[5:]
+    small, (tgt_corners, tgt_stage_ref, stage_ref, small_sems, src_sems, tgt_sems) = refs[:5], refs[5:]
     lattice_ref, modes_ref, polar_ref, azim_ref, angles_ref = small
     pitch, first_cos, cycle_count = sizes
-    src_dev = src_corners.shape[1] // near
+    src_dev = src_corners.shape[1] // group
     groups = row_total // group
     row = lax.axis_index("row")
     own_group = row // group
     place = row % group
-    first_copies = []
+    small_copies = []
     for k in range(5):
-        first_copies.append(pltpu.make_async_copy(small_refs[k], small[k], small_sems.at[k]))
-        first_copies[k].start()
-    copies = start_corners(
+        small_copies.append(pltpu.make_async_copy(small_refs[k], small[k], small_sems.at[k]))
+        small_copies[k].start()
+    tgt_copies = start_corners(
         connectivity_ref, tgt_corners, tgt_sems,
         [(partner(own_group, k + 1, groups) * group + place) * src_dev for k in range(groups)], BAND_DEV,
     )
-    copies += start_corners(
+    src_copies = start_corners(
         connectivity_ref, src_corners, src_sems,
-        [(own_group * group + (place ^ k)) * src_dev for k in range(near)], src_dev,
-    )
-    held_copy = pltpu.make_async_copy(density_refs[0], held_ref, density_sem)
-    held_copy.start()
-    copies.append(held_copy)
-    rest_copies = start_corners(
-        connectivity_ref, rest_ref, rest_sems,
-        [(own_group * group + (place ^ k)) * src_dev for k in range(near, group)], src_dev,
-    )
-
-    for copy in first_copies:
+        [(own_group * group + (place ^ k)) * src_dev for k in range(group)], src_dev,
+    )
+    for copy in small_copies:
         copy.wait()
     radius = radius_table(
         sample_ref[0], lattice_ref[...], modes_ref[...], polar_ref[...], azim_ref[...], pitch
@@ -337,62 +331,51 @@
     for k, level in enumerate(levels):
         origin_ref[rows + k : rows + k + 1] = jnp.broadcast_to(level, (1, 128))
     table_ref[...] = radius
-    for copy in copies:
+    for copy in tgt_copies + src_copies:
         copy.wait()
-
     geometry = (table_ref, angles_ref, cycle_count, levels)
     found = [
-        target_features(tgt_corners[:, first : first + BLOCK], geometry, stage_ref.at[0])
+        target_features(tgt_corners[:, first : first + BLOCK], geometry, tgt_stage_ref)
         for first in range(0, tgt_corners.shape[1], BLOCK)
     ]
     found = jnp.concatenate(found, axis=1)
     far_ref[...] = found[:, :-BAND_DEV]
-    first = 0
-    for ref in feature_refs:
-        ref[...] = found[:, first : first + ref.shape[1]]
-        first += ref.shape[1]
-    total_ref[...] = jnp.zeros_like(total_ref)
-    far_steps(
-        src_corners,
-        (held_ref, *density_refs[1:]),
-        far_ref, total_ref, dist_ref, flux_ref, geometry, stage_ref,
-    )
-    first = 0
-    for ref in part_refs:
-        ref[...] = total_ref[:, first : first + ref.shape[1]]
-        first += ref.shape[1]
-    for copy in rest_copies:
-        copy.wait()
-
-
-def second_kernel(
-    near, group, cycle_count, corners_ref, table_ref, origin_ref, far_ref, part_ref, *refs
-):
-    rest = group - near
-    density_refs, refs = refs[:rest], refs[rest:]
-    (*sums_refs, dist_ref, flux_ref, total_ref, stage_ref) = refs
+    own_ref[...] = found[:, -BAND_DEV:]
+
+
+def sources_kernel(first, count, cycle_count, corners_ref, table_ref, origin_ref, far_ref, *refs):
+    ready_refs, refs = (refs[:2], refs[2:]) if first else ((), refs)
+    part_refs, refs = (refs[:1], refs[1:]) if first else ((), refs)
+    density_refs, (*sums_refs, total_ref, stage_ref) = refs[:count], refs[count:]
+    sums_refs, next_refs = (sums_refs, ()) if first else (sums_refs[:-2], sums_refs[-2:])
+    sums_refs, kept_refs = sums_refs[:-2], sums_refs[-2:]
     rows = origin_ref.shape[0] - 8
     levels = [origin_ref[rows + k : rows + k + 1, 0:1] for k in range(6)]
     geometry = (table_ref, origin_ref, cycle_count, levels)
-    total_ref[...] = part_ref[...]
-    far_steps(
-        corners_ref, density_refs, far_ref, total_ref, dist_ref, flux_ref, geometry, stage_ref
-    )
+    if part_refs:
+        total_ref[...] = part_refs[0][:, : total_ref.shape[1]]
+    else:
+        total_ref[...] = jnp.zeros_like(total_ref)
+    source_steps(
+        corners_ref, first, density_refs, far_ref, total_ref, ready_refs, kept_refs, next_refs,
+        geometry, stage_ref,
+    )
+    width = sums_refs[0].shape[1]
     for k, ref in enumerate(sums_refs):
-        ref[...] = total_ref[:, k * BAND_DEV : (k + 1) * BAND_DEV].astype(BF16)
+        ref[...] = total_ref[:, k * width : (k + 1) * width].astype(ref.dtype)
 
 
 def kept_kernel(own, count, dist_ref, flux_ref, target_ref, *refs):
     density_refs, (*part_refs, sums_ref) = refs[:count], refs[count:]
     src_dev = density_refs[0].shape[1]
-    target = target_ref[...]
+    target = target_ref[:, -BAND_DEV:]
     apart = None
     if own:
         diagonal = lax.broadcasted_iota(
             jnp.int32, (BAND_DEV, BAND_DEV), 0
         ) == lax.broadcasted_iota(jnp.int32, (BAND_DEV, BAND_DEV), 1)
         apart = jnp.where(diagonal, 1e30, 0.0)
-    total = part_refs[0][...] if part_refs else None
+    total = part_refs[0][:, -BAND_DEV:] if part_refs else None
     step = KEPT_STEP
     for first in range(0, count * src_dev, step):
         here = slice(first, first + step)
@@ -436,65 +419,55 @@
 
     small = [lattice_vector.reshape(1, -1), mode_table, *map(jnp.asarray, tables)]
     stage = pltpu.VMEM((2 * min(CHUNK, src_dev) // BLOCK, 8 * FEATS, 128), F32)
-    early = far_total - BAND_DEV
-    table, origins, tgt_early, tgt_late, tgt_own, part_early, part_late, *near_features, corners = (
-        pl.pallas_call(
-            lambda *refs: first_kernel(near, row_total, group, sizes, *refs),
-            out_shape=[
-                shape(pitch, NPH, dtype=F32),
-                shape(tables[2].shape[0] + 8, 128, dtype=F32),
-                shape(FEATS, early),
-                shape(FEATS, BAND_DEV),
-                shape(FEATS, BAND_DEV),
-                shape(columns, early, dtype=F32),
-                shape(columns, BAND_DEV, dtype=F32),
-                shape(FEATS, near * src_dev),
-                shape(FEATS, near * src_dev),
-                shape(3, (group - near) * src_dev, dtype=jnp.int32),
-            ],
-            in_specs=[pl.BlockSpec(memory_space=pltpu.SMEM)] + [hbm] * 7 + [vmem] * (near - 1),
-            out_specs=[vmem] * 10,
-            scratch_shapes=[pltpu.VMEM(array.shape, array.dtype) for array in small]
-            + [
-                pltpu.VMEM((3, near * src_dev), jnp.int32),
-                pltpu.VMEM((3, groups * BAND_DEV), jnp.int32),
-                pltpu.VMEM((columns, src_dev), BF16),
-                stage,
-                pltpu.VMEM((FEATS, far_total), BF16),
-                pltpu.VMEM((columns, far_total), F32),
-                pltpu.SemaphoreType.DMA((5,)),
-                pltpu.SemaphoreType.DMA((near,)),
-                pltpu.SemaphoreType.DMA((group - near,)),
-                pltpu.SemaphoreType.DMA((groups,)),
-                pltpu.SemaphoreType.DMA,
-            ],
-            compiler_params=params,
-            cost_estimate=cost(near * src_dev, far_total),
-            name="near_sources",
-        )(
-            sample_index,
-            *[in_hbm(array) for array in (*small, connectivity, density)],
-            *densities[1:near],
-        )
-    )
-
-    relay, origins = lax.optimization_barrier((densities[2], origins))
-    densities.append(moved(relay, lambda r: r ^ 1))
-    rest = group - near
-    *sums, dist_rest, flux_rest = pl.pallas_call(
-        lambda *refs: second_kernel(near, group, cycle_count, *refs),
-        out_shape=[shape(columns, BAND_DEV)] * (groups - 2)
-        + [shape(FEATS, rest * src_dev)] * 2,
-        in_specs=[vmem] * (5 + rest),
-        out_specs=[vmem] * groups,
-        scratch_shapes=[
-            pltpu.VMEM((columns, early), F32),
+    ready_shapes = [shape(FEATS, min(CHUNK, src_dev))] * 2
+    table, origins, tgt_far, tgt_own, corners = pl.pallas_call(
+        lambda *refs: prepare_kernel(row_total, group, sizes, *refs),
+        out_shape=[
+            shape(pitch, NPH, dtype=F32),
+            shape(tables[2].shape[0] + 8, 128, dtype=F32),
+            shape(FEATS, far_total),
+            shape(FEATS, BAND_DEV),
+            shape(3, group * src_dev, dtype=jnp.int32),
+        ],
+        in_specs=[pl.BlockSpec(memory_space=pltpu.SMEM)] + [hbm] * 6,
+        out_specs=[vmem] * 5,
+        scratch_shapes=[pltpu.VMEM(array.shape, array.dtype) for array in small]
+        + [
+            pltpu.VMEM((3, groups * BAND_DEV), jnp.int32),
+            pltpu.VMEM((8 * FEATS, 128), F32),
             stage,
+            pltpu.SemaphoreType.DMA((5,)),
+            pltpu.SemaphoreType.DMA((group,)),
+            pltpu.SemaphoreType.DMA((groups,)),
         ],
         compiler_params=params,
-        cost_estimate=cost(rest * src_dev, early),
-        name="other_sources",
-    )(corners, table, origins, tgt_early, part_early, *densities[near:])
+        cost_estimate=cost(1024, 256),
+        name="prepare",
+    )(sample_index, *[in_hbm(array) for array in (*small, connectivity)])
+
+    def sources(first, blocks, ready, part, total, sums):
+        handed_on = [] if first else ready_shapes
+        *sums, dist, flux = pl.pallas_call(
+            lambda *refs: sources_kernel(first, len(blocks), cycle_count, *refs),
+            out_shape=sums + [shape(FEATS, len(blocks) * src_dev)] * 2 + handed_on,
+            in_specs=[vmem] * (4 + len(ready) + len(part) + len(blocks)),
+            out_specs=[vmem] * (len(sums) + 2 + len(handed_on)),
+            scratch_shapes=[pltpu.VMEM((columns, total), F32), stage],
+            compiler_params=params,
+            cost_estimate=cost(len(blocks) * src_dev, total),
+            name="other_sources" if first else "near_sources",
+        )(corners, table, origins, tgt_far, *ready, *part, *blocks)
+        return sums, (dist, flux)
+
+    early = far_total - BAND_DEV
+    (part, *near_features), ready = sources(
+        0, densities[:near], [], [], far_total, [shape(columns, far_total, dtype=F32)]
+    )
+    relay, part = lax.optimization_barrier((densities[2], part))
+    densities.append(moved(relay, lambda r: r ^ 1))
+    sums, rest_features = sources(
+        near, densities[near:], ready, [part], early, [shape(columns, BAND_DEV)] * (groups - 2)
+    )
 
     def kept(features, target, blocks, own, part, dtype=F32):
         return pl.pallas_call(
@@ -507,9 +480,8 @@
             name="own_first" if own else "late_targets" if dtype == BF16 else "own_last",
         )(*features, target, *blocks, *part)
 
-    rest_features = (dist_rest, flux_rest)
     own_sums = kept(near_features, tgt_own, densities[:near], True, [])
-    sums.append(kept(rest_features, tgt_late, densities[near:], False, [part_late], BF16))
+    sums.append(kept(rest_features, tgt_far, densities[near:], False, [part], BF16))
     own_sums = kept(rest_features, tgt_own, densities[near:], False, [own_sums])
     total = 0.5 * density[:, :BAND_DEV].astype(F32) + own_sums
     for k, block in enumerate(sums):

time: 28.1 us -> 27.5 us (0.979)
  Pallas kernels: 17.4 us -> 16.8 us
    pallas_call x2 -> x3, Pallas kernels: 11.9 us -> 11.5 us  [the longest x2 9.11 us: sources(): pl.pallas_call(lambda *refs: sources_kernel(first, len(blocks), cycle_cou...]
where the time goes in v7:
time: 27.5 us; the launch traced here: 27.4 us
  Pallas kernels  16.8 us (61%)
  starting transfers between devices  7.79 us (28%)
  waiting for transfers between devices  1.36 us (5%)
  between operations  0.74 us (3%)
  other arithmetic  0.65 us (2%)
    pallas_call x2, Pallas kernels, sources(): pl.pallas_call(lambda *refs: sources_kernel(first, len(blocks), cycle_cou...  9.11 us
    ppermute x6, starting transfers between devices, moved(): lax.ppermute(array, 'row', [(r, target_of(r)) for r in range(row_total)])  7.79 us
    pallas_call x3, Pallas kernels, kept(): pl.pallas_call(lambda *refs: kept_kernel(own, len(blocks), *refs), out_sh...  5.27 us
    pallas_call x1, Pallas kernels, per_device(): pl.pallas_call(lambda *refs: prepare_kernel(row_total, group, sizes, *ref...  2.44 us
    ppermute x6, waiting for transfers between devices, moved(): lax.ppermute(array, 'row', [(r, target_of(r)) for r in range(row_total)])  1.36 us
    transpose x1, other arithmetic, per_device(): return total.T  0.65 us
  transfers between devices with their start and end apart: 6, of which 2 were waited for; matrix products, arithmetic and copies ran while one was open for 0% of the time, Pallas kernels for 48%

profile of v7, /device:TPU:0, one launch (start us, length us, event | category | flops | bytes accessed | tf_op | source)
XLA Modules:
  0.0 27.4 jit_solution(6180651118830010164)
XLA Ops:
  0.0 0.5 %collective-permute-start = (bf16[64,2048]{1,0:T(8,128)(2,1)}, bf16[64,2048]{1,0:T(8,128)(2,1)S(1)}, u32[]{:S(2)}, u32[]{:S(2)}) collective-permute-start(bf16[64,2048]{1,0:T(8,128)(2,1)} %refs_3_.2), channel_id=1, source_target_pairs={{0,1},{1,0},{2,3},{3,2},{4,5},{5,4},{6,7},{7,6},{8,9},{9,8},{10,11... | collective-permute-start | bytes 786440 | tf_op jit(solution)/shard_map/ppermute | solution.py:405
  0.5 2.5 %collective-permute-start.1 = (bf16[64,2048]{1,0:T(8,128)(2,1)}, bf16[64,2048]{1,0:T(8,128)(2,1)S(1)}, u32[]{:S(2)}, u32[]{:S(2)}) collective-permute-start(bf16[64,2048]{1,0:T(8,128)(2,1)} %refs_3_.2), channel_id=1, source_target_pairs={{0,2},{1,3},{2,0},{3,1},{4,6},{5,7},{6,4},{7,5},{8,10},{9,11},{10,... | collective-permute-start | bytes 786440 | tf_op jit(solution)/shard_map/ppermute | solution.py:405
  3.6 0.0 copy-start
  3.6 2.4 %prepare.1 = (f32[72,256]{1,0:T(8,128)S(1)}, f32[16,128]{1,0:T(8,128)S(1)}, bf16[64,768]{1,0:T(8,128)(2,1)S(1)}, bf16[64,256]{1,0:T(8,128)(2,1)S(1)}, s32[3,8192]{1,0:T(4,128)S(1)}) custom-call(s32[1]{0:T(128)S(6)} %copy.9.refs_0_, s32[1,1024]{1,0:T(1,128)} %bitcast.3, s32[2,1024]{1,0:T(2,128)} %refs_2_.1, f32[144,32]{1,0:T(8,128)} %constant.8.clone.refs_3_, ...), custom_call_target="tpu_custom_call" | custom-call | flops 402653184 | bytes 1048576 | tf_op jit(solution)/shard_map/prepare/pallas_call | solution.py:423
  6.1 0.0 collective-permute-done.refs_5_.refs_4_
  6.1 0.0 copy-done
  6.1 5.5 %near_sources.1 = (f32[64,768]{1,0:T(8,128)S(1)}, bf16[64,4096]{1,0:T(8,128)(2,1)S(1)}, bf16[64,4096]{1,0:T(8,128)(2,1)S(1)}, bf16[64,1024]{1,0:T(8,128)(2,1)S(1)}, bf16[64,1024]{1,0:T(8,128)(2,1)S(1)}) custom-call(s32[3,8192]{1,0:T(4,128)S(1)} %get-tuple-element.21.refs_0_, f32[72,256]{1,0:T(8,128)S(1)} %get-tuple-element.22.refs_1_, ...), custom_call_target="tpu_custom_call" | custom-call | flops 4831838208 | bytes 1048576 | tf_op jit(solution)/shard_map/near_sources/pallas_call | solution.py:450
  11.6 0.0 collective-permute-done.1.refs_7_.refs_3_
  11.6 0.3 %collective-permute-start.2 = (bf16[64,2048]{1,0:T(8,128)(2,1)S(1)}, bf16[64,2048]{1,0:T(8,128)(2,1)S(1)}, u32[]{:S(2)}, u32[]{:S(2)}) collective-permute-start(bf16[64,2048]{1,0:T(8,128)(2,1)S(1)} %collective-permute-done.1.refs_7_.refs_3_), channel_id=1, source_target_pairs={{0,1},{1,0},{2,3},{3,2},{4,5},{5,4},{6,7},{7,6},{8,9},{9,8},{10,11... | collective-permute-start | bytes 786440 | tf_op jit(solution)/shard_map/ppermute | solution.py:405
  11.9 1.7 %own_first.1.refs_5_ = f32[64,256]{1,0:T(8,128)S(1)} custom-call(bf16[64,4096]{1,0:T(8,128)(2,1)S(1)} %get-tuple-element.33.refs_0_, bf16[64,4096]{1,0:T(8,128)(2,1)S(1)} %get-tuple-element.34.refs_1_, bf16[64,256]{1,0:T(8,128)(2,1)S(1)} %get-tuple-element.32.refs_2_, bf16[64,2048]{1,0:T(8,128)(2,1)S(1)} %copy-done, ...), custom_call_target="tpu_custom_call" | custom-call | flops 1610612736 | bytes 1048576 | tf_op jit(solution)/shard_map/own_first/pallas_call | solution.py:473
  13.7 0.0 collective-permute-done.2.refs_8_.refs_4_
  13.7 3.6 %other_sources.1 = (bf16[64,256]{1,0:T(8,128)(2,1)S(1)}, bf16[64,256]{1,0:T(8,128)(2,1)S(1)}, bf16[64,4096]{1,0:T(8,128)(2,1)S(1)}, bf16[64,4096]{1,0:T(8,128)(2,1)S(1)}) custom-call(s32[3,8192]{1,0:T(4,128)S(1)} %get-tuple-element.21.refs_0_, f32[72,256]{1,0:T(8,128)S(1)} %get-tuple-element.22.refs_1_, f32[16,128]{1,0:T(8,128)S(1)} %get-tuple-element.23.refs_2_, ...), custom_call_target="tpu_custom_call" | custom-call | flops 3221225472 | bytes 1048576 | tf_op jit(solution)/shard_map/other_sources/pallas_call | solution.py:450
  17.3 3.7 %collective-permute-start.3 = (bf16[64,256]{1,0:T(8,128)(2,1)S(1)}, bf16[64,256]{1,0:T(8,128)(2,1)S(1)}, u32[]{:S(2)}, u32[]{:S(2)}) collective-permute-start(bf16[64,256]{1,0:T(8,128)(2,1)S(1)} %get-tuple-element.35), channel_id=1, source_target_pairs={{0,12},{1,13},{2,14},{3,15},{4,8},{5,9},{6,10},{7,11},{8,4},{9,5},... | collective-permute-start | bytes 98312 | tf_op jit(solution)/shard_map/ppermute | solution.py:405
  21.0 0.0 collective-permute-start.4
  21.0 1.8 %late_targets.1 = bf16[64,256]{1,0:T(8,128)(2,1)S(1)} custom-call(bf16[64,4096]{1,0:T(8,128)(2,1)S(1)} %get-tuple-element.30.refs_0_, bf16[64,4096]{1,0:T(8,128)(2,1)S(1)} %get-tuple-element.31.refs_1_, bf16[64,768]{1,0:T(8,128)(2,1)S(1)} %get-tuple-element.24.refs_3_.refs_2_, bf16[64,2048]{1,0:T(8,128)(2,1)S(1)} %collective-permute-done.1.refs_7_.refs_3_, ...), custom_call_target="tpu_custom_call" | custom-call | flops 1610612736 | bytes 1048576 | tf_op jit(solution)/shard_map/late_targets/pallas_call | solution.py:473
  22.7 0.8 %collective-permute-start.5 = (bf16[64,256]{1,0:T(8,128)(2,1)S(1)}, bf16[64,256]{1,0:T(8,128)(2,1)S(1)}, u32[]{:S(2)}, u32[]{:S(2)}) collective-permute-start(bf16[64,256]{1,0:T(8,128)(2,1)S(1)} %late_targets.1), channel_id=1, source_target_pairs={{0,4},{1,5},{2,6},{3,7},{4,0},{5,1},{6,2},{7,3},{8,12},{9,13},{10,... | collective-permute-start | bytes 98312 | tf_op jit(solution)/shard_map/ppermute | solution.py:405
  23.6 1.8 %own_last.1 = f32[64,256]{1,0:T(8,128)S(1)} custom-call(bf16[64,4096]{1,0:T(8,128)(2,1)S(1)} %get-tuple-element.30.refs_0_, bf16[64,4096]{1,0:T(8,128)(2,1)S(1)} %get-tuple-element.31.refs_1_, bf16[64,256]{1,0:T(8,128)(2,1)S(1)} %get-tuple-element.32.refs_2_, bf16[64,2048]{1,0:T(8,128)(2,1)S(1)} %collective-permute-done.1.refs_7_.refs_3_, ...), custom_call_target="tpu_custom_call" | custom-call | flops 1610612736 | bytes 1048576 | tf_op jit(solution)/shard_map/own_last/pallas_call | solution.py:473
  25.4 0.0 collective-permute-done.3
  25.4 0.5 %collective-permute-done.4 = bf16[64,256]{1,0:T(8,128)(2,1)S(1)} collective-permute-done((bf16[64,256]{1,0:T(8,128)(2,1)S(1)}, bf16[64,256]{1,0:T(8,128)(2,1)S(1)}, u32[]{:S(2)}, u32[]{:S(2)}) %collective-permute-start.4) | collective-permute-done | bytes 32800 | tf_op jit(solution)/shard_map/ppermute | solution.py:405
  25.9 0.8 %collective-permute-done.5 = bf16[64,256]{1,0:T(8,128)(2,1)S(1)} collective-permute-done((bf16[64,256]{1,0:T(8,128)(2,1)S(1)}, bf16[64,256]{1,0:T(8,128)(2,1)S(1)}, u32[]{:S(2)}, u32[]{:S(2)}) %collective-permute-start.5) | collective-permute-done | bytes 32800 | tf_op jit(solution)/shard_map/ppermute | solution.py:405
  26.7 0.7 %add_bitcast_fusion = f32[256,64]{0,1:T(8,128)} fusion(bf16[64,256]{1,0:T(8,128)(2,1)S(1)} %collective-permute-done.5, bf16[64,256]{1,0:T(8,128)(2,1)S(1)} %collective-permute-done.4, bf16[64,256]{1,0:T(8,128)(2,1)S(1)} %collective-permute-done.3, f32[64,256]{1,0:T(8,128)S(1)} %own_last.1, bf16[64,2048]{1,0:T(8,128)(2,1)S(1)} %copy-done), kind=kLoop, calls=%fused_computation | loop fusion | flops 147456 | bytes 262144 | tf_op jit(solution)/shard_map/transpose | solution.py:491
Async XLA Ops:
  0.0 6.1 %collective-permute-start = (bf16[64,2048]{1,0:T(8,128)(2,1)}, bf16[64,2048]{1,0:T(8,128)(2,1)S(1)}, u32[]{:S(2)}, u32[]{:S(2)}) collective-permute-start(bf16[64,2048]{1,0:T(8,128)(2,1)} %refs_3_.2), channel_id=1, source_target_pairs={{0,1},{1,0},{2,3},{3,2},{4,5},{5,4},{6,7},{7,6},{8,9},{9,8},{10,11... | collective-permute-start | bytes 786440 | tf_op jit(solution)/shard_map/ppermute | solution.py:405
  0.5 11.2 %collective-permute-start.1 = (bf16[64,2048]{1,0:T(8,128)(2,1)}, bf16[64,2048]{1,0:T(8,128)(2,1)S(1)}, u32[]{:S(2)}, u32[]{:S(2)}) collective-permute-start(bf16[64,2048]{1,0:T(8,128)(2,1)} %refs_3_.2), channel_id=1, source_target_pairs={{0,2},{1,3},{2,0},{3,1},{4,6},{5,7},{6,4},{7,5},{8,10},{9,11},{10,... | collective-permute-start | bytes 786440 | tf_op jit(solution)/shard_map/ppermute | solution.py:405
  3.6 2.5 %copy-start = (bf16[64,2048]{1,0:T(8,128)(2,1)S(1)}, bf16[64,2048]{1,0:T(8,128)(2,1)}, u32[]{:S(2)}) copy-start(bf16[64,2048]{1,0:T(8,128)(2,1)} %refs_3_.2) | copy-start | bytes 786436
  11.6 2.1 %collective-permute-start.2 = (bf16[64,2048]{1,0:T(8,128)(2,1)S(1)}, bf16[64,2048]{1,0:T(8,128)(2,1)S(1)}, u32[]{:S(2)}, u32[]{:S(2)}) collective-permute-start(bf16[64,2048]{1,0:T(8,128)(2,1)S(1)} %collective-permute-done.1.refs_7_.refs_3_), channel_id=1, source_target_pairs={{0,1},{1,0},{2,3},{3,2},{4,5},{5,4},{6,7},{7,6},{8,9},{9,8},{10,11... | collective-permute-start | bytes 786440 | tf_op jit(solution)/shard_map/ppermute | solution.py:405
  17.3 8.1 %collective-permute-start.3 = (bf16[64,256]{1,0:T(8,128)(2,1)S(1)}, bf16[64,256]{1,0:T(8,128)(2,1)S(1)}, u32[]{:S(2)}, u32[]{:S(2)}) collective-permute-start(bf16[64,256]{1,0:T(8,128)(2,1)S(1)} %get-tuple-element.35), channel_id=1, source_target_pairs={{0,12},{1,13},{2,14},{3,15},{4,8},{5,9},{6,10},{7,11},{8,4},{9,5},... | collective-permute-start | bytes 98312 | tf_op jit(solution)/shard_map/ppermute | solution.py:405
  21.0 4.9 %collective-permute-start.4 = (bf16[64,256]{1,0:T(8,128)(2,1)S(1)}, bf16[64,256]{1,0:T(8,128)(2,1)S(1)}, u32[]{:S(2)}, u32[]{:S(2)}) collective-permute-start(bf16[64,256]{1,0:T(8,128)(2,1)S(1)} %get-tuple-element.36), channel_id=1, source_target_pairs={{0,8},{1,9},{2,10},{3,11},{4,12},{5,13},{6,14},{7,15},{8,0},{9,1},... | collective-permute-start | bytes 98312 | tf_op jit(solution)/shard_map/ppermute | solution.py:405
  22.7 4.0 %collective-permute-start.5 = (bf16[64,256]{1,0:T(8,128)(2,1)S(1)}, bf16[64,256]{1,0:T(8,128)(2,1)S(1)}, u32[]{:S(2)}, u32[]{:S(2)}) collective-permute-start(bf16[64,256]{1,0:T(8,128)(2,1)S(1)} %late_targets.1), channel_id=1, source_target_pairs={{0,4},{1,5},{2,6},{3,7},{4,0},{5,1},{6,2},{7,3},{8,12},{9,13},{10,... | collective-permute-start | bytes 98312 | tf_op jit(solution)/shard_map/ppermute | solution.py:405

commit v8 on v7

--- a/solution.py
+++ b/solution.py
@@ -17,7 +17,7 @@
 CHUNK = 1024
 TGT_STEP = 768
 KEPT_STEP = 1024
-VMEM = 30 << 20
+VMEM = 40 << 20
 F32 = jnp.float32
 BF16 = jnp.bfloat16
 
@@ -273,8 +273,8 @@
     for turn in range(steps):
         for ref, values in zip(kept_refs, kept):
             ref[:, turn * chunk : (turn + 1) * chunk] = values
+        apply(turn, *kept)
         following = make(turn + 1) if turn + 1 < steps or next_refs else None
-        apply(turn, *kept)
         kept = following
     for ref, values in zip(next_refs, kept or ()):
         ref[...] = values

time: 27.5 us -> 27.5 us (level)
  no operation moved by 1% of the time
where the time goes in v8:
time: 27.5 us; the launch traced here: 27.4 us
  Pallas kernels  16.8 us (61%)
  starting transfers between devices  7.78 us (28%)
  waiting for transfers between devices  1.37 us (5%)
  between operations  0.74 us (3%)
  other arithmetic  0.65 us (2%)
    pallas_call x2, Pallas kernels, sources(): pl.pallas_call(lambda *refs: sources_kernel(first, len(blocks), cycle_cou...  9.13 us
    ppermute x6, starting transfers between devices, moved(): lax.ppermute(array, 'row', [(r, target_of(r)) for r in range(row_total)])  7.78 us
    pallas_call x3, Pallas kernels, kept(): pl.pallas_call(lambda *refs: kept_kernel(own, len(blocks), *refs), out_sh...  5.26 us
    pallas_call x1, Pallas kernels, per_device(): pl.pallas_call(lambda *refs: prepare_kernel(row_total, group, sizes, *ref...  2.44 us
    ppermute x6, waiting for transfers between devices, moved(): lax.ppermute(array, 'row', [(r, target_of(r)) for r in range(row_total)])  1.37 us
    transpose x1, other arithmetic, per_device(): return total.T  0.65 us
  transfers between devices with their start and end apart: 6, of which 2 were waited for; matrix products, arithmetic and copies ran while one was open for 0% of the time, Pallas kernels for 48%

profile of v8, /device:TPU:0, one launch (start us, length us, event | category | flops | bytes accessed | tf_op | source)
XLA Modules:
  0.0 27.4 jit_solution(16906093146217073411)
XLA Ops:
  0.0 0.5 %collective-permute-start = (bf16[64,2048]{1,0:T(8,128)(2,1)}, bf16[64,2048]{1,0:T(8,128)(2,1)S(1)}, u32[]{:S(2)}, u32[]{:S(2)}) collective-permute-start(bf16[64,2048]{1,0:T(8,128)(2,1)} %refs_3_.2), channel_id=1, source_target_pairs={{0,1},{1,0},{2,3},{3,2},{4,5},{5,4},{6,7},{7,6},{8,9},{9,8},{10,11... | collective-permute-start | bytes 786440 | tf_op jit(solution)/shard_map/ppermute | solution.py:405
  0.5 2.5 %collective-permute-start.1 = (bf16[64,2048]{1,0:T(8,128)(2,1)}, bf16[64,2048]{1,0:T(8,128)(2,1)S(1)}, u32[]{:S(2)}, u32[]{:S(2)}) collective-permute-start(bf16[64,2048]{1,0:T(8,128)(2,1)} %refs_3_.2), channel_id=1, source_target_pairs={{0,2},{1,3},{2,0},{3,1},{4,6},{5,7},{6,4},{7,5},{8,10},{9,11},{10,... | collective-permute-start | bytes 786440 | tf_op jit(solution)/shard_map/ppermute | solution.py:405
  3.6 0.0 copy-start
  3.6 2.4 %prepare.1 = (f32[72,256]{1,0:T(8,128)S(1)}, f32[16,128]{1,0:T(8,128)S(1)}, bf16[64,768]{1,0:T(8,128)(2,1)S(1)}, bf16[64,256]{1,0:T(8,128)(2,1)S(1)}, s32[3,8192]{1,0:T(4,128)S(1)}) custom-call(s32[1]{0:T(128)S(6)} %copy.9.refs_0_, s32[1,1024]{1,0:T(1,128)} %bitcast.3, s32[2,1024]{1,0:T(2,128)} %refs_2_.1, f32[144,32]{1,0:T(8,128)} %constant.8.clone.refs_3_, ...), custom_call_target="tpu_custom_call" | custom-call | flops 402653184 | bytes 1048576 | tf_op jit(solution)/shard_map/prepare/pallas_call | solution.py:423
  6.1 0.0 collective-permute-done.refs_5_.refs_4_
  6.1 0.0 copy-done
  6.1 5.5 %near_sources.1 = (f32[64,768]{1,0:T(8,128)S(1)}, bf16[64,4096]{1,0:T(8,128)(2,1)S(1)}, bf16[64,4096]{1,0:T(8,128)(2,1)S(1)}, bf16[64,1024]{1,0:T(8,128)(2,1)S(1)}, bf16[64,1024]{1,0:T(8,128)(2,1)S(1)}) custom-call(s32[3,8192]{1,0:T(4,128)S(1)} %get-tuple-element.21.refs_0_, f32[72,256]{1,0:T(8,128)S(1)} %get-tuple-element.22.refs_1_, ...), custom_call_target="tpu_custom_call" | custom-call | flops 4831838208 | bytes 1048576 | tf_op jit(solution)/shard_map/near_sources/pallas_call | solution.py:450
  11.6 0.0 collective-permute-done.1.refs_7_.refs_3_
  11.6 0.3 %collective-permute-start.2 = (bf16[64,2048]{1,0:T(8,128)(2,1)S(1)}, bf16[64,2048]{1,0:T(8,128)(2,1)S(1)}, u32[]{:S(2)}, u32[]{:S(2)}) collective-permute-start(bf16[64,2048]{1,0:T(8,128)(2,1)S(1)} %collective-permute-done.1.refs_7_.refs_3_), channel_id=1, source_target_pairs={{0,1},{1,0},{2,3},{3,2},{4,5},{5,4},{6,7},{7,6},{8,9},{9,8},{10,11... | collective-permute-start | bytes 786440 | tf_op jit(solution)/shard_map/ppermute | solution.py:405
  11.9 1.7 %own_first.1.refs_5_ = f32[64,256]{1,0:T(8,128)S(1)} custom-call(bf16[64,4096]{1,0:T(8,128)(2,1)S(1)} %get-tuple-element.33.refs_0_, bf16[64,4096]{1,0:T(8,128)(2,1)S(1)} %get-tuple-element.34.refs_1_, bf16[64,256]{1,0:T(8,128)(2,1)S(1)} %get-tuple-element.32.refs_2_, bf16[64,2048]{1,0:T(8,128)(2,1)S(1)} %copy-done, ...), custom_call_target="tpu_custom_call" | custom-call | flops 1610612736 | bytes 1048576 | tf_op jit(solution)/shard_map/own_first/pallas_call | solution.py:473
  13.7 0.0 collective-permute-done.2.refs_8_.refs_4_
  13.7 3.6 %other_sources.1 = (bf16[64,256]{1,0:T(8,128)(2,1)S(1)}, bf16[64,256]{1,0:T(8,128)(2,1)S(1)}, bf16[64,4096]{1,0:T(8,128)(2,1)S(1)}, bf16[64,4096]{1,0:T(8,128)(2,1)S(1)}) custom-call(s32[3,8192]{1,0:T(4,128)S(1)} %get-tuple-element.21.refs_0_, f32[72,256]{1,0:T(8,128)S(1)} %get-tuple-element.22.refs_1_, f32[16,128]{1,0:T(8,128)S(1)} %get-tuple-element.23.refs_2_, ...), custom_call_target="tpu_custom_call" | custom-call | flops 3221225472 | bytes 1048576 | tf_op jit(solution)/shard_map/other_sources/pallas_call | solution.py:450
  17.3 3.7 %collective-permute-start.3 = (bf16[64,256]{1,0:T(8,128)(2,1)S(1)}, bf16[64,256]{1,0:T(8,128)(2,1)S(1)}, u32[]{:S(2)}, u32[]{:S(2)}) collective-permute-start(bf16[64,256]{1,0:T(8,128)(2,1)S(1)} %get-tuple-element.35), channel_id=1, source_target_pairs={{0,12},{1,13},{2,14},{3,15},{4,8},{5,9},{6,10},{7,11},{8,4},{9,5},... | collective-permute-start | bytes 98312 | tf_op jit(solution)/shard_map/ppermute | solution.py:405
  21.0 0.0 collective-permute-start.4
  21.0 1.8 %late_targets.1 = bf16[64,256]{1,0:T(8,128)(2,1)S(1)} custom-call(bf16[64,4096]{1,0:T(8,128)(2,1)S(1)} %get-tuple-element.30.refs_0_, bf16[64,4096]{1,0:T(8,128)(2,1)S(1)} %get-tuple-element.31.refs_1_, bf16[64,768]{1,0:T(8,128)(2,1)S(1)} %get-tuple-element.24.refs_3_.refs_2_, bf16[64,2048]{1,0:T(8,128)(2,1)S(1)} %collective-permute-done.1.refs_7_.refs_3_, ...), custom_call_target="tpu_custom_call" | custom-call | flops 1610612736 | bytes 1048576 | tf_op jit(solution)/shard_map/late_targets/pallas_call | solution.py:473
  22.7 0.8 %collective-permute-start.5 = (bf16[64,256]{1,0:T(8,128)(2,1)S(1)}, bf16[64,256]{1,0:T(8,128)(2,1)S(1)}, u32[]{:S(2)}, u32[]{:S(2)}) collective-permute-start(bf16[64,256]{1,0:T(8,128)(2,1)S(1)} %late_targets.1), channel_id=1, source_target_pairs={{0,4},{1,5},{2,6},{3,7},{4,0},{5,1},{6,2},{7,3},{8,12},{9,13},{10,... | collective-permute-start | bytes 98312 | tf_op jit(solution)/shard_map/ppermute | solution.py:405
  23.6 1.8 %own_last.1 = f32[64,256]{1,0:T(8,128)S(1)} custom-call(bf16[64,4096]{1,0:T(8,128)(2,1)S(1)} %get-tuple-element.30.refs_0_, bf16[64,4096]{1,0:T(8,128)(2,1)S(1)} %get-tuple-element.31.refs_1_, bf16[64,256]{1,0:T(8,128)(2,1)S(1)} %get-tuple-element.32.refs_2_, bf16[64,2048]{1,0:T(8,128)(2,1)S(1)} %collective-permute-done.1.refs_7_.refs_3_, ...), custom_call_target="tpu_custom_call" | custom-call | flops 1610612736 | bytes 1048576 | tf_op jit(solution)/shard_map/own_last/pallas_call | solution.py:473
  25.4 0.0 collective-permute-done.3
  25.4 0.5 %collective-permute-done.4 = bf16[64,256]{1,0:T(8,128)(2,1)S(1)} collective-permute-done((bf16[64,256]{1,0:T(8,128)(2,1)S(1)}, bf16[64,256]{1,0:T(8,128)(2,1)S(1)}, u32[]{:S(2)}, u32[]{:S(2)}) %collective-permute-start.4) | collective-permute-done | bytes 32800 | tf_op jit(solution)/shard_map/ppermute | solution.py:405
  25.9 0.8 %collective-permute-done.5 = bf16[64,256]{1,0:T(8,128)(2,1)S(1)} collective-permute-done((bf16[64,256]{1,0:T(8,128)(2,1)S(1)}, bf16[64,256]{1,0:T(8,128)(2,1)S(1)}, u32[]{:S(2)}, u32[]{:S(2)}) %collective-permute-start.5) | collective-permute-done | bytes 32800 | tf_op jit(solution)/shard_map/ppermute | solution.py:405
  26.7 0.7 %add_bitcast_fusion = f32[256,64]{0,1:T(8,128)} fusion(bf16[64,256]{1,0:T(8,128)(2,1)S(1)} %collective-permute-done.5, bf16[64,256]{1,0:T(8,128)(2,1)S(1)} %collective-permute-done.4, bf16[64,256]{1,0:T(8,128)(2,1)S(1)} %collective-permute-done.3, f32[64,256]{1,0:T(8,128)S(1)} %own_last.1, bf16[64,2048]{1,0:T(8,128)(2,1)S(1)} %copy-done), kind=kLoop, calls=%fused_computation | loop fusion | flops 147456 | bytes 262144 | tf_op jit(solution)/shard_map/transpose | solution.py:491
Async XLA Ops:
  0.0 6.1 %collective-permute-start = (bf16[64,2048]{1,0:T(8,128)(2,1)}, bf16[64,2048]{1,0:T(8,128)(2,1)S(1)}, u32[]{:S(2)}, u32[]{:S(2)}) collective-permute-start(bf16[64,2048]{1,0:T(8,128)(2,1)} %refs_3_.2), channel_id=1, source_target_pairs={{0,1},{1,0},{2,3},{3,2},{4,5},{5,4},{6,7},{7,6},{8,9},{9,8},{10,11... | collective-permute-start | bytes 786440 | tf_op jit(solution)/shard_map/ppermute | solution.py:405
  0.5 11.2 %collective-permute-start.1 = (bf16[64,2048]{1,0:T(8,128)(2,1)}, bf16[64,2048]{1,0:T(8,128)(2,1)S(1)}, u32[]{:S(2)}, u32[]{:S(2)}) collective-permute-start(bf16[64,2048]{1,0:T(8,128)(2,1)} %refs_3_.2), channel_id=1, source_target_pairs={{0,2},{1,3},{2,0},{3,1},{4,6},{5,7},{6,4},{7,5},{8,10},{9,11},{10,... | collective-permute-start | bytes 786440 | tf_op jit(solution)/shard_map/ppermute | solution.py:405
  3.6 2.5 %copy-start = (bf16[64,2048]{1,0:T(8,128)(2,1)S(1)}, bf16[64,2048]{1,0:T(8,128)(2,1)}, u32[]{:S(2)}) copy-start(bf16[64,2048]{1,0:T(8,128)(2,1)} %refs_3_.2) | copy-start | bytes 786436
  11.6 2.1 %collective-permute-start.2 = (bf16[64,2048]{1,0:T(8,128)(2,1)S(1)}, bf16[64,2048]{1,0:T(8,128)(2,1)S(1)}, u32[]{:S(2)}, u32[]{:S(2)}) collective-permute-start(bf16[64,2048]{1,0:T(8,128)(2,1)S(1)} %collective-permute-done.1.refs_7_.refs_3_), channel_id=1, source_target_pairs={{0,1},{1,0},{2,3},{3,2},{4,5},{5,4},{6,7},{7,6},{8,9},{9,8},{10,11... | collective-permute-start | bytes 786440 | tf_op jit(solution)/shard_map/ppermute | solution.py:405
  17.3 8.1 %collective-permute-start.3 = (bf16[64,256]{1,0:T(8,128)(2,1)S(1)}, bf16[64,256]{1,0:T(8,128)(2,1)S(1)}, u32[]{:S(2)}, u32[]{:S(2)}) collective-permute-start(bf16[64,256]{1,0:T(8,128)(2,1)S(1)} %get-tuple-element.35), channel_id=1, source_target_pairs={{0,12},{1,13},{2,14},{3,15},{4,8},{5,9},{6,10},{7,11},{8,4},{9,5},... | collective-permute-start | bytes 98312 | tf_op jit(solution)/shard_map/ppermute | solution.py:405
  21.0 4.9 %collective-permute-start.4 = (bf16[64,256]{1,0:T(8,128)(2,1)S(1)}, bf16[64,256]{1,0:T(8,128)(2,1)S(1)}, u32[]{:S(2)}, u32[]{:S(2)}) collective-permute-start(bf16[64,256]{1,0:T(8,128)(2,1)S(1)} %get-tuple-element.36), channel_id=1, source_target_pairs={{0,8},{1,9},{2,10},{3,11},{4,12},{5,13},{6,14},{7,15},{8,0},{9,1},... | collective-permute-start | bytes 98312 | tf_op jit(solution)/shard_map/ppermute | solution.py:405
  22.7 4.0 %collective-permute-start.5 = (bf16[64,256]{1,0:T(8,128)(2,1)S(1)}, bf16[64,256]{1,0:T(8,128)(2,1)S(1)}, u32[]{:S(2)}, u32[]{:S(2)}) collective-permute-start(bf16[64,256]{1,0:T(8,128)(2,1)S(1)} %late_targets.1), channel_id=1, source_target_pairs={{0,4},{1,5},{2,6},{3,7},{4,0},{5,1},{6,2},{7,3},{8,12},{9,13},{10,... | collective-permute-start | bytes 98312 | tf_op jit(solution)/shard_map/ppermute | solution.py:405

commit v9 on v7

--- a/solution.py
+++ b/solution.py
@@ -376,6 +376,8 @@
         ) == lax.broadcasted_iota(jnp.int32, (BAND_DEV, BAND_DEV), 1)
         apart = jnp.where(diagonal, 1e30, 0.0)
     total = part_refs[0][:, -BAND_DEV:] if part_refs else None
+    if own:
+        total = 0.5 * density_refs[0][:, :BAND_DEV].astype(F32)
     step = KEPT_STEP
     for first in range(0, count * src_dev, step):
         here = slice(first, first + step)
@@ -483,7 +485,7 @@
     own_sums = kept(near_features, tgt_own, densities[:near], True, [])
     sums.append(kept(rest_features, tgt_far, densities[near:], False, [part], BF16))
     own_sums = kept(rest_features, tgt_own, densities[near:], False, [own_sums])
-    total = 0.5 * density[:, :BAND_DEV].astype(F32) + own_sums
+    total = own_sums
     for k, block in enumerate(sums):
         total = total + moved(
             block, lambda r, k=k: partner(r // group, k + 1, groups) * group + r % group

time: 27.5 us -> 27.5 us (level)
  no operation moved by 1% of the time
where the time goes in v9:
time: 27.5 us; the launch traced here: 27.4 us
  Pallas kernels  16.8 us (61%)
  starting transfers between devices  7.79 us (28%)
  waiting for transfers between devices  1.36 us (5%)
  between operations  0.74 us (3%)
  other arithmetic  0.65 us (2%)
    pallas_call x2, Pallas kernels, sources(): pl.pallas_call(lambda *refs: sources_kernel(first, len(blocks), cycle_cou...  9.11 us
    ppermute x6, starting transfers between devices, moved(): lax.ppermute(array, 'row', [(r, target_of(r)) for r in range(row_total)])  7.79 us
    pallas_call x3, Pallas kernels, kept(): pl.pallas_call(lambda *refs: kept_kernel(own, len(blocks), *refs), out_sh...  5.3 us
    pallas_call x1, Pallas kernels, per_device(): pl.pallas_call(lambda *refs: prepare_kernel(row_total, group, sizes, *ref...  2.44 us
    ppermute x6, waiting for transfers between devices, moved(): lax.ppermute(array, 'row', [(r, target_of(r)) for r in range(row_total)])  1.36 us
    transpose x1, other arithmetic, per_device(): return total.T  0.65 us
  transfers between devices with their start and end apart: 6, of which 2 were waited for; matrix products, arithmetic and copies ran while one was open for 0% of the time, Pallas kernels for 48%

profile of v9, /device:TPU:0, one launch (start us, length us, event | category | flops | bytes accessed | tf_op | source)
XLA Modules:
  0.0 27.4 jit_solution(9916201092934570281)
XLA Ops:
  0.0 0.5 %collective-permute-start = (bf16[64,2048]{1,0:T(8,128)(2,1)}, bf16[64,2048]{1,0:T(8,128)(2,1)S(1)}, u32[]{:S(2)}, u32[]{:S(2)}) collective-permute-start(bf16[64,2048]{1,0:T(8,128)(2,1)} %refs_3_.2), channel_id=1, source_target_pairs={{0,1},{1,0},{2,3},{3,2},{4,5},{5,4},{6,7},{7,6},{8,9},{9,8},{10,11... | collective-permute-start | bytes 786440 | tf_op jit(solution)/shard_map/ppermute | solution.py:407
  0.5 2.5 %collective-permute-start.1 = (bf16[64,2048]{1,0:T(8,128)(2,1)}, bf16[64,2048]{1,0:T(8,128)(2,1)S(1)}, u32[]{:S(2)}, u32[]{:S(2)}) collective-permute-start(bf16[64,2048]{1,0:T(8,128)(2,1)} %refs_3_.2), channel_id=1, source_target_pairs={{0,2},{1,3},{2,0},{3,1},{4,6},{5,7},{6,4},{7,5},{8,10},{9,11},{10,... | collective-permute-start | bytes 786440 | tf_op jit(solution)/shard_map/ppermute | solution.py:407
  3.6 0.0 copy-start
  3.6 2.4 %prepare.1 = (f32[72,256]{1,0:T(8,128)S(1)}, f32[16,128]{1,0:T(8,128)S(1)}, bf16[64,768]{1,0:T(8,128)(2,1)S(1)}, bf16[64,256]{1,0:T(8,128)(2,1)S(1)}, s32[3,8192]{1,0:T(4,128)S(1)}) custom-call(s32[1]{0:T(128)S(6)} %copy.9.refs_0_, s32[1,1024]{1,0:T(1,128)} %bitcast.3, s32[2,1024]{1,0:T(2,128)} %refs_2_.1, f32[144,32]{1,0:T(8,128)} %constant.6.clone.refs_3_, ...), custom_call_target="tpu_custom_call" | custom-call | flops 402653184 | bytes 1048576 | tf_op jit(solution)/shard_map/prepare/pallas_call | solution.py:425
  6.1 0.0 collective-permute-done.refs_5_.refs_4_
  6.1 0.0 copy-done
  6.1 5.5 %near_sources.1 = (f32[64,768]{1,0:T(8,128)S(1)}, bf16[64,4096]{1,0:T(8,128)(2,1)S(1)}, bf16[64,4096]{1,0:T(8,128)(2,1)S(1)}, bf16[64,1024]{1,0:T(8,128)(2,1)S(1)}, bf16[64,1024]{1,0:T(8,128)(2,1)S(1)}) custom-call(s32[3,8192]{1,0:T(4,128)S(1)} %get-tuple-element.21.refs_0_, f32[72,256]{1,0:T(8,128)S(1)} %get-tuple-element.22.refs_1_, ...), custom_call_target="tpu_custom_call" | custom-call | flops 4831838208 | bytes 1048576 | tf_op jit(solution)/shard_map/near_sources/pallas_call | solution.py:452
  11.6 0.0 collective-permute-done.1.refs_7_.refs_3_
  11.6 0.3 %collective-permute-start.2 = (bf16[64,2048]{1,0:T(8,128)(2,1)S(1)}, bf16[64,2048]{1,0:T(8,128)(2,1)S(1)}, u32[]{:S(2)}, u32[]{:S(2)}) collective-permute-start(bf16[64,2048]{1,0:T(8,128)(2,1)S(1)} %collective-permute-done.1.refs_7_.refs_3_), channel_id=1, source_target_pairs={{0,1},{1,0},{2,3},{3,2},{4,5},{5,4},{6,7},{7,6},{8,9},{9,8},{10,11... | collective-permute-start | bytes 786440 | tf_op jit(solution)/shard_map/ppermute | solution.py:407
  11.9 1.8 %own_first.1.refs_5_ = f32[64,256]{1,0:T(8,128)S(1)} custom-call(bf16[64,4096]{1,0:T(8,128)(2,1)S(1)} %get-tuple-element.33.refs_0_, bf16[64,4096]{1,0:T(8,128)(2,1)S(1)} %get-tuple-element.34.refs_1_, bf16[64,256]{1,0:T(8,128)(2,1)S(1)} %get-tuple-element.32.refs_2_, bf16[64,2048]{1,0:T(8,128)(2,1)S(1)} %copy-done, ...), custom_call_target="tpu_custom_call" | custom-call | flops 1610612736 | bytes 1048576 | tf_op jit(solution)/shard_map/own_first/pallas_call | solution.py:475
  13.7 0.0 collective-permute-done.2.refs_8_.refs_4_
  13.7 3.6 %other_sources.1 = (bf16[64,256]{1,0:T(8,128)(2,1)S(1)}, bf16[64,256]{1,0:T(8,128)(2,1)S(1)}, bf16[64,4096]{1,0:T(8,128)(2,1)S(1)}, bf16[64,4096]{1,0:T(8,128)(2,1)S(1)}) custom-call(s32[3,8192]{1,0:T(4,128)S(1)} %get-tuple-element.21.refs_0_, f32[72,256]{1,0:T(8,128)S(1)} %get-tuple-element.22.refs_1_, f32[16,128]{1,0:T(8,128)S(1)} %get-tuple-element.23.refs_2_, ...), custom_call_target="tpu_custom_call" | custom-call | flops 3221225472 | bytes 1048576 | tf_op jit(solution)/shard_map/other_sources/pallas_call | solution.py:452
  17.3 3.7 %collective-permute-start.3 = (bf16[64,256]{1,0:T(8,128)(2,1)S(1)}, bf16[64,256]{1,0:T(8,128)(2,1)S(1)}, u32[]{:S(2)}, u32[]{:S(2)}) collective-permute-start(bf16[64,256]{1,0:T(8,128)(2,1)S(1)} %get-tuple-element.35), channel_id=1, source_target_pairs={{0,12},{1,13},{2,14},{3,15},{4,8},{5,9},{6,10},{7,11},{8,4},{9,5},... | collective-permute-start | bytes 98312 | tf_op jit(solution)/shard_map/ppermute | solution.py:407
  21.0 0.0 collective-permute-start.4
  21.0 1.8 %late_targets.1 = bf16[64,256]{1,0:T(8,128)(2,1)S(1)} custom-call(bf16[64,4096]{1,0:T(8,128)(2,1)S(1)} %get-tuple-element.30.refs_0_, bf16[64,4096]{1,0:T(8,128)(2,1)S(1)} %get-tuple-element.31.refs_1_, bf16[64,768]{1,0:T(8,128)(2,1)S(1)} %get-tuple-element.24.refs_3_.refs_2_, bf16[64,2048]{1,0:T(8,128)(2,1)S(1)} %collective-permute-done.1.refs_7_.refs_3_, ...), custom_call_target="tpu_custom_call" | custom-call | flops 1610612736 | bytes 1048576 | tf_op jit(solution)/shard_map/late_targets/pallas_call | solution.py:475
  22.8 0.8 %collective-permute-start.5 = (bf16[64,256]{1,0:T(8,128)(2,1)S(1)}, bf16[64,256]{1,0:T(8,128)(2,1)S(1)}, u32[]{:S(2)}, u32[]{:S(2)}) collective-permute-start(bf16[64,256]{1,0:T(8,128)(2,1)S(1)} %late_targets.1), channel_id=1, source_target_pairs={{0,4},{1,5},{2,6},{3,7},{4,0},{5,1},{6,2},{7,3},{8,12},{9,13},{10,... | collective-permute-start | bytes 98312 | tf_op jit(solution)/shard_map/ppermute | solution.py:407
  23.6 1.8 %own_last.1 = f32[64,256]{1,0:T(8,128)S(1)} custom-call(bf16[64,4096]{1,0:T(8,128)(2,1)S(1)} %get-tuple-element.30.refs_0_, bf16[64,4096]{1,0:T(8,128)(2,1)S(1)} %get-tuple-element.31.refs_1_, bf16[64,256]{1,0:T(8,128)(2,1)S(1)} %get-tuple-element.32.refs_2_, bf16[64,2048]{1,0:T(8,128)(2,1)S(1)} %collective-permute-done.1.refs_7_.refs_3_, ...), custom_call_target="tpu_custom_call" | custom-call | flops 1610612736 | bytes 1048576 | tf_op jit(solution)/shard_map/own_last/pallas_call | solution.py:475
  25.4 0.0 collective-permute-done.3
  25.4 0.5 %collective-permute-done.4 = bf16[64,256]{1,0:T(8,128)(2,1)S(1)} collective-permute-done((bf16[64,256]{1,0:T(8,128)(2,1)S(1)}, bf16[64,256]{1,0:T(8,128)(2,1)S(1)}, u32[]{:S(2)}, u32[]{:S(2)}) %collective-permute-start.4) | collective-permute-done | bytes 32800 | tf_op jit(solution)/shard_map/ppermute | solution.py:407
  25.9 0.8 %collective-permute-done.5 = bf16[64,256]{1,0:T(8,128)(2,1)S(1)} collective-permute-done((bf16[64,256]{1,0:T(8,128)(2,1)S(1)}, bf16[64,256]{1,0:T(8,128)(2,1)S(1)}, u32[]{:S(2)}, u32[]{:S(2)}) %collective-permute-start.5) | collective-permute-done | bytes 32800 | tf_op jit(solution)/shard_map/ppermute | solution.py:407
  26.7 0.6 %add_bitcast_fusion = f32[256,64]{0,1:T(8,128)} fusion(bf16[64,256]{1,0:T(8,128)(2,1)S(1)} %collective-permute-done.5, bf16[64,256]{1,0:T(8,128)(2,1)S(1)} %collective-permute-done.4, f32[64,256]{1,0:T(8,128)S(1)} %own_last.1, bf16[64,256]{1,0:T(8,128)(2,1)S(1)} %collective-permute-done.3), kind=kLoop, calls=%fused_computation | loop fusion | flops 98304 | bytes 229376 | tf_op jit(solution)/shard_map/transpose | solution.py:493
Async XLA Ops:
  0.0 6.1 %collective-permute-start = (bf16[64,2048]{1,0:T(8,128)(2,1)}, bf16[64,2048]{1,0:T(8,128)(2,1)S(1)}, u32[]{:S(2)}, u32[]{:S(2)}) collective-permute-start(bf16[64,2048]{1,0:T(8,128)(2,1)} %refs_3_.2), channel_id=1, source_target_pairs={{0,1},{1,0},{2,3},{3,2},{4,5},{5,4},{6,7},{7,6},{8,9},{9,8},{10,11... | collective-permute-start | bytes 786440 | tf_op jit(solution)/shard_map/ppermute | solution.py:407
  0.5 11.2 %collective-permute-start.1 = (bf16[64,2048]{1,0:T(8,128)(2,1)}, bf16[64,2048]{1,0:T(8,128)(2,1)S(1)}, u32[]{:S(2)}, u32[]{:S(2)}) collective-permute-start(bf16[64,2048]{1,0:T(8,128)(2,1)} %refs_3_.2), channel_id=1, source_target_pairs={{0,2},{1,3},{2,0},{3,1},{4,6},{5,7},{6,4},{7,5},{8,10},{9,11},{10,... | collective-permute-start | bytes 786440 | tf_op jit(solution)/shard_map/ppermute | solution.py:407
  3.6 2.5 %copy-start = (bf16[64,2048]{1,0:T(8,128)(2,1)S(1)}, bf16[64,2048]{1,0:T(8,128)(2,1)}, u32[]{:S(2)}) copy-start(bf16[64,2048]{1,0:T(8,128)(2,1)} %refs_3_.2) | copy-start | bytes 786436
  11.6 2.1 %collective-permute-start.2 = (bf16[64,2048]{1,0:T(8,128)(2,1)S(1)}, bf16[64,2048]{1,0:T(8,128)(2,1)S(1)}, u32[]{:S(2)}, u32[]{:S(2)}) collective-permute-start(bf16[64,2048]{1,0:T(8,128)(2,1)S(1)} %collective-permute-done.1.refs_7_.refs_3_), channel_id=1, source_target_pairs={{0,1},{1,0},{2,3},{3,2},{4,5},{5,4},{6,7},{7,6},{8,9},{9,8},{10,11... | collective-permute-start | bytes 786440 | tf_op jit(solution)/shard_map/ppermute | solution.py:407
  17.3 8.1 %collective-permute-start.3 = (bf16[64,256]{1,0:T(8,128)(2,1)S(1)}, bf16[64,256]{1,0:T(8,128)(2,1)S(1)}, u32[]{:S(2)}, u32[]{:S(2)}) collective-permute-start(bf16[64,256]{1,0:T(8,128)(2,1)S(1)} %get-tuple-element.35), channel_id=1, source_target_pairs={{0,12},{1,13},{2,14},{3,15},{4,8},{5,9},{6,10},{7,11},{8,4},{9,5},... | collective-permute-start | bytes 98312 | tf_op jit(solution)/shard_map/ppermute | solution.py:407
  21.0 4.9 %collective-permute-start.4 = (bf16[64,256]{1,0:T(8,128)(2,1)S(1)}, bf16[64,256]{1,0:T(8,128)(2,1)S(1)}, u32[]{:S(2)}, u32[]{:S(2)}) collective-permute-start(bf16[64,256]{1,0:T(8,128)(2,1)S(1)} %get-tuple-element.36), channel_id=1, source_target_pairs={{0,8},{1,9},{2,10},{3,11},{4,12},{5,13},{6,14},{7,15},{8,0},{9,1},... | collective-permute-start | bytes 98312 | tf_op jit(solution)/shard_map/ppermute | solution.py:407
  22.8 4.0 %collective-permute-start.5 = (bf16[64,256]{1,0:T(8,128)(2,1)S(1)}, bf16[64,256]{1,0:T(8,128)(2,1)S(1)}, u32[]{:S(2)}, u32[]{:S(2)}) collective-permute-start(bf16[64,256]{1,0:T(8,128)(2,1)S(1)} %late_targets.1), channel_id=1, source_target_pairs={{0,4},{1,5},{2,6},{3,7},{4,0},{5,1},{6,2},{7,3},{8,12},{9,13},{10,... | collective-permute-start | bytes 98312 | tf_op jit(solution)/shard_map/ppermute | solution.py:407
